TPU v7x, 128 devices: a whole 4x4x4 slice. The times are simulated.
128 devices in a mesh: gx: 32 (over z, y, core), gy: 4 (over x).
Axes of the slice: x: 4, y: 4, z: 4, core: 2. Of those that a mesh axis runs over, the one named last changes fastest.
Arguments:
- fields: float32 [6, 512, 96, 128], P(None, 'gx', 'gy'), may hold values from -6 to 6
- material: int32 [512, 96, 128], P('gx', 'gy'), may hold values from 0 to 15
- permittivity: float32 [16], replicated, may hold values from 1 to 4
- patch_cell: int32 [32768], P(('gx', 'gy')), may hold values from 0 to 49151
- patch_owner: int32 [32768, 1], P(('gx', 'gy')), may hold values from 0 to 127; in each aligned block of 256 rows (0 to 255, 256 to 511, ...) at most 4 rows name the same one
Outputs:
- new_fields: float32 [6, 512, 96, 128], P(None, 'gx', 'gy')
- far_field: float32 [12, 16384], P(None, ('gx', 'gy'))
Inputs may be any that keep to these rules, and one draw needn't show every extreme that they name: `patch_cell`: an index into the cells of the patch's own device block, x slowest and z fastest. `patch_owner`: among the rows of one device no sector is named by more than 4 rows, a bound that some block reaches; every sector is named by some row.
All inputs are finite; a program needn't handle non-finite values.
Results may differ from a plain program's by a relative error of at most 0.00022.
Values sent between devices are 32-bit elements; how exact they have to be, the bound alone decides.
No kernel may reach another device: no remote copies, remote signals or barrier semaphores. Data moves between devices by JAX's collectives and lax.ppermute only.
A program may use at most 128 MiB of HBM per device.

v0:
```python
import math

import jax
import jax.numpy as jnp
from jax import lax
from jax.experimental import pallas as pl
from jax.experimental.pallas import tpu as pltpu
from jax.sharding import PartitionSpec as P

F32 = jnp.float32
CX, CY, NZ = 16, 24, 128
NB = 32
NBY = 4
ROWS = 32
HALF = 32.0
XC = (1, 2, 4, 5)
YC = (0, 2, 3, 5)
SLOTS = 4
PATCH = 256
KAPPA = 0.5


def ds(start, size, stride=None):
    return pl.ds(start, size) if stride is None else pl.ds(start, size, stride=stride)


def call(body, outs, args, scratch=(), smem=()):
    specs = [
        pl.BlockSpec(memory_space=pltpu.SMEM if i in smem else pltpu.VMEM) for i in range(len(args))
    ]
    return pl.pallas_call(
        body,
        out_shape=[jax.ShapeDtypeStruct(s, F32) for s in outs],
        in_specs=specs,
        out_specs=[pl.BlockSpec(memory_space=pltpu.VMEM) for _ in outs],
        scratch_shapes=[pltpu.VMEM(s, F32) for s in scratch],
        compiler_params=pltpu.CompilerParams(vmem_limit_bytes=40 * 1024 * 1024),
    )(*args)


def flag(cond):
    return jnp.where(cond, 1.0, 0.0).astype(F32)


def row_of(shape):
    return lax.broadcasted_iota(jnp.int32, shape, 0)


def lane_of(shape):
    return lax.broadcasted_iota(jnp.int32, shape, 1)


def diff_z(f):
    lane = lane_of(f.shape)
    up = jnp.where(lane == NZ - 1, 0.0, pltpu.roll(f, NZ - 1, 1))
    down = jnp.where(lane == 0, 0.0, pltpu.roll(f, 1, 1))
    return up - down


def diff_y(f, below, above):
    row = row_of(f.shape)
    up = jnp.where(row == CY - 1, above, pltpu.roll(f, CY - 1, 0))
    down = jnp.where(row == 0, below, pltpu.roll(f, 1, 0))
    return up - down


def right_sides(f, s, dx, dy, dz):
    curl_h = (dy[5] - dz[4], dz[3] - dx[5], dx[4] - dy[3])
    curl_e = (dy[2] - dz[1], dz[0] - dx[2], dx[1] - dy[0])
    electric = [s * f[m] + (0.5 / HALF) * curl_h[m] for m in range(3)]
    magnetic = [s * (f[3 + m] - (0.5 * HALF) * curl_e[m]) for m in range(3)]
    return electric + magnetic


def edges_body(f, mat, perm, xh, xl, yh, yl, eps):
    m = mat[...]
    e = jnp.full(m.shape, perm[0], F32)
    for k in range(1, 16):
        e = jnp.where(m == k, perm[k], e)
    eps[...] = e
    for i, c in enumerate(XC):
        xh[ds(i * CY, CY), :] = f[ds((c * CX + CX - 1) * CY, CY), :]
        xl[ds(i * CY, CY), :] = f[ds(c * CX * CY, CY), :]
    for out, edge, inner in ((yh, CY - 1, CY - 2), (yl, 0, 1)):
        for c in range(6):
            out[ds(c * CX, CX), :] = f[ds(c * CX * CY + edge, CX, CY), :]
        for i, c in enumerate(YC):
            out[ds((6 + i) * CX, CX), :] = f[ds(c * CX * CY + inner, CX, CY), :]
        out[ds(10 * CX, CX), :] = eps[ds(edge, CX, CY), :]


def first_body(f, eps, xlo, xhi, ylo, yhi, sol, lsp, rsp, send, ht, hu, hd, he, gs):
    gx, gy = lax.axis_index("gx"), lax.axis_index("gy")
    mxl, mxh = flag(gx > 0), flag(gx < NB - 1)
    myl, myh = flag(gy > 0), flag(gy < NBY - 1)
    ht[...] = jnp.zeros(ht.shape, F32)
    hu[...] = jnp.zeros(hu.shape, F32)
    hd[...] = jnp.zeros(hd.shape, F32)
    he[...] = jnp.ones(he.shape, F32)
    for c in range(6):
        ht[ds(c * 128, CX, 8), :] = ylo[ds(c * CX, CX), :] * myl
        ht[ds(c * 128 + 1, CX, 8), :] = yhi[ds(c * CX, CX), :] * myh
    for i, c in enumerate(YC):
        hu[ds(i * 128, CX, 8), :] = f[ds(c * CX * CY, CX, CY), :]
        hu[ds(i * 128 + 1, CX, 8), :] = yhi[ds((6 + i) * CX, CX), :] * myh
        hd[ds(i * 128, CX, 8), :] = ylo[ds((6 + i) * CX, CX), :] * myl
        hd[ds(i * 128 + 1, CX, 8), :] = f[ds(c * CX * CY + CY - 1, CX, CY), :]
    he[ds(0, CX, 8), :] = jnp.where(myl > 0, ylo[ds(10 * CX, CX), :], 1.0)
    he[ds(1, CX, 8), :] = jnp.where(myh > 0, yhi[ds(10 * CX, CX), :], 1.0)
    row8 = row_of((8, NZ))
    inside = jnp.where(row8 == 0, myl, jnp.where(row8 == 1, myh, 0.0))

    def main(c, x):
        return f[ds(pl.multiple_of((c * CX + x) * CY, 8), CY), :]

    def halo(ref, i, x):
        return ref[ds(pl.multiple_of(i * 128 + x * 8, 8), 8), :]

    def forward(x, carry):
        wg, yl, ys = carry[0], carry[1], carry[2:]
        x_up, x_down = jnp.minimum(x + 1, CX - 1), jnp.maximum(x - 1, 0)
        fm = [main(c, x) for c in range(6)]
        fh = [halo(ht, c, x) for c in range(6)]
        both = [jnp.concatenate([fm[c], fh[c]], axis=0) for c in range(6)]
        dx, dy, dz = {}, {}, {}
        for i, c in enumerate(XC):
            up = jnp.where(x == CX - 1, xhi[ds(i * CY, CY), :] * mxh, main(c, x_up))
            down = jnp.where(x == 0, xlo[ds(i * CY, CY), :] * mxl, main(c, x_down))
            up_h = jnp.where(x == CX - 1, 0.0, halo(ht, c, x_up))
            down_h = jnp.where(x == 0, 0.0, halo(ht, c, x_down))
            dx[c] = jnp.concatenate([up - down, up_h - down_h], axis=0)
        for i, c in enumerate(YC):
            inner = diff_y(fm[c], fh[c][0:1], fh[c][1:2])
            dy[c] = jnp.concatenate([inner, halo(hu, i, x) - halo(hd, i, x)], axis=0)
        for c in (0, 1, 3, 4):
            dz[c] = diff_z(both[c])
        e = jnp.concatenate([eps[ds(pl.multiple_of(x * CY, 8), CY), :], halo(he, 0, x)], axis=0)
        s = e * (1.0 / (HALF * HALF))
        right = right_sides(both, s, dx, dy, dz)
        w = s + wg
        g = 1.0 / (1.0 + w)
        at = pl.multiple_of(x * ROWS, 8)
        gs[ds(at, ROWS), :] = g
        yl = yl * g
        lsp[ds(at, ROWS), :] = yl
        new = []
        for c in range(6):
            r = jnp.concatenate([right[c][:CY], right[c][CY:] * inside], axis=0)
            y = (r + ys[c]) * g
            sol[ds(pl.multiple_of(c * CX * ROWS + x * ROWS, 8), ROWS), :] = y
            new.append(y)
        return (w * g, yl, *new)

    one, zero = jnp.ones((ROWS, NZ), F32), jnp.zeros((ROWS, NZ), F32)
    lax.fori_loop(0, CX, forward, (one, one) + (zero,) * 6)

    def backward(k, carry):
        x = CX - 1 - k
        at = pl.multiple_of(x * ROWS, 8)
        g = gs[ds(at, ROWS), :]
        ul = lsp[ds(at, ROWS), :] + g * carry[0]
        ur = g * carry[1]
        lsp[ds(at, ROWS), :] = ul
        rsp[ds(at, ROWS), :] = ur
        new = []
        for c in range(6):
            here = ds(pl.multiple_of(c * CX * ROWS + x * ROWS, 8), ROWS)
            u = sol[here, :] + g * carry[2 + c]
            sol[here, :] = u
            new.append(u)
        return (ul, ur, *new)

    lead = lax.fori_loop(0, CX, backward, (zero, one) + (zero,) * 6)
    left_first, right_first, lead = lead[0], lead[1], lead[2:]
    tail = [sol[ds((c * CX + CX - 1) * ROWS, ROWS), :] for c in range(6)]

    def with_halo(value, extra):
        return jnp.concatenate([value[:CY], extra], axis=0)

    def end(i, x):
        return ht[ds(i * 128 + x * 8, 8), :]

    scale = 0.5 / HALF
    last = CX - 1
    lead_rows, tail_rows = list(lead), list(tail)
    lead_rows[1] = with_halo(lead[1], end(1, 0))
    tail_rows[1] = with_halo(tail[1], end(1, last))
    lead_rows[4] = with_halo(lead[4], he[ds(0, 8), :] * scale)
    tail_rows[4] = with_halo(tail[4], he[ds(last * 8, 8), :] * scale)
    lead_rows[2] = with_halo(lead[2], lead[2][CY:] + scale * end(4, 0))
    tail_rows[2] = with_halo(tail[2], tail[2][CY:] - scale * end(4, last))
    for c in range(6):
        send[ds(c, ROWS, 16), :] = lead_rows[c]
        send[ds(8 + c, ROWS, 16), :] = tail_rows[c]
    send[ds(6, ROWS, 16), :] = left_first
    send[ds(7, ROWS, 16), :] = right_first
    send[ds(14, ROWS, 16), :] = right_first
    send[ds(15, ROWS, 16), :] = rsp[ds((CX - 1) * ROWS, ROWS), :]


def join_body(rec, back, phis, psis, ms, ns):
    gx = lax.axis_index("gx")
    row8 = row_of((8, NZ))
    shifted = (row8 == 5) & ((gx == CY) | (gx == CY + 1))

    def line(b, k):
        return jnp.broadcast_to(rec[ds(b * 16 + k, 1), :], (8, NZ))

    def shifts(b):
        low = high = jnp.zeros((8, NZ), F32)
        if b > 0:
            low = jnp.where(shifted, line(b, 4) * line(b - 1, 9), 0.0)
        if b < NB - 1:
            high = jnp.where(shifted, -line(b, 12) * line(b + 1, 1), 0.0)
        return low, high

    m = n = jnp.zeros((8, NZ), F32)
    for b in range(NB):
        low, high = shifts(b)
        a, cross, d = line(b, 6), line(b, 7), line(b, 15)
        p = rec[ds(b * 16, 8), :] + a * low + cross * high
        q = rec[ds(b * 16 + 8, 8), :] + cross * low + d * high
        ms[ds(b * 8, 8), :] = m
        ns[ds(b * 8, 8), :] = n
        gain = 1.0 / (1.0 - a * n)
        phi = gain * (p + a * m)
        psi = gain * cross
        phis[ds(b * 8, 8), :] = phi
        psis[ds(b * 8, 8), :] = psi
        m = q + cross * (m + n * phi)
        n = d + cross * (n * psi)
    ahead = jnp.zeros((8, NZ), F32)
    for b in reversed(range(NB)):
        low, high = shifts(b)
        lead = phis[ds(b * 8, 8), :] + psis[ds(b * 8, 8), :] * ahead
        back[ds(b * 16, 8), :] = ms[ds(b * 8, 8), :] + ns[ds(b * 8, 8), :] * lead + low
        back[ds(b * 16 + 8, 8), :] = ahead + high
        ahead = lead


def second_body(back, sol, lsp, rsp, eps, soly, ly, ry, rec, mid, inc, out, r2, gys, yls):
    for c in range(6):
        inc[ds(c * ROWS, ROWS), :] = back[ds(c, ROWS, 16), :]
        out[ds(c * ROWS, ROWS), :] = back[ds(8 + c, ROWS, 16), :]

    def settle(x, carry):
        at = pl.multiple_of(x * ROWS, 8)
        left, right = lsp[ds(at, ROWS), :], rsp[ds(at, ROWS), :]
        for c in range(6):
            here = ds(pl.multiple_of((c * CX + x) * ROWS, 8), ROWS)
            mid[here, :] = (
                sol[here, :]
                + left * inc[ds(c * ROWS, ROWS), :]
                + right * out[ds(c * ROWS, ROWS), :]
            )
        return carry

    lax.fori_loop(0, CX, settle, 0)

    def main(c, x):
        return mid[ds(pl.multiple_of((c * CX + x) * ROWS, 8), CY), :]

    def stencil(x, carry):
        x_up, x_down = jnp.minimum(x + 1, CX - 1), jnp.maximum(x - 1, 0)
        f = [main(c, x) for c in range(6)]
        dx, dy, dz = {}, {}, {}
        for c in XC:
            up = jnp.where(x == CX - 1, out[ds(c * ROWS, CY), :], main(c, x_up))
            down = jnp.where(x == 0, inc[ds(c * ROWS, CY), :], main(c, x_down))
            dx[c] = up - down
        for c in YC:
            edge = mid[ds(pl.multiple_of((c * CX + x) * ROWS + CY, 8), 8), :]
            dy[c] = diff_y(f[c], edge[0:1], edge[1:2])
        for c in (0, 1, 3, 4):
            dz[c] = diff_z(f[c])
        s = eps[ds(pl.multiple_of(x * CY, 8), CY), :] * (1.0 / (HALF * HALF))
        right = right_sides(f, s, dx, dy, dz)
        for c in range(6):
            r2[ds(pl.multiple_of((c * CX + x) * CY, 8), CY), :] = right[c]
        return carry

    lax.fori_loop(0, CX, stencil, 0)

    one, zero = jnp.ones((CX, NZ), F32), jnp.zeros((CX, NZ), F32)

    wg, yl, ys = one, one, [zero] * 6
    for y in range(CY):
        s = eps[ds(y, CX, CY), :] * (1.0 / (HALF * HALF))
        w = s + wg
        g = 1.0 / (1.0 + w)
        wg = w * g
        gys[ds(y * CX, CX), :] = g
        yl = yl * g
        yls[ds(y * CX, CX), :] = yl
        for c in range(6):
            here = ds(c * CX * CY + y, CX, CY)
            ys[c] = (r2[here, :] + ys[c]) * g
            r2[here, :] = ys[c]
    tail = list(ys)
    ul, ur, us = zero, one, [zero] * 6
    right_last = None
    for y in reversed(range(CY)):
        g = gys[ds(y * CX, CX), :]
        ul = yls[ds(y * CX, CX), :] + g * ul
        ur = g * ur
        if y == CY - 1:
            right_last = ur
        ly[ds(y, CX, CY), :] = ul
        ry[ds(y, CX, CY), :] = ur
        for c in range(6):
            here = ds(c * CX * CY + y, CX, CY)
            us[c] = r2[here, :] + g * us[c]
            soly[here, :] = us[c]
    for c in range(6):
        rec[ds(c * CX, CX), :] = us[c]
        rec[ds((8 + c) * CX, CX), :] = tail[c]
    rec[ds(6 * CX, CX), :] = ul
    rec[ds(7 * CX, CX), :] = ur
    rec[ds(14 * CX, CX), :] = ur
    rec[ds(15 * CX, CX), :] = right_last


def finish_body(
    rec0, rec1, rec2, rec3, soly, ly, ry, cell, cell_row, owner_row, new, send, recs, inc, out, table
):
    gy = lax.axis_index("gy")
    size = 16 * CX
    for k, part in enumerate((rec0, rec1, rec2, rec3)):
        at = lax.rem(gy + (NBY - k), NBY)
        recs[ds(pl.multiple_of(at * size, 8), size), :] = part[...]

    def get(b, k):
        return recs[ds(b * size + k * CX, CX), :]

    zero = jnp.zeros((CX, NZ), F32)
    m, n = [zero] * 6, zero
    kept = []
    for b in range(NBY):
        a, cross, d = get(b, 6), get(b, 7), get(b, 15)
        gain = 1.0 / (1.0 - a * n)
        phi = [gain * (get(b, c) + a * m[c]) for c in range(6)]
        psi = gain * cross
        kept.append((m, n, phi, psi))
        m = [get(b, 8 + c) + cross * (m[c] + n * phi[c]) for c in range(6)]
        n = d + cross * (n * psi)
    ahead = [zero] * 6
    incoming, outgoing = [zero] * 6, [zero] * 6
    for b in reversed(range(NBY)):
        mb, nb, phi, psi = kept[b]
        lead = [phi[c] + psi * ahead[c] for c in range(6)]
        for c in range(6):
            incoming[c] = jnp.where(gy == b, mb[c] + nb * lead[c], incoming[c])
            outgoing[c] = jnp.where(gy == b, ahead[c], outgoing[c])
        ahead = lead
    for c in range(6):
        inc[ds(c * CX, CX), :] = incoming[c]
        out[ds(c * CX, CX), :] = outgoing[c]

    def settle(x, carry):
        at = pl.multiple_of(x * CY, 8)
        left, right = ly[ds(at, CY), :], ry[ds(at, CY), :]
        for c in range(6):
            here = ds(pl.multiple_of((c * CX + x) * CY, 8), CY)
            value = (
                soly[here, :]
                + left * inc[ds(c * CX + x, 1), :]
                + right * out[ds(c * CX + x, 1), :]
            )
            new[here, :] = value
            table[ds(x * (CY * 8) + c, CY, 8), :] = value
        return carry

    lax.fori_loop(0, CX, settle, 0)

    lane = lane_of((8, NZ))
    halves = []
    for half in range(PATCH // NZ):

        def pick(j, acc):
            at = cell[half * NZ + j]
            values = table[ds(pl.multiple_of((at >> 7) * 8, 8), 8), :]
            moved = pltpu.roll(values, (j - (at & 127)) & 127, 1)
            return jnp.where(lane == j, moved, acc)

        halves.append(lax.fori_loop(0, NZ, pick, jnp.zeros((8, NZ), F32), unroll=8))
    samples = jnp.concatenate(halves, axis=1)
    row8 = row_of((8, PATCH))
    samples = jnp.where(row8 < 6, samples, jnp.where(row8 == 6, cell_row[...].astype(F32), 0.0))
    owner = jnp.broadcast_to(owner_row[...], (PATCH, PATCH))
    rows, lanes = row_of((PATCH, PATCH)), lane_of((PATCH, PATCH))
    owner_col = jnp.sum(jnp.where(rows == lanes, owner, 0), axis=1, keepdims=True)
    earlier = (owner == owner_col) & (rows < lanes)
    rank = jnp.sum(jnp.where(earlier, 1, 0), axis=0, keepdims=True)
    slot = row_of((NZ, PATCH))
    spread = jnp.where(
        (slot >> 3) == rank, jnp.concatenate([samples] * (NZ // 8), axis=0), 0.0
    )
    hot = jnp.where(slot == owner[:NZ], 1.0, 0.0)
    send[...] = lax.dot_general(
        hot, spread, (((1,), (1,)), ((), ())),
        precision=lax.Precision.HIGHEST, preferred_element_type=F32,
    )


def sine_cosine(v):
    k = jnp.floor(v * (2.0 / math.pi) + 0.5)
    r = ((v - k * 1.5703125) - k * 4.837512969970703125e-4) - k * 7.54978995489188e-8
    z = r * r
    s = ((-1.9515295891e-4 * z + 8.3321608736e-3) * z - 1.6666654611e-1) * z * r + r
    c = ((2.443315711809948e-5 * z - 1.388731625493765e-3) * z + 4.166664568298827e-2) * (z * z)
    c = c - 0.5 * z + 1.0
    q = k.astype(jnp.int32)
    odd = (q & 1) == 1
    sine, cosine = jnp.where(odd, c, s), jnp.where(odd, s, c)
    sine = jnp.where((q & 2) == 2, -sine, sine)
    cosine = jnp.where(((q + 1) & 2) == 2, -cosine, cosine)
    return sine, cosine


def sector_body(recv, far):
    sector = lax.axis_index("gx") * NBY + lax.axis_index("gy")
    angle = lane_of((8, NZ)).astype(F32)
    sin_theta, cos_theta = sine_cosine(math.pi * (angle + 0.5) / NZ)
    turn = jnp.full((8, NZ), sector, jnp.int32).astype(F32) * (2.0 * math.pi / (NB * NBY))
    sin_phi, cos_phi = sine_cosine(turn)
    sin_theta, cos_theta = sin_theta[0:1], cos_theta[0:1]
    sin_phi, cos_phi = sin_phi[0:1], cos_phi[0:1]
    values = recv[...]
    flipped = jnp.transpose(values)
    source = row_of((NZ, 1))
    base_x, base_y = (source >> 2) * CX, (source & 3) * CY
    sine_sum = jnp.zeros((8, NZ), F32)
    cosine_sum = jnp.zeros((8, NZ), F32)
    for k in range(SLOTS):
        cells = values[:, 8 * k + 6 : 8 * k + 7].astype(jnp.int32)
        line = cells >> 7
        x = (line * 2731) >> 16
        px = (base_x + x).astype(F32)
        py = (base_y + line - x * CY).astype(F32)
        pz = (cells & 127).astype(F32)
        phase = KAPPA * (
            (px * sin_theta * cos_phi + py * sin_theta * sin_phi) + pz * cos_theta
        )
        sine, cosine = sine_cosine(phase)
        part = flipped[8 * k : 8 * k + 8]
        sine_sum += jnp.dot(
            part, sine, precision=lax.Precision.HIGHEST, preferred_element_type=F32
        )
        cosine_sum += jnp.dot(
            part, cosine, precision=lax.Precision.HIGHEST, preferred_element_type=F32
        )
    scale = 1.0 / math.sqrt(PATCH)
    far[0:6, :] = cosine_sum[0:6] * scale
    far[6:12, :] = sine_sum[0:6] * scale


def shift(value, axis, by):
    count = lax.axis_size(axis)
    return lax.ppermute(value, axis, [(i, (i + by) % count) for i in range(count)])


def local(fields, material, permittivity, patch_cell, patch_owner):
    f = fields.reshape(6 * CX * CY, NZ)
    mat = material.reshape(CX * CY, NZ)
    plane, cells = (len(XC) * CY, NZ), (CX * CY, NZ)
    xh, xl, yh, yl, eps = call(
        edges_body,
        [plane, plane, (11 * CX, NZ), (11 * CX, NZ), cells],
        [f, mat, permittivity],
        smem=(2,),
    )
    xlo, xhi = shift(xh, "gx", 1), shift(xl, "gx", -1)
    ylo, yhi = shift(yh, "gy", 1), shift(yl, "gy", -1)
    tall = (CX * ROWS, NZ)
    sol, lsp, rsp, send = call(
        first_body,
        [(6 * CX * ROWS, NZ), tall, tall, (ROWS * 16, NZ)],
        [f, eps, xlo, xhi, ylo, yhi],
        [(6 * 128, NZ), (4 * 128, NZ), (4 * 128, NZ), (128, NZ), tall],
    )
    rec = lax.all_to_all(send.reshape(NB, 16, NZ), "gx", 0, 0, tiled=True)
    (back,) = call(join_body, [(NB * 16, NZ)], [rec.reshape(NB * 16, NZ)], [(NB * 8, NZ)] * 4)
    back = lax.all_to_all(back.reshape(NB, 16, NZ), "gx", 0, 0, tiled=True)
    soly, ly, ry, rec = call(
        second_body,
        [(6 * CX * CY, NZ), cells, cells, (16 * CX, NZ)],
        [back.reshape(NB * 16, NZ), sol, lsp, rsp, eps],
        [(6 * CX * ROWS, NZ), (6 * ROWS, NZ), (6 * ROWS, NZ), (6 * CX * CY, NZ), cells, cells],
    )
    others = [shift(rec, "gy", k) for k in (1, 2, 3)]
    new, send = call(
        finish_body,
        [(6 * CX * CY, NZ), (NB * NBY, NZ)],
        [
            rec, *others, soly, ly, ry,
            patch_cell, patch_cell.reshape(1, PATCH), patch_owner.reshape(1, PATCH),
        ],
        [(NBY * 16 * CX, NZ), (6 * CX, NZ), (6 * CX, NZ), (CX * CY * 8, NZ)],
        smem=(7,),
    )
    recv = lax.all_to_all(send, ("gx", "gy"), 0, 0, tiled=True)
    (far,) = call(sector_body, [(12, NZ)], [recv])
    return new.reshape(6, CX, CY, NZ), far


def solution(mesh):
    return jax.shard_map(
        local,
        mesh=mesh,
        in_specs=(
            P(None, "gx", "gy", None),
            P("gx", "gy", None),
            P(),
            P(("gx", "gy")),
            P(("gx", "gy"), None),
        ),
        out_specs=(P(None, "gx", "gy", None), P(None, ("gx", "gy"))),
        check_vma=False,
    )
```

profile of v0, /device:TPU:1, one launch (start us, length us, event | category | flops | bytes accessed | tf_op | source)
XLA Modules:
  0.0 80.9 jit_solution(12213550166467783042)
XLA Ops:
  0.6 1.3 %copy-done = f32[6,16,24,128]{3,2,1,0:T(8,128)S(1)} copy-done((f32[6,16,24,128]{3,2,1,0:T(8,128)S(1)}, f32[6,16,24,128]{3,2,1,0:T(8,128)}, u32[]{:S(2)}) %copy-start) | copy-done | bytes 1179672
  1.9 0.9 %copy-done.1 = s32[16,24,128]{2,1,0:T(8,128)S(1)} copy-done((s32[16,24,128]{2,1,0:T(8,128)S(1)}, s32[16,24,128]{2,1,0:T(8,128)}, u32[]{:S(2)}) %copy-start.1) | copy-done | bytes 196632
  2.8 0.7 copy-done.4
  3.5 0.8 shard_map.68
  4.3 2.1 %collective-permute-start.2 = (f32[176,128]{1,0:T(8,128)S(1)}, f32[176,128]{1,0:T(8,128)S(1)}, u32[]{:S(2)}, u32[]{:S(2)}) collective-permute-start(f32[176,128]{1,0:T(8,128)S(1)} %get-tuple-element.20), channel_id=1, source_target_pairs={{0,1},{1,2},{2,3},{3,0},{4,5},{5,6},{6,7},{7,4},{8,9},{9,10},{10,1... | collective-permute-start | bytes 270344 | tf_op jit(solution)/shard_map/ppermute | solution.py:459
  6.4 1.3 %collective-permute-start.3 = (f32[176,128]{1,0:T(8,128)S(1)}, f32[176,128]{1,0:T(8,128)S(1)}, u32[]{:S(2)}, u32[]{:S(2)}) collective-permute-start(f32[176,128]{1,0:T(8,128)S(1)} %get-tuple-element.21), channel_id=1, source_target_pairs={{0,3},{1,0},{2,1},{3,2},{4,7},{5,4},{6,5},{7,6},{8,11},{9,8},{10,9... | collective-permute-start | bytes 270344 | tf_op jit(solution)/shard_map/ppermute | solution.py:459
  7.7 2.5 %collective-permute-start = (f32[96,128]{1,0:T(8,128)S(1)}, f32[96,128]{1,0:T(8,128)S(1)}, u32[]{:S(2)}, u32[]{:S(2)}) collective-permute-start(f32[96,128]{1,0:T(8,128)S(1)} %get-tuple-element.18), channel_id=1, source_target_pairs={{0,4},{4,8},{8,12},{12,16},{16,20},{20,24},{24,28},{28,32},{32,36}... | collective-permute-start | bytes 147464 | tf_op jit(solution)/shard_map/ppermute | solution.py:459
  10.3 1.2 %collective-permute-done.xlo = f32[96,128]{1,0:T(8,128)S(1)} collective-permute-done((f32[96,128]{1,0:T(8,128)S(1)}, f32[96,128]{1,0:T(8,128)S(1)}, u32[]{:S(2)}, u32[]{:S(2)}) %collective-permute-start) | collective-permute-done | bytes 49184 | tf_op jit(solution)/shard_map/ppermute | solution.py:459
  11.5 2.3 %collective-permute-done.1.xhi = f32[96,128]{1,0:T(8,128)S(1)} collective-permute-done((f32[96,128]{1,0:T(8,128)S(1)}, f32[96,128]{1,0:T(8,128)S(1)}, u32[]{:S(2)}, u32[]{:S(2)}) %collective-permute-start.1) | collective-permute-done | bytes 49184 | tf_op jit(solution)/shard_map/ppermute | solution.py:459
  13.8 0.0 collective-permute-done.2.ylo
  13.8 2.3 %shard_map.69 = (f32[3072,128]{1,0:T(8,128)S(1)}, f32[512,128]{1,0:T(8,128)S(1)}, f32[512,128]{1,0:T(8,128)S(1)}, f32[512,128]{1,0:T(8,128)S(1)}) custom-call(f32[2304,128]{1,0:T(8,128)S(1)} %bitcast.14, f32[384,128]{1,0:T(8,128)S(1)} %get-tuple-element.17.eps, f32[96,128]{1,0:T(8,128)S(1)} %collective-permute-done.xlo, ...), custom_call_target="tpu_custom_call" | custom-call | tf_op jit(solution)/shard_map/pallas_call | solution.py:31
  16.1 18.4 %all_to_all.21 = f32[32,16,128]{2,1,0:T(8,128)S(1)} all-to-all(f32[32,16,128]{2,1,0:T(8,128)S(1)} %bitcast.18), channel_id=1, replica_groups=mesh['gx'=32,'gy'=4] {'gx'}, dimensions={0} | all-to-all | bytes 524288 | tf_op jit(solution)/shard_map/all_to_all | solution.py:481
  34.5 0.5 shard_map.70
  35.0 12.5 %all_to_all.22 = f32[32,16,128]{2,1,0:T(8,128)S(1)} all-to-all(f32[32,16,128]{2,1,0:T(8,128)S(1)} %bitcast.17), channel_id=1, replica_groups=mesh['gx'=32,'gy'=4] {'gx'}, dimensions={0} | all-to-all | bytes 524288 | tf_op jit(solution)/shard_map/all_to_all | solution.py:483
  47.4 2.9 %shard_map.71 = (f32[2304,128]{1,0:T(8,128)S(1)}, f32[384,128]{1,0:T(8,128)S(1)}, f32[384,128]{1,0:T(8,128)S(1)}, f32[256,128]{1,0:T(8,128)S(1)}) custom-call(f32[512,128]{1,0:T(8,128)S(1)} %bitcast.15, f32[3072,128]{1,0:T(8,128)S(1)} %get-tuple-element.23.sol, f32[512,128]{1,0:T(8,128)S(1)} %get-tuple-element.24.lsp, f32[512,128]{1,0:T(8,128)S(1)} %get-tuple-element.25.rsp, ...), custom_call_target="tpu_custom_call" | custom-call | tf_op jit(solution)/shard_map/pallas_call | solution.py:31
  50.3 1.3 %collective-permute-start.6 = (f32[256,128]{1,0:T(8,128)S(1)}, f32[256,128]{1,0:T(8,128)S(1)}, u32[]{:S(2)}, u32[]{:S(2)}) collective-permute-start(f32[256,128]{1,0:T(8,128)S(1)} %get-tuple-element.26.rec0), channel_id=1, source_target_pairs={{0,3},{1,0},{2,1},{3,2},{4,7},{5,4},{6,5},{7,6},{8,11},{9,8},{10,9... | collective-permute-start | bytes 393224 | tf_op jit(solution)/shard_map/ppermute | solution.py:459
  51.6 0.5 collective-permute-start.5
  52.2 0.6 collective-permute-start.4
  52.8 2.5 %collective-permute-done.6.rec3 = f32[256,128]{1,0:T(8,128)S(1)} collective-permute-done((f32[256,128]{1,0:T(8,128)S(1)}, f32[256,128]{1,0:T(8,128)S(1)}, u32[]{:S(2)}, u32[]{:S(2)}) %collective-permute-start.6) | collective-permute-done | bytes 131104 | tf_op jit(solution)/shard_map/ppermute | solution.py:459
  55.2 2.5 %collective-permute-done.5.rec2 = f32[256,128]{1,0:T(8,128)S(1)} collective-permute-done((f32[256,128]{1,0:T(8,128)S(1)}, f32[256,128]{1,0:T(8,128)S(1)}, u32[]{:S(2)}, u32[]{:S(2)}) %collective-permute-start.5) | collective-permute-done | bytes 131104 | tf_op jit(solution)/shard_map/ppermute | solution.py:459
  57.7 3.7 %collective-permute-done.4.rec1 = f32[256,128]{1,0:T(8,128)S(1)} collective-permute-done((f32[256,128]{1,0:T(8,128)S(1)}, f32[256,128]{1,0:T(8,128)S(1)}, u32[]{:S(2)}, u32[]{:S(2)}) %collective-permute-start.4) | collective-permute-done | bytes 131104 | tf_op jit(solution)/shard_map/ppermute | solution.py:459
  61.4 5.0 %shard_map.72 = (f32[2304,128]{1,0:T(8,128)}, f32[128,128]{1,0:T(8,128)S(1)}) custom-call(f32[256,128]{1,0:T(8,128)S(1)} %get-tuple-element.26.rec0, f32[256,128]{1,0:T(8,128)S(1)} %collective-permute-done.4.rec1, f32[256,128]{1,0:T(8,128)S(1)} %collective-permute-done.5.rec2, f32[256,128]{1,0:T(8,128)S(1)} %collective-permute-done.6.rec3, ...), custom_call_target="tpu_custom_call" | custom-call | tf_op jit(solution)/shard_map/pallas_call | solution.py:31
  66.3 13.1 %all_to_all.23 = f32[128,1,128]{2,1,0:T(1,128)S(1)} all-to-all(f32[128,1,128]{2,1,0:T(1,128)S(1)} %bitcast.21), channel_id=1, replica_groups=mesh['gx'=32,'gy'=4] {'gx','gy'}, dimensions={0} | all-to-all | bytes 131072 | tf_op jit(solution)/shard_map/all_to_all | solution.py:501
  79.4 1.4 %shard_map.73 = f32[12,128]{1,0:T(8,128)} custom-call(f32[128,128]{1,0:T(8,128)S(1)} %bitcast.19), custom_call_target="tpu_custom_call" | custom-call | tf_op jit(solution)/shard_map/pallas_call | solution.py:31
  (9 shorter events, 0.0 us)
Async XLA Ops:
  0.6 1.3 %copy-start = (f32[6,16,24,128]{3,2,1,0:T(8,128)S(1)}, f32[6,16,24,128]{3,2,1,0:T(8,128)}, u32[]{:S(2)}) copy-start(f32[6,16,24,128]{3,2,1,0:T(8,128)} %param.5) | copy-start | bytes 3538948
  1.9 0.9 %copy-start.1 = (s32[16,24,128]{2,1,0:T(8,128)S(1)}, s32[16,24,128]{2,1,0:T(8,128)}, u32[]{:S(2)}) copy-start(s32[16,24,128]{2,1,0:T(8,128)} %param.6) | copy-start | bytes 589828
  2.8 0.7 copy-start.4
  4.3 9.5 %collective-permute-start.2 = (f32[176,128]{1,0:T(8,128)S(1)}, f32[176,128]{1,0:T(8,128)S(1)}, u32[]{:S(2)}, u32[]{:S(2)}) collective-permute-start(f32[176,128]{1,0:T(8,128)S(1)} %get-tuple-element.20), channel_id=1, source_target_pairs={{0,1},{1,2},{2,3},{3,0},{4,5},{5,6},{6,7},{7,4},{8,9},{9,10},{10,1... | collective-permute-start | bytes 270344 | tf_op jit(solution)/shard_map/ppermute | solution.py:459
  6.4 7.4 %collective-permute-start.3 = (f32[176,128]{1,0:T(8,128)S(1)}, f32[176,128]{1,0:T(8,128)S(1)}, u32[]{:S(2)}, u32[]{:S(2)}) collective-permute-start(f32[176,128]{1,0:T(8,128)S(1)} %get-tuple-element.21), channel_id=1, source_target_pairs={{0,3},{1,0},{2,1},{3,2},{4,7},{5,4},{6,5},{7,6},{8,11},{9,8},{10,9... | collective-permute-start | bytes 270344 | tf_op jit(solution)/shard_map/ppermute | solution.py:459
  7.7 3.7 %collective-permute-start = (f32[96,128]{1,0:T(8,128)S(1)}, f32[96,128]{1,0:T(8,128)S(1)}, u32[]{:S(2)}, u32[]{:S(2)}) collective-permute-start(f32[96,128]{1,0:T(8,128)S(1)} %get-tuple-element.18), channel_id=1, source_target_pairs={{0,4},{4,8},{8,12},{12,16},{16,20},{20,24},{24,28},{28,32},{32,36}... | collective-permute-start | bytes 147464 | tf_op jit(solution)/shard_map/ppermute | solution.py:459
  10.3 3.5 %collective-permute-start.1 = (f32[96,128]{1,0:T(8,128)S(1)}, f32[96,128]{1,0:T(8,128)S(1)}, u32[]{:S(2)}, u32[]{:S(2)}) collective-permute-start(f32[96,128]{1,0:T(8,128)S(1)} %get-tuple-element.19), channel_id=1, source_target_pairs={{0,124},{4,0},{8,4},{12,8},{16,12},{20,16},{24,20},{28,24},{32,28}... | collective-permute-start | bytes 147464 | tf_op jit(solution)/shard_map/ppermute | solution.py:459
  47.4 14.0 %copy-start.2 = (s32[256]{0:T(256)S(1)}, s32[256]{0:T(256)}, u32[]{:S(2)}) copy-start(s32[256]{0:T(256)} %cell.1) | copy-start | bytes 3076
  47.4 14.0 %copy-start.3 = (s32[256,1]{0,1:T(1,128)S(1)}, s32[256,1]{0,1:T(1,128)}, u32[]{:S(2)}) copy-start(s32[256,1]{0,1:T(1,128)} %param.9) | copy-start | bytes 3076
  50.3 4.9 %collective-permute-start.6 = (f32[256,128]{1,0:T(8,128)S(1)}, f32[256,128]{1,0:T(8,128)S(1)}, u32[]{:S(2)}, u32[]{:S(2)}) collective-permute-start(f32[256,128]{1,0:T(8,128)S(1)} %get-tuple-element.26.rec0), channel_id=1, source_target_pairs={{0,3},{1,0},{2,1},{3,2},{4,7},{5,4},{6,5},{7,6},{8,11},{9,8},{10,9... | collective-permute-start | bytes 393224 | tf_op jit(solution)/shard_map/ppermute | solution.py:459
  51.6 6.1 %collective-permute-start.5 = (f32[256,128]{1,0:T(8,128)S(1)}, f32[256,128]{1,0:T(8,128)S(1)}, u32[]{:S(2)}, u32[]{:S(2)}) collective-permute-start(f32[256,128]{1,0:T(8,128)S(1)} %get-tuple-element.26.rec0), channel_id=1, source_target_pairs={{0,2},{1,3},{2,0},{3,1},{4,6},{5,7},{6,4},{7,5},{8,10},{9,11},{10,... | collective-permute-start | bytes 393224 | tf_op jit(solution)/shard_map/ppermute | solution.py:459
  52.2 9.2 %collective-permute-start.4 = (f32[256,128]{1,0:T(8,128)S(1)}, f32[256,128]{1,0:T(8,128)S(1)}, u32[]{:S(2)}, u32[]{:S(2)}) collective-permute-start(f32[256,128]{1,0:T(8,128)S(1)} %get-tuple-element.26.rec0), channel_id=1, source_target_pairs={{0,1},{1,2},{2,3},{3,0},{4,5},{5,6},{6,7},{7,4},{8,9},{9,10},{10,1... | collective-permute-start | bytes 393224 | tf_op jit(solution)/shard_map/ppermute | solution.py:459
where the time goes:
time: 81.2 us; the launch traced here: 80.9 us
  blocking collectives  44 us (54%)
  Pallas kernels  12.8 us (16%)
  waiting for transfers between devices  12.1 us (15%)
  starting transfers between devices  8.46 us (10%)
  local copies, waits for them, and re-layouts  2.85 us (4%)
    all_to_all x1, blocking collectives, local(): rec = lax.all_to_all(send.reshape(NB, 16, NZ), 'gx', 0, 0, tiled=True)  18.4 us
    all_to_all x1, blocking collectives, local(): recv = lax.all_to_all(send, ('gx', 'gy'), 0, 0, tiled=True)  13.1 us
    pallas_call x6, Pallas kernels, call(): pl.pallas_call(body, out_shape=[jax.ShapeDtypeStruct(s, F32) for s in out...  12.8 us
    all_to_all x1, blocking collectives, local(): back = lax.all_to_all(back.reshape(NB, 16, NZ), 'gx', 0, 0, tiled=True)  12.5 us
    ppermute x7, waiting for transfers between devices, shift(): lax.ppermute(value, axis, [(i, (i + by) % count) for i in range(count)])  12.1 us
    ppermute x7, starting transfers between devices, shift(): lax.ppermute(value, axis, [(i, (i + by) % count) for i in range(count)])  8.46 us
    unnamed x10, local copies, waits for them, and re-layouts  2.85 us
  transfers between devices with their start and end apart: 7, of which 5 were waited for; matrix products, arithmetic and copies ran while one was open for 0% of the time, Pallas kernels for 0%

commit v1 on v0

v1 whole, which is shorter than its diff:
```python
import math

import jax
import jax.numpy as jnp
from jax import lax
from jax.experimental import pallas as pl
from jax.experimental.pallas import tpu as pltpu
from jax.sharding import PartitionSpec as P

F32 = jnp.float32
CX, CY, NZ = 16, 24, 128
NB = 32
NBY = 4
ROWS = 32
HALF = 32.0
XC = (1, 2, 4, 5)
YC = (0, 2, 3, 5)
SLOTS = 4
PATCH = 256
KAPPA = 0.5
PICKS = 32
COST = 4_000_000
VM = 63


def ds(start, size, stride=None):
    return pl.ds(start, size) if stride is None else pl.ds(start, size, stride=stride)


def call(body, outs, args, scratch=(), smem=(), hbm=(), hbm_outs=(), sems=0, cost=0, vmem=40):
    def place(i, slow):
        if i in slow:
            return pl.BlockSpec(memory_space=pltpu.HBM)
        return pl.BlockSpec(memory_space=pltpu.SMEM if slow is hbm and i in smem else pltpu.VMEM)

    shapes = [o if isinstance(o, jax.ShapeDtypeStruct) else jax.ShapeDtypeStruct(o, F32) for o in outs]
    space = [o if not isinstance(o, tuple) else pltpu.VMEM(o, F32) for o in scratch]
    if sems:
        space.append(pltpu.SemaphoreType.DMA((sems,)))
    estimate = None
    if cost:
        estimate = pl.CostEstimate(flops=cost, bytes_accessed=cost, transcendentals=0)
    return pl.pallas_call(
        body,
        out_shape=shapes,
        in_specs=[place(i, hbm) for i in range(len(args))],
        out_specs=[place(i, hbm_outs) for i in range(len(outs))],
        scratch_shapes=space,
        cost_estimate=estimate,
        compiler_params=pltpu.CompilerParams(vmem_limit_bytes=vmem * 1024 * 1024),
    )(*args)


def flag(cond):
    return jnp.where(cond, 1.0, 0.0).astype(F32)


def row_of(shape):
    return lax.broadcasted_iota(jnp.int32, shape, 0)


def lane_of(shape):
    return lax.broadcasted_iota(jnp.int32, shape, 1)


def diff_z(f):
    lane = lane_of(f.shape)
    up = jnp.where(lane == NZ - 1, 0.0, pltpu.roll(f, NZ - 1, 1))
    down = jnp.where(lane == 0, 0.0, pltpu.roll(f, 1, 1))
    return up - down


def diff_y(f, below, above):
    row = row_of(f.shape)
    up = jnp.where(row == CY - 1, above, pltpu.roll(f, CY - 1, 0))
    down = jnp.where(row == 0, below, pltpu.roll(f, 1, 0))
    return up - down


def right_sides(f, s, dx, dy, dz):
    curl_h = (dy[5] - dz[4], dz[3] - dx[5], dx[4] - dy[3])
    curl_e = (dy[2] - dz[1], dz[0] - dx[2], dx[1] - dy[0])
    electric = [s * f[m] + (0.5 / HALF) * curl_h[m] for m in range(3)]
    magnetic = [s * (f[3 + m] - (0.5 * HALF) * curl_e[m]) for m in range(3)]
    return electric + magnetic


def lookup(m, perm):
    e = jnp.full(m.shape, perm[0], F32)
    for k in range(1, 16):
        e = jnp.where(m == k, perm[k], e)
    return e


def edges_body(f_hbm, mat_hbm, perm_hbm, xh, xl, yh, yl, f, mat, perm, sem):
    copies = [
        pltpu.make_async_copy(f_hbm, f, sem.at[0]),
        pltpu.make_async_copy(mat_hbm, mat, sem.at[1]),
        pltpu.make_async_copy(perm_hbm, perm, sem.at[2]),
    ]
    for copy in copies:
        copy.start()
    for copy in copies:
        copy.wait()
    for i, c in enumerate(XC):
        xh[ds(i * CY, CY), :] = f[ds((c * CX + CX - 1) * CY, CY), :]
        xl[ds(i * CY, CY), :] = f[ds(c * CX * CY, CY), :]
    for out, edge, inner in ((yh, CY - 1, CY - 2), (yl, 0, 1)):
        for c in range(6):
            out[ds(c * CX, CX), :] = f[ds(c * CX * CY + edge, CX, CY), :]
        for i, c in enumerate(YC):
            out[ds((6 + i) * CX, CX), :] = f[ds(c * CX * CY + inner, CX, CY), :]
        out[ds(10 * CX, CX), :] = lookup(mat[ds(edge, CX, CY), :], perm)


def inner_body(f, mat, perm_hbm, scaled, right, gx_out, lsp, rsp, gy_out, ly, ry, perm, yls, sem):
    copy = pltpu.make_async_copy(perm_hbm, perm, sem.at[0])
    copy.start()
    copy.wait()

    def main(c, x):
        return f[ds((c * CX + x) * CY, CY), :]

    one, zero = jnp.ones((CY, NZ), F32), jnp.zeros((CY, NZ), F32)
    wg, yl = one, one
    for x in range(CX):
        at = ds(x * CY, CY)
        s = lookup(mat[at, :], perm) * (1.0 / (HALF * HALF))
        scaled[at, :] = s
        w = s + wg
        g = 1.0 / (1.0 + w)
        wg = w * g
        gx_out[at, :] = g
        yl = yl * g
        lsp[at, :] = yl
        fm = [main(c, x) for c in range(6)]
        dx, dy, dz = {}, {}, {}
        for c in XC:
            up = main(c, x + 1) if x < CX - 1 else zero
            down = main(c, x - 1) if x > 0 else zero
            dx[c] = up - down
        for c in YC:
            dy[c] = diff_y(fm[c], 0.0, 0.0)
        for c in (0, 1, 3, 4):
            dz[c] = diff_z(fm[c])
        for c, r in enumerate(right_sides(fm, s, dx, dy, dz)):
            right[ds((c * CX + x) * CY, CY), :] = r
    ul, ur = zero, one
    for x in reversed(range(CX)):
        at = ds(x * CY, CY)
        g = gx_out[at, :]
        ul = lsp[at, :] + g * ul
        ur = g * ur
        lsp[at, :] = ul
        rsp[at, :] = ur
    one, zero = jnp.ones((CX, NZ), F32), jnp.zeros((CX, NZ), F32)
    wg, yl = one, one
    for y in range(CY):
        w = scaled[ds(y, CX, CY), :] + wg
        g = 1.0 / (1.0 + w)
        wg = w * g
        gy_out[ds(y * CX, CX), :] = g
        yl = yl * g
        yls[ds(y * CX, CX), :] = yl
    ul, ur = zero, one
    for y in reversed(range(CY)):
        g = gy_out[ds(y * CX, CX), :]
        ul = yls[ds(y * CX, CX), :] + g * ul
        ur = g * ur
        ly[ds(y, CX, CY), :] = ul
        ry[ds(y, CX, CY), :] = ur


def first_body(
    f, scaled, right, gxs, lsp, rsp, xlo, xhi, ylo, yhi,
    sol, lsp_h, rsp_h, send, ht, hu, hd, he, gs,
):
    gx, gy = lax.axis_index("gx"), lax.axis_index("gy")
    mxl, mxh = flag(gx > 0), flag(gx < NB - 1)
    myl, myh = flag(gy > 0), flag(gy < NBY - 1)
    ht[...] = jnp.zeros(ht.shape, F32)
    hu[...] = jnp.zeros(hu.shape, F32)
    hd[...] = jnp.zeros(hd.shape, F32)
    he[...] = jnp.ones(he.shape, F32)
    for c in range(6):
        ht[ds(c * 128, CX, 8), :] = ylo[ds(c * CX, CX), :] * myl
        ht[ds(c * 128 + 1, CX, 8), :] = yhi[ds(c * CX, CX), :] * myh
    for i, c in enumerate(YC):
        hu[ds(i * 128, CX, 8), :] = f[ds(c * CX * CY, CX, CY), :]
        hu[ds(i * 128 + 1, CX, 8), :] = yhi[ds((6 + i) * CX, CX), :] * myh
        hd[ds(i * 128, CX, 8), :] = ylo[ds((6 + i) * CX, CX), :] * myl
        hd[ds(i * 128 + 1, CX, 8), :] = f[ds(c * CX * CY + CY - 1, CX, CY), :]
    he[ds(0, CX, 8), :] = jnp.where(myl > 0, ylo[ds(10 * CX, CX), :], 1.0)
    he[ds(1, CX, 8), :] = jnp.where(myh > 0, yhi[ds(10 * CX, CX), :], 1.0)
    row8 = row_of((8, NZ))
    inside = jnp.where(row8 == 0, myl, jnp.where(row8 == 1, myh, 0.0))
    zero8, one8 = jnp.zeros((8, NZ), F32), jnp.ones((8, NZ), F32)
    e_scale, h_scale = 0.5 / HALF, 0.5 * HALF

    def halo(ref, i, x):
        return ref[ds(i * 128 + x * 8, 8), :]

    def x_side(i, x):
        if x == 0:
            return -xlo[ds(i * CY, CY), :] * mxl
        return xhi[ds(i * CY, CY), :] * mxh

    wg, yl = one8, one8
    ys = [jnp.zeros((ROWS, NZ), F32)] * 6
    for x in range(CX):
        fh = [halo(ht, c, x) for c in range(6)]
        dx, dy, dz = {}, {}, {}
        for c in XC:
            up = halo(ht, c, x + 1) if x < CX - 1 else zero8
            down = halo(ht, c, x - 1) if x > 0 else zero8
            dx[c] = up - down
        for i, c in enumerate(YC):
            dy[c] = halo(hu, i, x) - halo(hd, i, x)
        for c in (0, 1, 3, 4):
            dz[c] = diff_z(fh[c])
        s_h = halo(he, 0, x) * (1.0 / (HALF * HALF))
        right_h = right_sides(fh, s_h, dx, dy, dz)
        w = s_h + wg
        g_h = 1.0 / (1.0 + w)
        wg = w * g_h
        yl = yl * g_h
        gs[ds(x * 8, 8), :] = g_h
        lsp_h[ds(x * 8, 8), :] = yl
        s = scaled[ds(x * CY, CY), :]
        g = jnp.concatenate([gxs[ds(x * CY, CY), :], g_h], axis=0)
        own = [right[ds((c * CX + x) * CY, CY), :] for c in range(6)]
        if x in (0, CX - 1):
            own[1] = own[1] - e_scale * x_side(3, x)
            own[2] = own[2] + e_scale * x_side(2, x)
            own[4] = own[4] + h_scale * s * x_side(1, x)
            own[5] = own[5] - h_scale * s * x_side(0, x)
        side = {}
        for c in YC:
            low = jnp.where(row8 == 0, -fh[c][0:1], 0.0)
            high = jnp.where(row8 == 7, fh[c][1:2], 0.0)
            side[c] = (low, high)

        def at_rows(value, weight, c):
            low, high = side[c]
            return jnp.concatenate(
                [value[:8] + weight[:8] * low, value[8:16], value[16:] + weight[16:] * high], axis=0
            )

        h_weight = h_scale * s
        e_weight = jnp.full((CY, NZ), e_scale, F32)
        own[0] = at_rows(own[0], e_weight, 5)
        own[2] = at_rows(own[2], -e_weight, 3)
        own[3] = at_rows(own[3], -h_weight, 2)
        own[5] = at_rows(own[5], h_weight, 0)
        for c in range(6):
            r = jnp.concatenate([own[c], right_h[c] * inside], axis=0)
            ys[c] = (r + ys[c]) * g
            sol[ds((c * CX + x) * ROWS, ROWS), :] = ys[c]
    tail = list(ys)
    ul, ur, us = zero8, one8, [jnp.zeros((ROWS, NZ), F32)] * 6
    right_last = None
    for x in reversed(range(CX)):
        g_h = gs[ds(x * 8, 8), :]
        g = jnp.concatenate([gxs[ds(x * CY, CY), :], g_h], axis=0)
        ul = lsp_h[ds(x * 8, 8), :] + g_h * ul
        ur = g_h * ur
        if x == CX - 1:
            right_last = ur
        lsp_h[ds(x * 8, 8), :] = ul
        rsp_h[ds(x * 8, 8), :] = ur
        for c in range(6):
            here = ds((c * CX + x) * ROWS, ROWS)
            us[c] = sol[here, :] + g * us[c]
            sol[here, :] = us[c]
    lead = us
    last = CX - 1
    left_first = jnp.concatenate([lsp[ds(0, CY), :], ul], axis=0)
    right_first = jnp.concatenate([rsp[ds(0, CY), :], ur], axis=0)
    right_last = jnp.concatenate([rsp[ds(last * CY, CY), :], right_last], axis=0)

    def with_halo(value, extra):
        return jnp.concatenate([value[:CY], extra], axis=0)

    lead_rows, tail_rows = list(lead), list(tail)
    lead_rows[1] = with_halo(lead[1], halo(ht, 1, 0))
    tail_rows[1] = with_halo(tail[1], halo(ht, 1, last))
    lead_rows[4] = with_halo(lead[4], halo(he, 0, 0) * e_scale)
    tail_rows[4] = with_halo(tail[4], halo(he, 0, last) * e_scale)
    lead_rows[2] = with_halo(lead[2], lead[2][CY:] + e_scale * halo(ht, 4, 0))
    tail_rows[2] = with_halo(tail[2], tail[2][CY:] - e_scale * halo(ht, 4, last))
    for c in range(6):
        send[ds(c, ROWS, 16), :] = lead_rows[c]
        send[ds(8 + c, ROWS, 16), :] = tail_rows[c]
    send[ds(6, ROWS, 16), :] = left_first
    send[ds(7, ROWS, 16), :] = right_first
    send[ds(14, ROWS, 16), :] = right_first
    send[ds(15, ROWS, 16), :] = right_last


def join_body(rec, back, phis, psis, ms, ns):
    gx = lax.axis_index("gx")
    row8 = row_of((8, NZ))
    shifted = (row8 == 5) & ((gx == CY) | (gx == CY + 1))

    def line(b, k):
        return jnp.broadcast_to(rec[ds(b * 16 + k, 1), :], (8, NZ))

    def shifts(b):
        low = high = jnp.zeros((8, NZ), F32)
        if b > 0:
            low = jnp.where(shifted, line(b, 4) * line(b - 1, 9), 0.0)
        if b < NB - 1:
            high = jnp.where(shifted, -line(b, 12) * line(b + 1, 1), 0.0)
        return low, high

    m = n = jnp.zeros((8, NZ), F32)
    for b in range(NB):
        low, high = shifts(b)
        a, cross, d = line(b, 6), line(b, 7), line(b, 15)
        p = rec[ds(b * 16, 8), :] + a * low + cross * high
        q = rec[ds(b * 16 + 8, 8), :] + cross * low + d * high
        ms[ds(b * 8, 8), :] = m
        ns[ds(b * 8, 8), :] = n
        gain = 1.0 / (1.0 - a * n)
        phi = gain * (p + a * m)
        psi = gain * cross
        phis[ds(b * 8, 8), :] = phi
        psis[ds(b * 8, 8), :] = psi
        m = q + cross * (m + n * phi)
        n = d + cross * (n * psi)
    ahead = jnp.zeros((8, NZ), F32)
    for b in reversed(range(NB)):
        low, high = shifts(b)
        lead = phis[ds(b * 8, 8), :] + psis[ds(b * 8, 8), :] * ahead
        back[ds(b * 16, 8), :] = ms[ds(b * 8, 8), :] + ns[ds(b * 8, 8), :] * lead + low
        back[ds(b * 16 + 8, 8), :] = ahead + high
        ahead = lead


def second_body(
    back, sol, lsp, rsp, lsp_h, rsp_h, scaled, gys, ly, ry, soly, rec, mid, inc, out, r2
):
    for c in range(6):
        inc[ds(c * ROWS, ROWS), :] = back[ds(c, ROWS, 16), :]
        out[ds(c * ROWS, ROWS), :] = back[ds(8 + c, ROWS, 16), :]

    def settle(x, carry):
        at, at_h = ds(pl.multiple_of(x * CY, 8), CY), ds(pl.multiple_of(x * 8, 8), 8)
        left = jnp.concatenate([lsp[at, :], lsp_h[at_h, :]], axis=0)
        right = jnp.concatenate([rsp[at, :], rsp_h[at_h, :]], axis=0)
        for c in range(6):
            here = ds(pl.multiple_of((c * CX + x) * ROWS, 8), ROWS)
            mid[here, :] = (
                sol[here, :]
                + left * inc[ds(c * ROWS, ROWS), :]
                + right * out[ds(c * ROWS, ROWS), :]
            )
        return carry

    lax.fori_loop(0, CX, settle, 0, unroll=2)

    def main(c, x):
        return mid[ds((c * CX + x) * ROWS, CY), :]

    for x in range(CX):
        f = [main(c, x) for c in range(6)]
        dx, dy, dz = {}, {}, {}
        for c in XC:
            up = main(c, x + 1) if x < CX - 1 else out[ds(c * ROWS, CY), :]
            down = main(c, x - 1) if x > 0 else inc[ds(c * ROWS, CY), :]
            dx[c] = up - down
        for c in YC:
            edge = mid[ds((c * CX + x) * ROWS + CY, 8), :]
            dy[c] = diff_y(f[c], edge[0:1], edge[1:2])
        for c in (0, 1, 3, 4):
            dz[c] = diff_z(f[c])
        s = scaled[ds(x * CY, CY), :]
        for c, r in enumerate(right_sides(f, s, dx, dy, dz)):
            r2[ds((c * CX + x) * CY, CY), :] = r

    ys = [jnp.zeros((CX, NZ), F32)] * 6
    for y in range(CY):
        g = gys[ds(y * CX, CX), :]
        for c in range(6):
            here = ds(c * CX * CY + y, CX, CY)
            ys[c] = (r2[here, :] + ys[c]) * g
            r2[here, :] = ys[c]
    for c in range(6):
        rec[ds((8 + c) * CX, CX), :] = ys[c]
    us = [jnp.zeros((CX, NZ), F32)] * 6
    for y in reversed(range(CY)):
        g = gys[ds(y * CX, CX), :]
        for c in range(6):
            here = ds(c * CX * CY + y, CX, CY)
            us[c] = r2[here, :] + g * us[c]
            soly[here, :] = us[c]
    for c in range(6):
        rec[ds(c * CX, CX), :] = us[c]
    rec[ds(6 * CX, CX), :] = ly[ds(0, CX, CY), :]
    rec[ds(7 * CX, CX), :] = ry[ds(0, CX, CY), :]
    rec[ds(14 * CX, CX), :] = ry[ds(0, CX, CY), :]
    rec[ds(15 * CX, CX), :] = ry[ds(CY - 1, CX, CY), :]


WIDTH = NZ // SLOTS


def patches_body(cell_row, owner_row, hot, spread, ranks, table):
    gx, gy = lax.axis_index("gx"), lax.axis_index("gy")
    owner = jnp.broadcast_to(owner_row[...], (PATCH, PATCH))
    rows, lanes = row_of((PATCH, PATCH)), lane_of((PATCH, PATCH))
    owner_col = jnp.sum(jnp.where(rows == lanes, owner, 0), axis=1, keepdims=True)
    earlier = (owner == owner_col) & (rows < lanes)
    rank = jnp.sum(jnp.where(earlier, 1, 0), axis=0, keepdims=True)
    ranks[...] = jnp.broadcast_to(rank, (8, PATCH))
    hot[...] = jnp.where(row_of((NZ, PATCH)) == owner[:NZ], 1.0, 0.0)
    cell = jnp.broadcast_to(cell_row[...], (8, PATCH))
    line = cell >> 7
    x = (line * 2731) >> 16
    px, py, pz = gx * CX + x, gy * CY + line - x * CY, cell & 127
    row8 = row_of((8, PATCH))
    place = jnp.where(row8 == 0, px, jnp.where(row8 == 1, py, jnp.where(row8 == 2, pz, 0)))
    place = place.astype(F32)
    spread[...] = jnp.zeros(spread.shape, F32)
    for k in range(SLOTS):
        spread[ds(k * WIDTH + 8, 8), :] = jnp.where(ranks[...] == k, place, 0.0)
    sector = gx * NBY + gy
    angle = lane_of((8, NZ)).astype(F32)
    sin_theta, cos_theta = sine_cosine(math.pi * (angle + 0.5) / NZ)
    turn = jnp.full((8, NZ), sector, jnp.int32).astype(F32) * (2.0 * math.pi / (NB * NBY))
    sin_phi, cos_phi = sine_cosine(turn)
    table[ds(0, 8), :] = KAPPA * sin_theta * cos_phi
    table[ds(8, 8), :] = KAPPA * sin_theta * sin_phi
    table[ds(16, 8), :] = KAPPA * cos_theta


def finish_body(
    rec0, rec1, rec2, rec3, soly, ly, ry, cell, hot, static, ranks, new, send,
    value_of, inc, out, table, spread, sem,
):
    gy = lax.axis_index("gy")

    def get(rec, k):
        return rec[ds(k * CX, CX), :]

    zero = jnp.zeros((CX, NZ), F32)

    def sweep(order, up):
        m, n = [zero] * 6, zero
        near, far, own, other = (8, 0, 15, 6) if up else (0, 8, 6, 15)
        for rec, valid in order:
            cross = get(rec, 7)
            gain = 1.0 / (1.0 - get(rec, other) * n)
            value = [
                get(rec, near + c)
                + cross * (m[c] + n * (gain * (get(rec, far + c) + get(rec, other) * m[c])))
                for c in range(6)
            ]
            m = [jnp.where(valid, v, 0.0) for v in value]
            n = jnp.where(valid, get(rec, own) + cross * (n * (gain * cross)), 0.0)
        return m, n

    below, below_gain = sweep([(rec3, gy >= 3), (rec2, gy >= 2), (rec1, gy >= 1)], True)
    above, above_gain = sweep([(rec1, gy <= 0), (rec2, gy <= 1), (rec3, gy <= 2)], False)
    a, cross, d = get(rec0, 6), get(rec0, 7), get(rec0, 15)
    ll, lt = 1.0 - a * below_gain, -cross * above_gain
    tl, tt = -cross * below_gain, 1.0 - d * above_gain
    over = 1.0 / (ll * tt - lt * tl)
    for c in range(6):
        p = get(rec0, c) + a * below[c] + cross * above[c]
        q = get(rec0, 8 + c) + cross * below[c] + d * above[c]
        lead, tail = (p * tt - lt * q) * over, (ll * q - tl * p) * over
        inc[ds(c * CX, CX), :] = below[c] + below_gain * lead
        out[ds(c * CX, CX), :] = above[c] + above_gain * tail

    copies = []
    for x in range(CX):
        at = ds(x * CY, CY)
        left, right = ly[at, :], ry[at, :]
        for c in range(6):
            here = ds((c * CX + x) * CY, CY)
            value = (
                soly[here, :]
                + left * inc[ds(c * CX + x, 1), :]
                + right * out[ds(c * CX + x, 1), :]
            )
            value_of[here, :] = value
            table[ds(x * (CY * 8) + c, CY, 8), :] = value
        if x % 4 == 3:
            for c in range(6):
                part = ds((c * CX + x - 3) * CY, 4 * CY)
                copy = pltpu.make_async_copy(
                    value_of.at[part, :], new.at[part, :], sem.at[len(copies)]
                )
                copy.start()
                copies.append(copy)

    lane = lane_of((8, NZ))
    halves = []
    for half in range(PATCH // NZ):

        def pick(j, acc):
            at = cell[half * NZ + j]
            values = table[ds(pl.multiple_of((at >> 7) * 8, 8), 8), :]
            moved = pltpu.roll(values, (j - (at & 127)) & 127, 1)
            return jnp.where(lane == j, moved, acc)

        halves.append(lax.fori_loop(0, NZ, pick, jnp.zeros((8, NZ), F32), unroll=PICKS))
    samples = jnp.concatenate(halves, axis=1)
    samples = jnp.where(row_of((8, PATCH)) < 6, samples, 0.0)
    spread[...] = static[...]
    for k in range(SLOTS):
        spread[ds(k * WIDTH, 8), :] = jnp.where(ranks[...] == k, samples, 0.0)
    send[...] = lax.dot_general(
        hot[...], spread[...], (((1,), (1,)), ((), ())),
        precision=lax.Precision.HIGHEST, preferred_element_type=F32,
    )
    for copy in copies:
        copy.wait()


def sine_cosine(v):
    k = jnp.floor(v * (2.0 / math.pi) + 0.5)
    r = ((v - k * 1.5703125) - k * 4.837512969970703125e-4) - k * 7.54978995489188e-8
    z = r * r
    s = ((-1.9515295891e-4 * z + 8.3321608736e-3) * z - 1.6666654611e-1) * z * r + r
    c = ((2.443315711809948e-5 * z - 1.388731625493765e-3) * z + 4.166664568298827e-2) * (z * z)
    c = c - 0.5 * z + 1.0
    q = k.astype(jnp.int32)
    odd = (q & 1) == 1
    sine, cosine = jnp.where(odd, c, s), jnp.where(odd, s, c)
    sine = jnp.where((q & 2) == 2, -sine, sine)
    cosine = jnp.where(((q + 1) & 2) == 2, -cosine, cosine)
    return sine, cosine


def sector_body(recv, table, far):
    values = recv[...]
    flipped = jnp.transpose(values)
    along_x, along_y, along_z = (table[ds(8 * i, 1), :] for i in range(3))
    sums = jnp.zeros((8, 2 * NZ), F32)
    for k in range(SLOTS):
        px, py, pz = (values[:, k * WIDTH + 8 + i : k * WIDTH + 9 + i] for i in range(3))
        sine, cosine = sine_cosine((px * along_x + py * along_y) + pz * along_z)
        sums += jnp.dot(
            flipped[k * WIDTH : k * WIDTH + 8], jnp.concatenate([cosine, sine], axis=1),
            precision=lax.Precision.HIGHEST, preferred_element_type=F32,
        )
    scale = 1.0 / math.sqrt(PATCH)
    far[0:6, :] = sums[0:6, :NZ] * scale
    far[6:12, :] = sums[0:6, NZ:] * scale


def shift(value, axis, by):
    count = lax.axis_size(axis)
    return lax.ppermute(value, axis, [(i, (i + by) % count) for i in range(count)])


def local(fields, material, permittivity, patch_cell, patch_owner):
    f = fields.reshape(6 * CX * CY, NZ)
    mat = material.reshape(CX * CY, NZ)
    plane, cells, block = (len(XC) * CY, NZ), (CX * CY, NZ), (6 * CX * CY, NZ)
    edge, halo = (11 * CX, NZ), (CX * 8, NZ)
    table16 = pltpu.SMEM((16,), F32)
    xh, xl, yh, yl = call(
        edges_body,
        [plane, plane, edge, edge],
        [f, mat, permittivity],
        [pltpu.VMEM(block, F32), pltpu.VMEM(cells, jnp.int32), table16],
        hbm=(0, 1, 2),
        sems=3,
        vmem=VM,
    )
    xlo, xhi = shift(xh, "gx", 1), shift(xl, "gx", -1)
    ylo, yhi = shift(yh, "gy", 1), shift(yl, "gy", -1)
    scaled, right, gxs, lsp, rsp, gys, ly, ry = call(
        inner_body,
        [cells, block] + [cells] * 6,
        [f, mat, permittivity],
        [table16, cells],
        hbm=(2,),
        sems=1,
        cost=COST,
    )
    sol, lsp_h, rsp_h, send = call(
        first_body,
        [(6 * CX * ROWS, NZ), halo, halo, (ROWS * 16, NZ)],
        [f, scaled, right, gxs, lsp, rsp, xlo, xhi, ylo, yhi],
        [(6 * 128, NZ), (4 * 128, NZ), (4 * 128, NZ), halo, halo],
    )
    rec = lax.all_to_all(send.reshape(NB, 16, NZ), "gx", 0, 0, tiled=True)
    (back,) = call(join_body, [(NB * 16, NZ)], [rec.reshape(NB * 16, NZ)], [(NB * 8, NZ)] * 4)
    back = lax.all_to_all(back.reshape(NB, 16, NZ), "gx", 0, 0, tiled=True)
    soly, rec = call(
        second_body,
        [block, (16 * CX, NZ)],
        [back.reshape(NB * 16, NZ), sol, lsp, rsp, lsp_h, rsp_h, scaled, gys, ly, ry],
        [(6 * CX * ROWS, NZ), (6 * ROWS, NZ), (6 * ROWS, NZ), block],
    )
    others = [shift(rec, "gy", k) for k in (1, 2, 3)]
    hot, static, ranks, table = call(
        patches_body,
        [(NZ, PATCH), (NZ, PATCH), jax.ShapeDtypeStruct((8, PATCH), jnp.int32), (24, NZ)],
        [patch_cell.reshape(1, PATCH), patch_owner.reshape(1, PATCH)],
        cost=COST,
    )
    new, send = call(
        finish_body,
        [block, (NB * NBY, NZ)],
        [rec, *others, soly, ly, ry, patch_cell, hot, static, ranks],
        [block, (6 * CX, NZ), (6 * CX, NZ), (CX * CY * 8, NZ), (NZ, PATCH)],
        smem=(7,),
        hbm_outs=(0,),
        sems=24,
    )
    recv = lax.all_to_all(send, ("gx", "gy"), 0, 0, tiled=True)
    (far,) = call(sector_body, [(12, NZ)], [recv, table])
    return new.reshape(6, CX, CY, NZ), far


def solution(mesh):
    return jax.shard_map(
        local,
        mesh=mesh,
        in_specs=(
            P(None, "gx", "gy", None),
            P("gx", "gy", None),
            P(),
            P(("gx", "gy")),
            P(("gx", "gy"), None),
        ),
        out_specs=(P(None, "gx", "gy", None), P(None, ("gx", "gy"))),
        check_vma=False,
    )
```

time: 81.2 us -> 75.4 us (0.929)
  waiting for transfers between devices: 12.1 us -> 6.35 us
  blocking collectives: 44 us -> 46.7 us
  Pallas kernels: 12.8 us -> 10.4 us
  local copies, waits for them, and re-layouts: 2.85 us -> 1.28 us
  starting transfers between devices: 8.46 us -> 9.66 us
    ppermute x7, waiting for transfers between devices: 12.1 us -> 6.35 us  [shift(): lax.ppermute(value, axis, [(i, (i + by) % count) for i in range(count)])]
    all_to_all x1, blocking collectives: 13.1 us -> 15.9 us  [local(): recv = lax.all_to_all(send, ('gx', 'gy'), 0, 0, tiled=True)]
    pallas_call x6 -> x8, Pallas kernels: 12.8 us -> 10.4 us  [call(): pl.pallas_call(body, out_shape=shapes, in_specs=[place(i, hbm) for i in r...]
    unnamed x10, local copies, waits for them, and re-layouts: 2.85 us -> 1.28 us
    ppermute x7, starting transfers between devices: 8.46 us -> 9.66 us  [shift(): lax.ppermute(value, axis, [(i, (i + by) % count) for i in range(count)])]
  transfers between devices with their start and end apart: 7 -> 7, of which waited for: 5 -> 4; matrix products, arithmetic and copies ran while one was open for 0% -> 0% of each run, Pallas kernels for 0% -> 2%
where the time goes in v1:
time: 75.4 us; the launch traced here: 75.1 us
  blocking collectives  46.7 us (62%)
  Pallas kernels  10.4 us (14%)
  starting transfers between devices  9.66 us (13%)
  waiting for transfers between devices  6.35 us (8%)
  local copies, waits for them, and re-layouts  1.28 us (2%)
    all_to_all x1, blocking collectives, local(): rec = lax.all_to_all(send.reshape(NB, 16, NZ), 'gx', 0, 0, tiled=True)  18.4 us
    all_to_all x1, blocking collectives, local(): recv = lax.all_to_all(send, ('gx', 'gy'), 0, 0, tiled=True)  15.9 us
    all_to_all x1, blocking collectives, local(): back = lax.all_to_all(back.reshape(NB, 16, NZ), 'gx', 0, 0, tiled=True)  12.5 us
    pallas_call x8, Pallas kernels, call(): pl.pallas_call(body, out_shape=shapes, in_specs=[place(i, hbm) for i in r...  10.4 us
    ppermute x7, starting transfers between devices, shift(): lax.ppermute(value, axis, [(i, (i + by) % count) for i in range(count)])  9.66 us
    ppermute x7, waiting for transfers between devices, shift(): lax.ppermute(value, axis, [(i, (i + by) % count) for i in range(count)])  6.35 us
  transfers between devices with their start and end apart: 7, of which 4 were waited for; matrix products, arithmetic and copies ran while one was open for 0% of the time, Pallas kernels for 2%

profile of v1, /device:TPU:1, one launch (start us, length us, event | category | flops | bytes accessed | tf_op | source)
XLA Modules:
  0.0 75.1 jit_solution(11417952712532070117)
XLA Ops:
  0.6 2.1 %shard_map.69 = (f32[96,128]{1,0:T(8,128)}, f32[96,128]{1,0:T(8,128)}, f32[176,128]{1,0:T(8,128)}, f32[176,128]{1,0:T(8,128)}) custom-call(f32[2304,128]{1,0:T(8,128)} %bitcast.13, s32[384,128]{1,0:T(8,128)} %bitcast.19, f32[16]{0:T(128)} %perm_hbm.3), custom_call_target="tpu_custom_call" | custom-call | tf_op jit(solution)/shard_map/pallas_call | solution.py:43
  2.7 2.1 %collective-permute-start.2 = (f32[176,128]{1,0:T(8,128)}, f32[176,128]{1,0:T(8,128)S(1)}, u32[]{:S(2)}, u32[]{:S(2)}) collective-permute-start(f32[176,128]{1,0:T(8,128)} %get-tuple-element.33), channel_id=1, source_target_pairs={{0,1},{1,2},{2,3},{3,0},{4,5},{5,6},{6,7},{7,4},{8,9},{9,10},{10,1... | collective-permute-start | bytes 270344 | tf_op jit(solution)/shard_map/ppermute | solution.py:556
  4.9 1.3 %collective-permute-start.3 = (f32[176,128]{1,0:T(8,128)}, f32[176,128]{1,0:T(8,128)S(1)}, u32[]{:S(2)}, u32[]{:S(2)}) collective-permute-start(f32[176,128]{1,0:T(8,128)} %get-tuple-element.34), channel_id=1, source_target_pairs={{0,3},{1,0},{2,1},{3,2},{4,7},{5,4},{6,5},{7,6},{8,11},{9,8},{10,9... | collective-permute-start | bytes 270344 | tf_op jit(solution)/shard_map/ppermute | solution.py:556
  6.2 2.5 %collective-permute-start = (f32[96,128]{1,0:T(8,128)}, f32[96,128]{1,0:T(8,128)S(1)}, u32[]{:S(2)}, u32[]{:S(2)}) collective-permute-start(f32[96,128]{1,0:T(8,128)} %get-tuple-element.31), channel_id=1, source_target_pairs={{0,4},{4,8},{8,12},{12,16},{16,20},{20,24},{24,28},{28,32},{32,36}... | collective-permute-start | bytes 147464 | tf_op jit(solution)/shard_map/ppermute | solution.py:556
  8.7 0.0 copy-start
  8.8 1.3 %copy-done = f32[6,16,24,128]{3,2,1,0:T(8,128)S(1)} copy-done((f32[6,16,24,128]{3,2,1,0:T(8,128)S(1)}, f32[6,16,24,128]{3,2,1,0:T(8,128)}, u32[]{:S(2)}) %copy-start) | copy-done | bytes 1179672
  10.0 1.5 %shard_map.68 = (f32[384,128]{1,0:T(8,128)S(1)}, f32[2304,128]{1,0:T(8,128)S(1)}, f32[384,128]{1,0:T(8,128)S(1)}, f32[384,128]{1,0:T(8,128)S(1)}, f32[384,128]{1...) custom-call(f32[2304,128]{1,0:T(8,128)S(1)} %bitcast.14, ...), custom_call_target="tpu_custom_call" | custom-call | flops 4000000 | bytes 4000000 | tf_op jit(solution)/shard_map/pallas_call | solution.py:43
  11.5 0.0 collective-permute-done.xlo
  11.5 1.0 %collective-permute-done.1.xhi = f32[96,128]{1,0:T(8,128)S(1)} collective-permute-done((f32[96,128]{1,0:T(8,128)}, f32[96,128]{1,0:T(8,128)S(1)}, u32[]{:S(2)}, u32[]{:S(2)}) %collective-permute-start.1) | collective-permute-done | bytes 49184 | tf_op jit(solution)/shard_map/ppermute | solution.py:556
  12.5 0.7 shard_map.70
  13.1 18.4 %all_to_all.21 = f32[32,16,128]{2,1,0:T(8,128)S(1)} all-to-all(f32[32,16,128]{2,1,0:T(8,128)S(1)} %bitcast.21), channel_id=1, replica_groups=mesh['gx'=32,'gy'=4] {'gx'}, dimensions={0} | all-to-all | bytes 524288 | tf_op jit(solution)/shard_map/all_to_all | solution.py:591
  31.5 0.5 shard_map.71
  32.0 12.5 %all_to_all.22 = f32[32,16,128]{2,1,0:T(8,128)S(1)} all-to-all(f32[32,16,128]{2,1,0:T(8,128)S(1)} %bitcast.18), channel_id=1, replica_groups=mesh['gx'=32,'gy'=4] {'gx'}, dimensions={0} | all-to-all | bytes 524288 | tf_op jit(solution)/shard_map/all_to_all | solution.py:593
  44.4 1.5 %shard_map.72 = (f32[2304,128]{1,0:T(8,128)S(1)}, f32[256,128]{1,0:T(8,128)S(1)}) custom-call(f32[512,128]{1,0:T(8,128)S(1)} %bitcast.16, f32[3072,128]{1,0:T(8,128)S(1)} %get-tuple-element.36.sol, f32[384,128]{1,0:T(8,128)S(1)} %get-tuple-element.29.lsp, f32[384,128]{1,0:T(8,128)S(1)} %get-tuple-element.30.rsp, f32[128,128]{1,0:T(8,128)S(1)} %get-tuple-element.37.lsp_h, ...), custom_call_target="tpu_custom_call" | custom-call | tf_op jit(solution)/shard_map/pallas_call | solution.py:43
  45.9 0.1 collective-permute-start.4
  46.0 2.4 %collective-permute-start.5 = (f32[256,128]{1,0:T(8,128)S(1)}, f32[256,128]{1,0:T(8,128)S(1)}, u32[]{:S(2)}, u32[]{:S(2)}) collective-permute-start(f32[256,128]{1,0:T(8,128)S(1)} %get-tuple-element.42.rec0), channel_id=1, source_target_pairs={{0,2},{1,3},{2,0},{3,1},{4,6},{5,7},{6,4},{7,5},{8,10},{9,11},{10,... | collective-permute-start | bytes 393224 | tf_op jit(solution)/shard_map/ppermute | solution.py:556
  48.5 1.2 %collective-permute-start.6 = (f32[256,128]{1,0:T(8,128)S(1)}, f32[256,128]{1,0:T(8,128)S(1)}, u32[]{:S(2)}, u32[]{:S(2)}) collective-permute-start(f32[256,128]{1,0:T(8,128)S(1)} %get-tuple-element.42.rec0), channel_id=1, source_target_pairs={{0,3},{1,0},{2,1},{3,2},{4,7},{5,4},{6,5},{7,6},{8,11},{9,8},{10,9... | collective-permute-start | bytes 393224 | tf_op jit(solution)/shard_map/ppermute | solution.py:556
  49.6 0.2 shard_map.73
  49.8 2.5 %collective-permute-done.4.rec1 = f32[256,128]{1,0:T(8,128)S(1)} collective-permute-done((f32[256,128]{1,0:T(8,128)S(1)}, f32[256,128]{1,0:T(8,128)S(1)}, u32[]{:S(2)}, u32[]{:S(2)}) %collective-permute-start.4) | collective-permute-done | bytes 131104 | tf_op jit(solution)/shard_map/ppermute | solution.py:556
  52.3 2.4 %collective-permute-done.5.rec2 = f32[256,128]{1,0:T(8,128)S(1)} collective-permute-done((f32[256,128]{1,0:T(8,128)S(1)}, f32[256,128]{1,0:T(8,128)S(1)}, u32[]{:S(2)}, u32[]{:S(2)}) %collective-permute-start.5) | collective-permute-done | bytes 131104 | tf_op jit(solution)/shard_map/ppermute | solution.py:556
  54.7 0.4 collective-permute-done.6.rec3
  55.1 2.7 %shard_map.74 = (f32[2304,128]{1,0:T(8,128)}, f32[128,128]{1,0:T(8,128)S(1)}) custom-call(f32[256,128]{1,0:T(8,128)S(1)} %get-tuple-element.42.rec0, f32[256,128]{1,0:T(8,128)S(1)} %collective-permute-done.4.rec1, f32[256,128]{1,0:T(8,128)S(1)} %collective-permute-done.5.rec2, f32[256,128]{1,0:T(8,128)S(1)} %collective-permute-done.6.rec3, ...), custom_call_target="tpu_custom_call" | custom-call | tf_op jit(solution)/shard_map/pallas_call | solution.py:43
  57.8 15.9 %all_to_all.23 = f32[128,1,128]{2,1,0:T(1,128)S(1)} all-to-all(f32[128,1,128]{2,1,0:T(1,128)S(1)} %bitcast.23), channel_id=1, replica_groups=mesh['gx'=32,'gy'=4] {'gx','gy'}, dimensions={0} | all-to-all | bytes 131072 | tf_op jit(solution)/shard_map/all_to_all | solution.py:616
  73.7 1.4 %shard_map.75 = f32[12,128]{1,0:T(8,128)} custom-call(f32[128,128]{1,0:T(8,128)S(1)} %bitcast.22, f32[24,128]{1,0:T(8,128)S(1)} %get-tuple-element.49.table), custom_call_target="tpu_custom_call" | custom-call | tf_op jit(solution)/shard_map/pallas_call | solution.py:43
  (11 shorter events, 0.0 us)
Async XLA Ops:
  0.6 8.1 %copy-start.1 = (s32[16,24,128]{2,1,0:T(8,128)S(1)}, s32[16,24,128]{2,1,0:T(8,128)}, u32[]{:S(2)}) copy-start(s32[16,24,128]{2,1,0:T(8,128)} %param.6) | copy-start | bytes 589828
  0.6 8.1 %copy-start.2 = (f32[16]{0:T(128)S(1)}, f32[16]{0:T(128)}, u32[]{:S(2)}) copy-start(f32[16]{0:T(128)} %perm_hbm.3) | copy-start | bytes 196
  2.7 9.7 %collective-permute-start.2 = (f32[176,128]{1,0:T(8,128)}, f32[176,128]{1,0:T(8,128)S(1)}, u32[]{:S(2)}, u32[]{:S(2)}) collective-permute-start(f32[176,128]{1,0:T(8,128)} %get-tuple-element.33), channel_id=1, source_target_pairs={{0,1},{1,2},{2,3},{3,0},{4,5},{5,6},{6,7},{7,4},{8,9},{9,10},{10,1... | collective-permute-start | bytes 270344 | tf_op jit(solution)/shard_map/ppermute | solution.py:556
  4.9 7.6 %collective-permute-start.3 = (f32[176,128]{1,0:T(8,128)}, f32[176,128]{1,0:T(8,128)S(1)}, u32[]{:S(2)}, u32[]{:S(2)}) collective-permute-start(f32[176,128]{1,0:T(8,128)} %get-tuple-element.34), channel_id=1, source_target_pairs={{0,3},{1,0},{2,1},{3,2},{4,7},{5,4},{6,5},{7,6},{8,11},{9,8},{10,9... | collective-permute-start | bytes 270344 | tf_op jit(solution)/shard_map/ppermute | solution.py:556
  6.2 5.3 %collective-permute-start = (f32[96,128]{1,0:T(8,128)}, f32[96,128]{1,0:T(8,128)S(1)}, u32[]{:S(2)}, u32[]{:S(2)}) collective-permute-start(f32[96,128]{1,0:T(8,128)} %get-tuple-element.31), channel_id=1, source_target_pairs={{0,4},{4,8},{8,12},{12,16},{16,20},{20,24},{24,28},{28,32},{32,36}... | collective-permute-start | bytes 147464 | tf_op jit(solution)/shard_map/ppermute | solution.py:556
  8.7 3.7 %collective-permute-start.1 = (f32[96,128]{1,0:T(8,128)}, f32[96,128]{1,0:T(8,128)S(1)}, u32[]{:S(2)}, u32[]{:S(2)}) collective-permute-start(f32[96,128]{1,0:T(8,128)} %get-tuple-element.32), channel_id=1, source_target_pairs={{0,124},{4,0},{8,4},{12,8},{16,12},{20,16},{24,20},{28,24},{32,28}... | collective-permute-start | bytes 147464 | tf_op jit(solution)/shard_map/ppermute | solution.py:556
  8.7 1.3 %copy-start = (f32[6,16,24,128]{3,2,1,0:T(8,128)S(1)}, f32[6,16,24,128]{3,2,1,0:T(8,128)}, u32[]{:S(2)}) copy-start(f32[6,16,24,128]{3,2,1,0:T(8,128)} %param.5) | copy-start | bytes 3538948
  44.4 5.2 %copy-start.3 = (s32[256]{0:T(256)S(1)}, s32[256]{0:T(256)}, u32[]{:S(2)}) copy-start(s32[256]{0:T(256)} %cell.1) | copy-start | bytes 3076
  44.4 5.2 %copy-start.4 = (s32[256,1]{0,1:T(1,128)S(1)}, s32[256,1]{0,1:T(1,128)}, u32[]{:S(2)}) copy-start(s32[256,1]{0,1:T(1,128)} %param.9) | copy-start | bytes 3076
  45.9 6.4 %collective-permute-start.4 = (f32[256,128]{1,0:T(8,128)S(1)}, f32[256,128]{1,0:T(8,128)S(1)}, u32[]{:S(2)}, u32[]{:S(2)}) collective-permute-start(f32[256,128]{1,0:T(8,128)S(1)} %get-tuple-element.42.rec0), channel_id=1, source_target_pairs={{0,1},{1,2},{2,3},{3,0},{4,5},{5,6},{6,7},{7,4},{8,9},{9,10},{10,1... | collective-permute-start | bytes 393224 | tf_op jit(solution)/shard_map/ppermute | solution.py:556
  46.0 8.7 %collective-permute-start.5 = (f32[256,128]{1,0:T(8,128)S(1)}, f32[256,128]{1,0:T(8,128)S(1)}, u32[]{:S(2)}, u32[]{:S(2)}) collective-permute-start(f32[256,128]{1,0:T(8,128)S(1)} %get-tuple-element.42.rec0), channel_id=1, source_target_pairs={{0,2},{1,3},{2,0},{3,1},{4,6},{5,7},{6,4},{7,5},{8,10},{9,11},{10,... | collective-permute-start | bytes 393224 | tf_op jit(solution)/shard_map/ppermute | solution.py:556
  48.5 6.7 %collective-permute-start.6 = (f32[256,128]{1,0:T(8,128)S(1)}, f32[256,128]{1,0:T(8,128)S(1)}, u32[]{:S(2)}, u32[]{:S(2)}) collective-permute-start(f32[256,128]{1,0:T(8,128)S(1)} %get-tuple-element.42.rec0), channel_id=1, source_target_pairs={{0,3},{1,0},{2,1},{3,2},{4,7},{5,4},{6,5},{7,6},{8,11},{9,8},{10,9... | collective-permute-start | bytes 393224 | tf_op jit(solution)/shard_map/ppermute | solution.py:556

commit v2 on v1

--- a/solution.py
+++ b/solution.py
@@ -8,6 +8,7 @@
 from jax.sharding import PartitionSpec as P
 
 F32 = jnp.float32
+BF16 = jnp.bfloat16
 CX, CY, NZ = 16, 24, 128
 NB = 32
 NBY = 4
@@ -18,22 +19,25 @@
 SLOTS = 4
 PATCH = 256
 KAPPA = 0.5
+EDGES = (CY - 1, CY - 2, 0, 1)
 PICKS = 32
 COST = 4_000_000
-VM = 63
+VM = 56
 
 
 def ds(start, size, stride=None):
     return pl.ds(start, size) if stride is None else pl.ds(start, size, stride=stride)
 
 
-def call(body, outs, args, scratch=(), smem=(), hbm=(), hbm_outs=(), sems=0, cost=0, vmem=40):
+def call(body, outs, args, scratch=(), smem=(), hbm=(), hbm_outs=(), sems=0, cost=0, vmem=40, pinned=False):
     def place(i, slow):
         if i in slow:
             return pl.BlockSpec(memory_space=pltpu.HBM)
         return pl.BlockSpec(memory_space=pltpu.SMEM if slow is hbm and i in smem else pltpu.VMEM)
 
     shapes = [o if isinstance(o, jax.ShapeDtypeStruct) else jax.ShapeDtypeStruct(o, F32) for o in outs]
+    if pinned:
+        shapes = [pltpu.VMEM(o.shape, o.dtype) for o in shapes]
     space = [o if not isinstance(o, tuple) else pltpu.VMEM(o, F32) for o in scratch]
     if sems:
         space.append(pltpu.SemaphoreType.DMA((sems,)))
@@ -86,37 +90,45 @@
 
 
 def lookup(m, perm):
-    e = jnp.full(m.shape, perm[0], F32)
+    e = jnp.broadcast_to(perm[0], m.shape)
     for k in range(1, 16):
         e = jnp.where(m == k, perm[k], e)
     return e
 
 
-def edges_body(f_hbm, mat_hbm, perm_hbm, xh, xl, yh, yl, f, mat, perm, sem):
-    copies = [
-        pltpu.make_async_copy(f_hbm, f, sem.at[0]),
-        pltpu.make_async_copy(mat_hbm, mat, sem.at[1]),
-        pltpu.make_async_copy(perm_hbm, perm, sem.at[2]),
-    ]
-    for copy in copies:
+def edges_body(f, mat, xh, xl, yh, yl, rows, mats, sem):
+    copies = []
+
+    def fetch(source, target):
+        copy = pltpu.make_async_copy(source, target, sem.at[len(copies)])
         copy.start()
+        copies.append(copy)
+
+    for i, y in enumerate(EDGES):
+        fetch(f.at[:, ds(y, 1), :], rows.at[i])
+    for i, y in enumerate((CY - 1, 0)):
+        fetch(mat.at[:, ds(y, 1), :], mats.at[i])
+    for i, c in enumerate(XC):
+        fetch(f.at[c * CX + CX - 1], xh.at[ds(i * CY, CY), :])
+        fetch(f.at[c * CX], xl.at[ds(i * CY, CY), :])
     for copy in copies:
         copy.wait()
-    for i, c in enumerate(XC):
-        xh[ds(i * CY, CY), :] = f[ds((c * CX + CX - 1) * CY, CY), :]
-        xl[ds(i * CY, CY), :] = f[ds(c * CX * CY, CY), :]
-    for out, edge, inner in ((yh, CY - 1, CY - 2), (yl, 0, 1)):
+    for k, out in enumerate((yh, yl)):
         for c in range(6):
-            out[ds(c * CX, CX), :] = f[ds(c * CX * CY + edge, CX, CY), :]
+            out[ds(c * CX, CX), :] = rows[2 * k, ds(c * CX, CX), 0, :]
         for i, c in enumerate(YC):
-            out[ds((6 + i) * CX, CX), :] = f[ds(c * CX * CY + inner, CX, CY), :]
-        out[ds(10 * CX, CX), :] = lookup(mat[ds(edge, CX, CY), :], perm)
-
-
-def inner_body(f, mat, perm_hbm, scaled, right, gx_out, lsp, rsp, gy_out, ly, ry, perm, yls, sem):
+            out[ds((6 + i) * CX, CX), :] = rows[2 * k + 1, ds(c * CX, CX), 0, :]
+        out[ds(10 * CX, CX), :] = mats[k, :, 0, :].astype(F32)
+
+
+def inner_body(
+    f, mat, perm_hbm, scaled, right, gx_out, lsp, rsp, gy_out, ly, ry, perm_rows, perm, yls, sem
+):
     copy = pltpu.make_async_copy(perm_hbm, perm, sem.at[0])
     copy.start()
     copy.wait()
+    for k in range(16):
+        perm_rows[ds(k, 1), :] = jnp.full((1, NZ), perm[k], F32)
 
     def main(c, x):
         return f[ds((c * CX + x) * CY, CY), :]
@@ -172,7 +184,7 @@
 
 
 def first_body(
-    f, scaled, right, gxs, lsp, rsp, xlo, xhi, ylo, yhi,
+    f, scaled, right, gxs, lsp, rsp, xlo, xhi, ylo, yhi, perm_rows,
     sol, lsp_h, rsp_h, send, ht, hu, hd, he, gs,
 ):
     gx, gy = lax.axis_index("gx"), lax.axis_index("gy")
@@ -190,8 +202,9 @@
         hu[ds(i * 128 + 1, CX, 8), :] = yhi[ds((6 + i) * CX, CX), :] * myh
         hd[ds(i * 128, CX, 8), :] = ylo[ds((6 + i) * CX, CX), :] * myl
         hd[ds(i * 128 + 1, CX, 8), :] = f[ds(c * CX * CY + CY - 1, CX, CY), :]
-    he[ds(0, CX, 8), :] = jnp.where(myl > 0, ylo[ds(10 * CX, CX), :], 1.0)
-    he[ds(1, CX, 8), :] = jnp.where(myh > 0, yhi[ds(10 * CX, CX), :], 1.0)
+    perm = [perm_rows[ds(k, 1), :] for k in range(16)]
+    he[ds(0, CX, 8), :] = jnp.where(myl > 0, lookup(ylo[ds(10 * CX, CX), :], perm), 1.0)
+    he[ds(1, CX, 8), :] = jnp.where(myh > 0, lookup(yhi[ds(10 * CX, CX), :], perm), 1.0)
     row8 = row_of((8, NZ))
     inside = jnp.where(row8 == 0, myl, jnp.where(row8 == 1, myh, 0.0))
     zero8, one8 = jnp.zeros((8, NZ), F32), jnp.ones((8, NZ), F32)
@@ -413,7 +426,7 @@
     earlier = (owner == owner_col) & (rows < lanes)
     rank = jnp.sum(jnp.where(earlier, 1, 0), axis=0, keepdims=True)
     ranks[...] = jnp.broadcast_to(rank, (8, PATCH))
-    hot[...] = jnp.where(row_of((NZ, PATCH)) == owner[:NZ], 1.0, 0.0)
+    hot[...] = jnp.where(row_of((NZ, PATCH)) == owner[:NZ], 1.0, 0.0).astype(BF16)
     cell = jnp.broadcast_to(cell_row[...], (8, PATCH))
     line = cell >> 7
     x = (line * 2731) >> 16
@@ -425,20 +438,22 @@
     for k in range(SLOTS):
         spread[ds(k * WIDTH + 8, 8), :] = jnp.where(ranks[...] == k, place, 0.0)
     sector = gx * NBY + gy
-    angle = lane_of((8, NZ)).astype(F32)
+    angle = row_of((NZ, NZ)).astype(F32)
     sin_theta, cos_theta = sine_cosine(math.pi * (angle + 0.5) / NZ)
     turn = jnp.full((8, NZ), sector, jnp.int32).astype(F32) * (2.0 * math.pi / (NB * NBY))
     sin_phi, cos_phi = sine_cosine(turn)
-    table[ds(0, 8), :] = KAPPA * sin_theta * cos_phi
-    table[ds(8, 8), :] = KAPPA * sin_theta * sin_phi
-    table[ds(16, 8), :] = KAPPA * cos_theta
+    table[ds(0, NZ), :] = KAPPA * sin_theta * cos_phi[0:1]
+    table[ds(NZ, NZ), :] = KAPPA * sin_theta * sin_phi[0:1]
+    table[ds(2 * NZ, NZ), :] = KAPPA * cos_theta
 
 
 def finish_body(
-    rec0, rec1, rec2, rec3, soly, ly, ry, cell, hot, static, ranks, new, send,
-    value_of, inc, out, table, spread, sem,
+    rec0, rec1, rec2, rec3, soly, ly, ry, cell_hbm, hot, static, ranks, new, send,
+    value_of, inc, out, table, spread, cell, sem,
 ):
     gy = lax.axis_index("gy")
+    cells = pltpu.make_async_copy(cell_hbm, cell, sem.at[24])
+    cells.start()
 
     def get(rec, k):
         return rec[ds(k * CX, CX), :]
@@ -495,6 +510,7 @@
                 copy.start()
                 copies.append(copy)
 
+    cells.wait()
     lane = lane_of((8, NZ))
     halves = []
     for half in range(PATCH // NZ):
@@ -511,10 +527,14 @@
     spread[...] = static[...]
     for k in range(SLOTS):
         spread[ds(k * WIDTH, 8), :] = jnp.where(ranks[...] == k, samples, 0.0)
-    send[...] = lax.dot_general(
-        hot[...], spread[...], (((1,), (1,)), ((), ())),
-        precision=lax.Precision.HIGHEST, preferred_element_type=F32,
-    )
+    rest, total = spread[...], jnp.zeros((NZ, NZ), F32)
+    for _ in range(3):
+        part = rest.astype(BF16)
+        rest = rest - part.astype(F32)
+        total += lax.dot_general(
+            hot[...], part, (((1,), (1,)), ((), ())), preferred_element_type=F32
+        )
+    send[...] = total
     for copy in copies:
         copy.wait()
 
@@ -535,17 +555,26 @@
 
 
 def sector_body(recv, table, far):
-    values = recv[...]
-    flipped = jnp.transpose(values)
-    along_x, along_y, along_z = (table[ds(8 * i, 1), :] for i in range(3))
+    flipped = jnp.transpose(recv[...])
+    along = [table[ds(i * NZ, NZ), :] for i in range(3)]
+    parts, cosines, sines = [], [], []
+    for k in range(SLOTS):
+        parts.append(flipped[k * WIDTH : k * WIDTH + 8])
+        px, py, pz = (flipped[k * WIDTH + 8 + i : k * WIDTH + 9 + i] for i in range(3))
+        sine, cosine = sine_cosine((px * along[0] + py * along[1]) + pz * along[2])
+        cosines.append(cosine)
+        sines.append(sine)
+    value = jnp.concatenate(parts, axis=1)
+    wave = jnp.concatenate(
+        [jnp.concatenate(cosines, axis=1), jnp.concatenate(sines, axis=1)], axis=0
+    )
+    value_high = value.astype(BF16)
+    value_low = (value - value_high.astype(F32)).astype(BF16)
+    wave_high = wave.astype(BF16)
+    wave_low = (wave - wave_high.astype(F32)).astype(BF16)
     sums = jnp.zeros((8, 2 * NZ), F32)
-    for k in range(SLOTS):
-        px, py, pz = (values[:, k * WIDTH + 8 + i : k * WIDTH + 9 + i] for i in range(3))
-        sine, cosine = sine_cosine((px * along_x + py * along_y) + pz * along_z)
-        sums += jnp.dot(
-            flipped[k * WIDTH : k * WIDTH + 8], jnp.concatenate([cosine, sine], axis=1),
-            precision=lax.Precision.HIGHEST, preferred_element_type=F32,
-        )
+    for a, b in ((value_high, wave_high), (value_low, wave_high), (value_high, wave_low)):
+        sums += lax.dot_general(a, b, (((1,), (1,)), ((), ())), preferred_element_type=F32)
     scale = 1.0 / math.sqrt(PATCH)
     far[0:6, :] = sums[0:6, :NZ] * scale
     far[6:12, :] = sums[0:6, NZ:] * scale
@@ -564,18 +593,19 @@
     table16 = pltpu.SMEM((16,), F32)
     xh, xl, yh, yl = call(
         edges_body,
-        [plane, plane, edge, edge],
-        [f, mat, permittivity],
-        [pltpu.VMEM(block, F32), pltpu.VMEM(cells, jnp.int32), table16],
-        hbm=(0, 1, 2),
-        sems=3,
+        [(184, NZ), (184, NZ), edge, edge],
+        [fields.reshape(6 * CX, CY, NZ), material],
+        [(4, 6 * CX, 1, NZ), pltpu.VMEM((2, CX, 1, NZ), jnp.int32)],
+        hbm=(0, 1),
+        sems=6 + 2 * len(XC),
         vmem=VM,
+        pinned=True,
     )
     xlo, xhi = shift(xh, "gx", 1), shift(xl, "gx", -1)
     ylo, yhi = shift(yh, "gy", 1), shift(yl, "gy", -1)
-    scaled, right, gxs, lsp, rsp, gys, ly, ry = call(
+    scaled, right, gxs, lsp, rsp, gys, ly, ry, perm_rows = call(
         inner_body,
-        [cells, block] + [cells] * 6,
+        [cells, block] + [cells] * 6 + [(16, NZ)],
         [f, mat, permittivity],
         [table16, cells],
         hbm=(2,),
@@ -585,7 +615,7 @@
     sol, lsp_h, rsp_h, send = call(
         first_body,
         [(6 * CX * ROWS, NZ), halo, halo, (ROWS * 16, NZ)],
-        [f, scaled, right, gxs, lsp, rsp, xlo, xhi, ylo, yhi],
+        [f, scaled, right, gxs, lsp, rsp, xlo, xhi, ylo, yhi, perm_rows],
         [(6 * 128, NZ), (4 * 128, NZ), (4 * 128, NZ), halo, halo],
     )
     rec = lax.all_to_all(send.reshape(NB, 16, NZ), "gx", 0, 0, tiled=True)
@@ -600,7 +630,10 @@
     others = [shift(rec, "gy", k) for k in (1, 2, 3)]
     hot, static, ranks, table = call(
         patches_body,
-        [(NZ, PATCH), (NZ, PATCH), jax.ShapeDtypeStruct((8, PATCH), jnp.int32), (24, NZ)],
+        [
+            jax.ShapeDtypeStruct((NZ, PATCH), BF16), (NZ, PATCH),
+            jax.ShapeDtypeStruct((8, PATCH), jnp.int32), (3 * NZ, NZ),
+        ],
         [patch_cell.reshape(1, PATCH), patch_owner.reshape(1, PATCH)],
         cost=COST,
     )
@@ -608,10 +641,11 @@
         finish_body,
         [block, (NB * NBY, NZ)],
         [rec, *others, soly, ly, ry, patch_cell, hot, static, ranks],
-        [block, (6 * CX, NZ), (6 * CX, NZ), (CX * CY * 8, NZ), (NZ, PATCH)],
-        smem=(7,),
+        [block, (6 * CX, NZ), (6 * CX, NZ), (CX * CY * 8, NZ), (NZ, PATCH)]
+        + [pltpu.SMEM((PATCH,), jnp.int32)],
+        hbm=(7,),
         hbm_outs=(0,),
-        sems=24,
+        sems=25,
     )
     recv = lax.all_to_all(send, ("gx", "gy"), 0, 0, tiled=True)
     (far,) = call(sector_body, [(12, NZ)], [recv, table])

time: 75.4 us -> 72.1 us (0.956)
  Pallas kernels: 10.4 us -> 9.09 us
  local copies, waits for them, and re-layouts: 1.28 us -> 0.02 us
    pallas_call x8, Pallas kernels: 10.4 us -> 9.09 us  [call(): pl.pallas_call(body, out_shape=shapes, in_specs=[place(i, hbm) for i in r...]
    unnamed x10, local copies, waits for them, and re-layouts: 1.28 us -> 0.02 us
    all_to_all x1, blocking collectives: 15.9 us -> 15 us  [local(): recv = lax.all_to_all(send, ('gx', 'gy'), 0, 0, tiled=True)]
  transfers between devices with their start and end apart: 7 -> 7, of which waited for: 4 -> 3; matrix products, arithmetic and copies ran while one was open for 0% -> 0% of each run, Pallas kernels for 2% -> 2%
where the time goes in v2:
time: 72.1 us; the launch traced here: 71.8 us
  blocking collectives  46.3 us (64%)
  starting transfers between devices  10 us (14%)
  Pallas kernels  9.09 us (13%)
  waiting for transfers between devices  5.71 us (8%)
    all_to_all x1, blocking collectives, local(): rec = lax.all_to_all(send.reshape(NB, 16, NZ), 'gx', 0, 0, tiled=True)  18.8 us
    all_to_all x1, blocking collectives, local(): recv = lax.all_to_all(send, ('gx', 'gy'), 0, 0, tiled=True)  15 us
    all_to_all x1, blocking collectives, local(): back = lax.all_to_all(back.reshape(NB, 16, NZ), 'gx', 0, 0, tiled=True)  12.5 us
    ppermute x7, starting transfers between devices, shift(): lax.ppermute(value, axis, [(i, (i + by) % count) for i in range(count)])  10 us
    pallas_call x8, Pallas kernels, call(): pl.pallas_call(body, out_shape=shapes, in_specs=[place(i, hbm) for i in r...  9.09 us
    ppermute x7, waiting for transfers between devices, shift(): lax.ppermute(value, axis, [(i, (i + by) % count) for i in range(count)])  5.71 us
  transfers between devices with their start and end apart: 7, of which 3 were waited for; matrix products, arithmetic and copies ran while one was open for 0% of the time, Pallas kernels for 2%

profile of v2, /device:TPU:1, one launch (start us, length us, event | category | flops | bytes accessed | tf_op | source)
XLA Modules:
  0.0 71.8 jit_solution(4236548162885934965)
XLA Ops:
  0.7 1.2 %shard_map.69 = (f32[184,128]{1,0:T(8,128)S(1)}, f32[184,128]{1,0:T(8,128)S(1)}, f32[176,128]{1,0:T(8,128)S(1)}, f32[176,128]{1,0:T(8,128)S(1)}) custom-call(f32[96,24,128]{2,1,0:T(8,128)} %bitcast.14, s32[16,24,128]{2,1,0:T(8,128)} %mat.1), custom_call_target="tpu_custom_call" | custom-call | tf_op jit(solution)/shard_map/pallas_call | solution.py:47
  1.9 2.8 %collective-permute-start = (f32[184,128]{1,0:T(8,128)S(1)}, f32[184,128]{1,0:T(8,128)S(1)}, u32[]{:S(2)}, u32[]{:S(2)}) collective-permute-start(f32[184,128]{1,0:T(8,128)S(1)} %get-tuple-element.32), channel_id=1, source_target_pairs={{0,4},{4,8},{8,12},{12,16},{16,20},{20,24},{24,28},{28,32},{32,36}... | collective-permute-start | bytes 282632 | tf_op jit(solution)/shard_map/ppermute | solution.py:585
  4.6 0.0 collective-permute-start.1
  4.6 1.2 %collective-permute-start.2 = (f32[176,128]{1,0:T(8,128)S(1)}, f32[176,128]{1,0:T(8,128)S(1)}, u32[]{:S(2)}, u32[]{:S(2)}) collective-permute-start(f32[176,128]{1,0:T(8,128)S(1)} %get-tuple-element.34), channel_id=1, source_target_pairs={{0,1},{1,2},{2,3},{3,0},{4,5},{5,6},{6,7},{7,4},{8,9},{9,10},{10,1... | collective-permute-start | bytes 270344 | tf_op jit(solution)/shard_map/ppermute | solution.py:585
  5.9 1.5 %collective-permute-start.3 = (f32[176,128]{1,0:T(8,128)S(1)}, f32[176,128]{1,0:T(8,128)S(1)}, u32[]{:S(2)}, u32[]{:S(2)}) collective-permute-start(f32[176,128]{1,0:T(8,128)S(1)} %get-tuple-element.35), channel_id=1, source_target_pairs={{0,3},{1,0},{2,1},{3,2},{4,7},{5,4},{6,5},{7,6},{8,11},{9,8},{10,9... | collective-permute-start | bytes 270344 | tf_op jit(solution)/shard_map/ppermute | solution.py:585
  7.3 1.5 %shard_map.68 = (f32[384,128]{1,0:T(8,128)S(1)}, f32[2304,128]{1,0:T(8,128)S(1)}, f32[384,128]{1,0:T(8,128)S(1)}, f32[384,128]{1,0:T(8,128)S(1)}, f32[384,128]{1...) custom-call(f32[2304,128]{1,0:T(8,128)S(1)} %bitcast.15, ...), custom_call_target="tpu_custom_call" | custom-call | flops 4000000 | bytes 4000000 | tf_op jit(solution)/shard_map/pallas_call | solution.py:47
  8.8 0.4 collective-permute-done.2.ylo
  9.2 0.0 collective-permute-done.xlo
  9.2 0.0 collective-permute-done.1.xhi
  9.2 0.7 shard_map.70
  9.9 18.8 %all_to_all.21 = f32[32,16,128]{2,1,0:T(8,128)S(1)} all-to-all(f32[32,16,128]{2,1,0:T(8,128)S(1)} %bitcast.21), channel_id=1, replica_groups=mesh['gx'=32,'gy'=4] {'gx'}, dimensions={0} | all-to-all | bytes 524288 | tf_op jit(solution)/shard_map/all_to_all | solution.py:621
  28.7 0.5 shard_map.71
  29.2 12.5 %all_to_all.22 = f32[32,16,128]{2,1,0:T(8,128)S(1)} all-to-all(f32[32,16,128]{2,1,0:T(8,128)S(1)} %bitcast.19), channel_id=1, replica_groups=mesh['gx'=32,'gy'=4] {'gx'}, dimensions={0} | all-to-all | bytes 524288 | tf_op jit(solution)/shard_map/all_to_all | solution.py:623
  41.6 1.4 %shard_map.72 = (f32[2304,128]{1,0:T(8,128)S(1)}, f32[256,128]{1,0:T(8,128)S(1)}) custom-call(f32[512,128]{1,0:T(8,128)S(1)} %bitcast.17, f32[3072,128]{1,0:T(8,128)S(1)} %get-tuple-element.38.sol, f32[384,128]{1,0:T(8,128)S(1)} %get-tuple-element.30.lsp, f32[384,128]{1,0:T(8,128)S(1)} %get-tuple-element.31.rsp, f32[128,128]{1,0:T(8,128)S(1)} %get-tuple-element.39.lsp_h, ...), custom_call_target="tpu_custom_call" | custom-call | tf_op jit(solution)/shard_map/pallas_call | solution.py:47
  43.1 1.3 %collective-permute-start.4 = (f32[256,128]{1,0:T(8,128)S(1)}, f32[256,128]{1,0:T(8,128)S(1)}, u32[]{:S(2)}, u32[]{:S(2)}) collective-permute-start(f32[256,128]{1,0:T(8,128)S(1)} %get-tuple-element.44.rec0), channel_id=1, source_target_pairs={{0,1},{1,2},{2,3},{3,0},{4,5},{5,6},{6,7},{7,4},{8,9},{9,10},{10,1... | collective-permute-start | bytes 393224 | tf_op jit(solution)/shard_map/ppermute | solution.py:585
  44.4 2.6 %collective-permute-start.5 = (f32[256,128]{1,0:T(8,128)S(1)}, f32[256,128]{1,0:T(8,128)S(1)}, u32[]{:S(2)}, u32[]{:S(2)}) collective-permute-start(f32[256,128]{1,0:T(8,128)S(1)} %get-tuple-element.44.rec0), channel_id=1, source_target_pairs={{0,2},{1,3},{2,0},{3,1},{4,6},{5,7},{6,4},{7,5},{8,10},{9,11},{10,... | collective-permute-start | bytes 393224 | tf_op jit(solution)/shard_map/ppermute | solution.py:585
  47.0 0.7 collective-permute-start.6
  47.7 0.3 shard_map.73
  47.9 1.3 %collective-permute-done.4.rec1 = f32[256,128]{1,0:T(8,128)S(1)} collective-permute-done((f32[256,128]{1,0:T(8,128)S(1)}, f32[256,128]{1,0:T(8,128)S(1)}, u32[]{:S(2)}, u32[]{:S(2)}) %collective-permute-start.4) | collective-permute-done | bytes 131104 | tf_op jit(solution)/shard_map/ppermute | solution.py:585
  49.2 4.0 %collective-permute-done.5.rec2 = f32[256,128]{1,0:T(8,128)S(1)} collective-permute-done((f32[256,128]{1,0:T(8,128)S(1)}, f32[256,128]{1,0:T(8,128)S(1)}, u32[]{:S(2)}, u32[]{:S(2)}) %collective-permute-start.5) | collective-permute-done | bytes 131104 | tf_op jit(solution)/shard_map/ppermute | solution.py:585
  53.2 0.0 collective-permute-done.6.rec3
  53.2 2.2 %shard_map.74 = (f32[2304,128]{1,0:T(8,128)}, f32[128,128]{1,0:T(8,128)S(1)}) custom-call(f32[256,128]{1,0:T(8,128)S(1)} %get-tuple-element.44.rec0, f32[256,128]{1,0:T(8,128)S(1)} %collective-permute-done.4.rec1, f32[256,128]{1,0:T(8,128)S(1)} %collective-permute-done.5.rec2, f32[256,128]{1,0:T(8,128)S(1)} %collective-permute-done.6.rec3, ...), custom_call_target="tpu_custom_call" | custom-call | tf_op jit(solution)/shard_map/pallas_call | solution.py:47
  55.4 15.0 %all_to_all.23 = f32[128,1,128]{2,1,0:T(1,128)S(1)} all-to-all(f32[128,1,128]{2,1,0:T(1,128)S(1)} %bitcast.23), channel_id=1, replica_groups=mesh['gx'=32,'gy'=4] {'gx','gy'}, dimensions={0} | all-to-all | bytes 131072 | tf_op jit(solution)/shard_map/all_to_all | solution.py:650
  70.5 1.4 %shard_map.75 = f32[12,128]{1,0:T(8,128)} custom-call(f32[128,128]{1,0:T(8,128)S(1)} %bitcast.22, f32[384,128]{1,0:T(8,128)S(1)} %get-tuple-element.51.table), custom_call_target="tpu_custom_call" | custom-call | tf_op jit(solution)/shard_map/pallas_call | solution.py:47
  (11 shorter events, 0.0 us)
Async XLA Ops:
  0.6 6.7 %copy-start.1 = (s32[16,24,128]{2,1,0:T(8,128)S(1)}, s32[16,24,128]{2,1,0:T(8,128)}, u32[]{:S(2)}) copy-start(s32[16,24,128]{2,1,0:T(8,128)} %mat.1) | copy-start | bytes 589828
  0.6 6.7 %copy-start = (f32[6,16,24,128]{3,2,1,0:T(8,128)S(1)}, f32[6,16,24,128]{3,2,1,0:T(8,128)}, u32[]{:S(2)}) copy-start(f32[6,16,24,128]{3,2,1,0:T(8,128)} %param.5) | copy-start | bytes 3538948
  0.6 6.7 %copy-start.3 = (f32[16]{0:T(128)S(1)}, f32[16]{0:T(128)}, u32[]{:S(2)}) copy-start(f32[16]{0:T(128)} %perm_hbm.1) | copy-start | bytes 196
  1.9 7.4 %collective-permute-start = (f32[184,128]{1,0:T(8,128)S(1)}, f32[184,128]{1,0:T(8,128)S(1)}, u32[]{:S(2)}, u32[]{:S(2)}) collective-permute-start(f32[184,128]{1,0:T(8,128)S(1)} %get-tuple-element.32), channel_id=1, source_target_pairs={{0,4},{4,8},{8,12},{12,16},{16,20},{20,24},{24,28},{28,32},{32,36}... | collective-permute-start | bytes 282632 | tf_op jit(solution)/shard_map/ppermute | solution.py:585
  4.6 4.6 %collective-permute-start.1 = (f32[184,128]{1,0:T(8,128)S(1)}, f32[184,128]{1,0:T(8,128)S(1)}, u32[]{:S(2)}, u32[]{:S(2)}) collective-permute-start(f32[184,128]{1,0:T(8,128)S(1)} %get-tuple-element.33), channel_id=1, source_target_pairs={{0,124},{4,0},{8,4},{12,8},{16,12},{20,16},{24,20},{28,24},{32,28}... | collective-permute-start | bytes 282632 | tf_op jit(solution)/shard_map/ppermute | solution.py:585
  4.6 4.6 %collective-permute-start.2 = (f32[176,128]{1,0:T(8,128)S(1)}, f32[176,128]{1,0:T(8,128)S(1)}, u32[]{:S(2)}, u32[]{:S(2)}) collective-permute-start(f32[176,128]{1,0:T(8,128)S(1)} %get-tuple-element.34), channel_id=1, source_target_pairs={{0,1},{1,2},{2,3},{3,0},{4,5},{5,6},{6,7},{7,4},{8,9},{9,10},{10,1... | collective-permute-start | bytes 270344 | tf_op jit(solution)/shard_map/ppermute | solution.py:585
  5.9 3.4 %collective-permute-start.3 = (f32[176,128]{1,0:T(8,128)S(1)}, f32[176,128]{1,0:T(8,128)S(1)}, u32[]{:S(2)}, u32[]{:S(2)}) collective-permute-start(f32[176,128]{1,0:T(8,128)S(1)} %get-tuple-element.35), channel_id=1, source_target_pairs={{0,3},{1,0},{2,1},{3,2},{4,7},{5,4},{6,5},{7,6},{8,11},{9,8},{10,9... | collective-permute-start | bytes 270344 | tf_op jit(solution)/shard_map/ppermute | solution.py:585
  41.6 6.1 %copy-start.2 = (s32[256]{0:T(256)S(1)}, s32[256]{0:T(256)}, u32[]{:S(2)}) copy-start(s32[256]{0:T(256)} %cell_hbm.1) | copy-start | bytes 3076
  41.6 6.1 %copy-start.4 = (s32[256,1]{0,1:T(1,128)S(1)}, s32[256,1]{0,1:T(1,128)}, u32[]{:S(2)}) copy-start(s32[256,1]{0,1:T(1,128)} %param.9) | copy-start | bytes 3076
  43.1 6.2 %collective-permute-start.4 = (f32[256,128]{1,0:T(8,128)S(1)}, f32[256,128]{1,0:T(8,128)S(1)}, u32[]{:S(2)}, u32[]{:S(2)}) collective-permute-start(f32[256,128]{1,0:T(8,128)S(1)} %get-tuple-element.44.rec0), channel_id=1, source_target_pairs={{0,1},{1,2},{2,3},{3,0},{4,5},{5,6},{6,7},{7,4},{8,9},{9,10},{10,1... | collective-permute-start | bytes 393224 | tf_op jit(solution)/shard_map/ppermute | solution.py:585
  44.4 8.9 %collective-permute-start.5 = (f32[256,128]{1,0:T(8,128)S(1)}, f32[256,128]{1,0:T(8,128)S(1)}, u32[]{:S(2)}, u32[]{:S(2)}) collective-permute-start(f32[256,128]{1,0:T(8,128)S(1)} %get-tuple-element.44.rec0), channel_id=1, source_target_pairs={{0,2},{1,3},{2,0},{3,1},{4,6},{5,7},{6,4},{7,5},{8,10},{9,11},{10,... | collective-permute-start | bytes 393224 | tf_op jit(solution)/shard_map/ppermute | solution.py:585
  47.0 6.2 %collective-permute-start.6 = (f32[256,128]{1,0:T(8,128)S(1)}, f32[256,128]{1,0:T(8,128)S(1)}, u32[]{:S(2)}, u32[]{:S(2)}) collective-permute-start(f32[256,128]{1,0:T(8,128)S(1)} %get-tuple-element.44.rec0), channel_id=1, source_target_pairs={{0,3},{1,0},{2,1},{3,2},{4,7},{5,4},{6,5},{7,6},{8,11},{9,8},{10,9... | collective-permute-start | bytes 393224 | tf_op jit(solution)/shard_map/ppermute | solution.py:585

commit v3 on v2

--- a/solution.py
+++ b/solution.py
@@ -22,6 +22,7 @@
 EDGES = (CY - 1, CY - 2, 0, 1)
 PICKS = 32
 COST = 4_000_000
+OUTS = 1
 VM = 56
 
 
@@ -29,15 +30,14 @@
     return pl.ds(start, size) if stride is None else pl.ds(start, size, stride=stride)
 
 
-def call(body, outs, args, scratch=(), smem=(), hbm=(), hbm_outs=(), sems=0, cost=0, vmem=40, pinned=False):
+def call(body, outs, args, scratch=(), smem=(), hbm=(), hbm_outs=(), sems=0, cost=0, vmem=40, pinned=()):
     def place(i, slow):
         if i in slow:
             return pl.BlockSpec(memory_space=pltpu.HBM)
         return pl.BlockSpec(memory_space=pltpu.SMEM if slow is hbm and i in smem else pltpu.VMEM)
 
     shapes = [o if isinstance(o, jax.ShapeDtypeStruct) else jax.ShapeDtypeStruct(o, F32) for o in outs]
-    if pinned:
-        shapes = [pltpu.VMEM(o.shape, o.dtype) for o in shapes]
+    shapes = [pltpu.VMEM(o.shape, o.dtype) if i in pinned else o for i, o in enumerate(shapes)]
     space = [o if not isinstance(o, tuple) else pltpu.VMEM(o, F32) for o in scratch]
     if sems:
         space.append(pltpu.SemaphoreType.DMA((sems,)))
@@ -411,14 +411,18 @@
         rec[ds(c * CX, CX), :] = us[c]
     rec[ds(6 * CX, CX), :] = ly[ds(0, CX, CY), :]
     rec[ds(7 * CX, CX), :] = ry[ds(0, CX, CY), :]
-    rec[ds(14 * CX, CX), :] = ry[ds(0, CX, CY), :]
-    rec[ds(15 * CX, CX), :] = ry[ds(CY - 1, CX, CY), :]
+    rec[ds(14 * CX, CX), :] = ry[ds(CY - 1, CX, CY), :]
 
 
 WIDTH = NZ // SLOTS
 
 
-def patches_body(cell_row, owner_row, hot, spread, ranks, table):
+def patches_body(
+    cell_row, owner_row, cell_hbm, soly, ly, ry,
+    hot, spread, ranks, table, base, z_hot, x_left, x_right, lines, cell, sem,
+):
+    copy = pltpu.make_async_copy(cell_hbm, cell, sem.at[0])
+    copy.start()
     gx, gy = lax.axis_index("gx"), lax.axis_index("gy")
     owner = jnp.broadcast_to(owner_row[...], (PATCH, PATCH))
     rows, lanes = row_of((PATCH, PATCH)), lane_of((PATCH, PATCH))
@@ -427,10 +431,10 @@
     rank = jnp.sum(jnp.where(earlier, 1, 0), axis=0, keepdims=True)
     ranks[...] = jnp.broadcast_to(rank, (8, PATCH))
     hot[...] = jnp.where(row_of((NZ, PATCH)) == owner[:NZ], 1.0, 0.0).astype(BF16)
-    cell = jnp.broadcast_to(cell_row[...], (8, PATCH))
-    line = cell >> 7
+    place = jnp.broadcast_to(cell_row[...], (8, PATCH))
+    line, pz = place >> 7, place & 127
     x = (line * 2731) >> 16
-    px, py, pz = gx * CX + x, gy * CY + line - x * CY, cell & 127
+    px, py = gx * CX + x, gy * CY + line - x * CY
     row8 = row_of((8, PATCH))
     place = jnp.where(row8 == 0, px, jnp.where(row8 == 1, py, jnp.where(row8 == 2, pz, 0)))
     place = place.astype(F32)
@@ -445,15 +449,45 @@
     table[ds(0, NZ), :] = KAPPA * sin_theta * cos_phi[0:1]
     table[ds(NZ, NZ), :] = KAPPA * sin_theta * sin_phi[0:1]
     table[ds(2 * NZ, NZ), :] = KAPPA * cos_theta
+    for x_own in range(CX):
+        at = ds(x_own * CY, CY)
+        for c in range(6):
+            lines[ds(x_own * (CY * 8) + c, CY, 8), :] = soly[ds((c * CX + x_own) * CY, CY), :]
+        lines[ds(x_own * (CY * 8) + 6, CY, 8), :] = ly[at, :]
+        lines[ds(x_own * (CY * 8) + 7, CY, 8), :] = ry[at, :]
+    copy.wait()
+    lane = lane_of((8, NZ))
+    halves = []
+    for half in range(PATCH // NZ):
+
+        def pick(j, acc):
+            at = cell[half * NZ + j]
+            values = lines[ds(pl.multiple_of((at >> 7) * 8, 8), 8), :]
+            moved = pltpu.roll(values, (j - (at & 127)) & 127, 1)
+            return jnp.where(lane == j, moved, acc)
+
+        halves.append(lax.fori_loop(0, NZ, pick, jnp.zeros((8, NZ), F32), unroll=PICKS))
+    samples = jnp.concatenate(halves, axis=1)
+    base[...] = jnp.where(row8 < 6, samples, 0.0)
+    z_hot[...] = jnp.where(row_of((NZ, PATCH)) == pz[0:1], 1.0, 0.0).astype(BF16)
+    here = row_of((CX, PATCH)) == x[0:1]
+    x_left[...] = jnp.where(here, samples[6:7], 0.0)
+    x_right[...] = jnp.where(here, samples[7:8], 0.0)
+
+
+def in_parts(value):
+    parts = []
+    for _ in range(3):
+        parts.append(value.astype(BF16))
+        value = value - parts[-1].astype(F32)
+    return parts
 
 
 def finish_body(
-    rec0, rec1, rec2, rec3, soly, ly, ry, cell_hbm, hot, static, ranks, new, send,
-    value_of, inc, out, table, spread, cell, sem,
+    rec0, rec1, rec2, rec3, base, z_hot, x_left, x_right, hot, static, ranks, soly, ly, ry,
+    new, send, inc, out, spread,
 ):
     gy = lax.axis_index("gy")
-    cells = pltpu.make_async_copy(cell_hbm, cell, sem.at[24])
-    cells.start()
 
     def get(rec, k):
         return rec[ds(k * CX, CX), :]
@@ -462,7 +496,7 @@
 
     def sweep(order, up):
         m, n = [zero] * 6, zero
-        near, far, own, other = (8, 0, 15, 6) if up else (0, 8, 6, 15)
+        near, far, own, other = (8, 0, 14, 6) if up else (0, 8, 6, 14)
         for rec, valid in order:
             cross = get(rec, 7)
             gain = 1.0 / (1.0 - get(rec, other) * n)
@@ -477,7 +511,7 @@
 
     below, below_gain = sweep([(rec3, gy >= 3), (rec2, gy >= 2), (rec1, gy >= 1)], True)
     above, above_gain = sweep([(rec1, gy <= 0), (rec2, gy <= 1), (rec3, gy <= 2)], False)
-    a, cross, d = get(rec0, 6), get(rec0, 7), get(rec0, 15)
+    a, cross, d = get(rec0, 6), get(rec0, 7), get(rec0, 14)
     ll, lt = 1.0 - a * below_gain, -cross * above_gain
     tl, tt = -cross * below_gain, 1.0 - d * above_gain
     over = 1.0 / (ll * tt - lt * tl)
@@ -488,55 +522,33 @@
         inc[ds(c * CX, CX), :] = below[c] + below_gain * lead
         out[ds(c * CX, CX), :] = above[c] + above_gain * tail
 
-    copies = []
+    reach = jnp.zeros((12 * CX, PATCH), F32)
+    for part in in_parts(jnp.concatenate([inc[...], out[...]], axis=0)):
+        reach += jnp.dot(part, z_hot[...], preferred_element_type=F32)
+    added = []
+    for c in range(6):
+        low, high = reach[c * CX : (c + 1) * CX], reach[(6 + c) * CX : (7 + c) * CX]
+        weighed = low * x_left[...] + high * x_right[...]
+        added.append(jnp.sum(weighed, axis=0, keepdims=True))
+    samples = base[...] + jnp.concatenate(added + [jnp.zeros((2, PATCH), F32)], axis=0)
+    spread[...] = static[...]
+    for k in range(SLOTS):
+        spread[ds(k * WIDTH, 8), :] = jnp.where(ranks[...] == k, samples, 0.0)
+    total = jnp.zeros((NZ, NZ), F32)
+    for part in in_parts(spread[...]):
+        total += lax.dot_general(
+            hot[...], part, (((1,), (1,)), ((), ())), preferred_element_type=F32
+        )
+    send[...] = total
     for x in range(CX):
-        at = ds(x * CY, CY)
-        left, right = ly[at, :], ry[at, :]
+        left, right = ly[ds(x * CY, CY), :], ry[ds(x * CY, CY), :]
         for c in range(6):
             here = ds((c * CX + x) * CY, CY)
-            value = (
+            new[here, :] = (
                 soly[here, :]
                 + left * inc[ds(c * CX + x, 1), :]
                 + right * out[ds(c * CX + x, 1), :]
             )
-            value_of[here, :] = value
-            table[ds(x * (CY * 8) + c, CY, 8), :] = value
-        if x % 4 == 3:
-            for c in range(6):
-                part = ds((c * CX + x - 3) * CY, 4 * CY)
-                copy = pltpu.make_async_copy(
-                    value_of.at[part, :], new.at[part, :], sem.at[len(copies)]
-                )
-                copy.start()
-                copies.append(copy)
-
-    cells.wait()
-    lane = lane_of((8, NZ))
-    halves = []
-    for half in range(PATCH // NZ):
-
-        def pick(j, acc):
-            at = cell[half * NZ + j]
-            values = table[ds(pl.multiple_of((at >> 7) * 8, 8), 8), :]
-            moved = pltpu.roll(values, (j - (at & 127)) & 127, 1)
-            return jnp.where(lane == j, moved, acc)
-
-        halves.append(lax.fori_loop(0, NZ, pick, jnp.zeros((8, NZ), F32), unroll=PICKS))
-    samples = jnp.concatenate(halves, axis=1)
-    samples = jnp.where(row_of((8, PATCH)) < 6, samples, 0.0)
-    spread[...] = static[...]
-    for k in range(SLOTS):
-        spread[ds(k * WIDTH, 8), :] = jnp.where(ranks[...] == k, samples, 0.0)
-    rest, total = spread[...], jnp.zeros((NZ, NZ), F32)
-    for _ in range(3):
-        part = rest.astype(BF16)
-        rest = rest - part.astype(F32)
-        total += lax.dot_general(
-            hot[...], part, (((1,), (1,)), ((), ())), preferred_element_type=F32
-        )
-    send[...] = total
-    for copy in copies:
-        copy.wait()
 
 
 def sine_cosine(v):
@@ -554,7 +566,12 @@
     return sine, cosine
 
 
-def sector_body(recv, table, far):
+def sector_body(recv, table, made, far, new, sem):
+    copies = []
+    for k in range(OUTS):
+        part = ds(k * (6 * CX * CY // OUTS), 6 * CX * CY // OUTS)
+        copies.append(pltpu.make_async_copy(made.at[part, :], new.at[part, :], sem.at[k]))
+        copies[-1].start()
     flipped = jnp.transpose(recv[...])
     along = [table[ds(i * NZ, NZ), :] for i in range(3)]
     parts, cosines, sines = [], [], []
@@ -578,6 +595,8 @@
     scale = 1.0 / math.sqrt(PATCH)
     far[0:6, :] = sums[0:6, :NZ] * scale
     far[6:12, :] = sums[0:6, NZ:] * scale
+    for copy in copies:
+        copy.wait()
 
 
 def shift(value, axis, by):
@@ -599,7 +618,7 @@
         hbm=(0, 1),
         sems=6 + 2 * len(XC),
         vmem=VM,
-        pinned=True,
+        pinned=(0, 1, 2, 3),
     )
     xlo, xhi = shift(xh, "gx", 1), shift(xl, "gx", -1)
     ylo, yhi = shift(yh, "gy", 1), shift(yl, "gy", -1)
@@ -623,32 +642,36 @@
     back = lax.all_to_all(back.reshape(NB, 16, NZ), "gx", 0, 0, tiled=True)
     soly, rec = call(
         second_body,
-        [block, (16 * CX, NZ)],
+        [block, (15 * CX, NZ)],
         [back.reshape(NB * 16, NZ), sol, lsp, rsp, lsp_h, rsp_h, scaled, gys, ly, ry],
         [(6 * CX * ROWS, NZ), (6 * ROWS, NZ), (6 * ROWS, NZ), block],
     )
     others = [shift(rec, "gy", k) for k in (1, 2, 3)]
-    hot, static, ranks, table = call(
+    ints, sampled = jax.ShapeDtypeStruct((8, PATCH), jnp.int32), (CX, PATCH)
+    ones = jax.ShapeDtypeStruct((NZ, PATCH), BF16)
+    hot, static, ranks, table, base, z_hot, x_left, x_right = call(
         patches_body,
+        [ones, (NZ, PATCH), ints, (3 * NZ, NZ), (8, PATCH), ones, sampled, sampled],
         [
-            jax.ShapeDtypeStruct((NZ, PATCH), BF16), (NZ, PATCH),
-            jax.ShapeDtypeStruct((8, PATCH), jnp.int32), (3 * NZ, NZ),
+            patch_cell.reshape(1, PATCH), patch_owner.reshape(1, PATCH), patch_cell,
+            soly, ly, ry,
         ],
-        [patch_cell.reshape(1, PATCH), patch_owner.reshape(1, PATCH)],
+        [(CX * CY * 8, NZ), pltpu.SMEM((PATCH,), jnp.int32)],
+        hbm=(2,),
+        sems=1,
         cost=COST,
     )
     new, send = call(
         finish_body,
         [block, (NB * NBY, NZ)],
-        [rec, *others, soly, ly, ry, patch_cell, hot, static, ranks],
-        [block, (6 * CX, NZ), (6 * CX, NZ), (CX * CY * 8, NZ), (NZ, PATCH)]
-        + [pltpu.SMEM((PATCH,), jnp.int32)],
-        hbm=(7,),
-        hbm_outs=(0,),
-        sems=25,
+        [rec, *others, base, z_hot, x_left, x_right, hot, static, ranks, soly, ly, ry],
+        [(6 * CX, NZ), (6 * CX, NZ), (NZ, PATCH)],
+        pinned=(0,),
     )
     recv = lax.all_to_all(send, ("gx", "gy"), 0, 0, tiled=True)
-    (far,) = call(sector_body, [(12, NZ)], [recv, table])
+    far, new = call(
+        sector_body, [(12, NZ), block], [recv, table, new], hbm_outs=(1,), sems=OUTS
+    )
     return new.reshape(6, CX, CY, NZ), far
 
 

time: 72.1 us -> 71.2 us (0.988)
  blocking collectives: 46.3 us -> 44.3 us
  waiting for transfers between devices: 5.71 us -> 7.35 us
  starting transfers between devices: 10 us -> 8.85 us
    all_to_all x1, blocking collectives: 15 us -> 13.1 us  [local(): recv = lax.all_to_all(send, ('gx', 'gy'), 0, 0, tiled=True)]
    ppermute x7, waiting for transfers between devices: 5.71 us -> 7.35 us  [shift(): lax.ppermute(value, axis, [(i, (i + by) % count) for i in range(count)])]
    ppermute x7, starting transfers between devices: 10 us -> 8.85 us  [shift(): lax.ppermute(value, axis, [(i, (i + by) % count) for i in range(count)])]
  transfers between devices with their start and end apart: 7 -> 7, of which waited for: 3 -> 4; matrix products, arithmetic and copies ran while one was open for 0% -> 0% of each run, Pallas kernels for 2% -> 5%
where the time goes in v3:
time: 71.2 us; the launch traced here: 71 us
  blocking collectives  44.3 us (62%)
  Pallas kernels  9.7 us (14%)
  starting transfers between devices  8.85 us (12%)
  waiting for transfers between devices  7.35 us (10%)
  between operations  0.72 us (1%)
    all_to_all x1, blocking collectives, local(): rec = lax.all_to_all(send.reshape(NB, 16, NZ), 'gx', 0, 0, tiled=True)  18.8 us
    all_to_all x1, blocking collectives, local(): recv = lax.all_to_all(send, ('gx', 'gy'), 0, 0, tiled=True)  13.1 us
    all_to_all x1, blocking collectives, local(): back = lax.all_to_all(back.reshape(NB, 16, NZ), 'gx', 0, 0, tiled=True)  12.5 us
    pallas_call x8, Pallas kernels, call(): pl.pallas_call(body, out_shape=shapes, in_specs=[place(i, hbm) for i in r...  9.7 us
    ppermute x7, starting transfers between devices, shift(): lax.ppermute(value, axis, [(i, (i + by) % count) for i in range(count)])  8.85 us
    ppermute x7, waiting for transfers between devices, shift(): lax.ppermute(value, axis, [(i, (i + by) % count) for i in range(count)])  7.35 us
  transfers between devices with their start and end apart: 7, of which 4 were waited for; matrix products, arithmetic and copies ran while one was open for 0% of the time, Pallas kernels for 5%

profile of v3, /device:TPU:1, one launch (start us, length us, event | category | flops | bytes accessed | tf_op | source)
XLA Modules:
  0.0 71.0 jit_solution(14140602187422216008)
XLA Ops:
  0.7 1.2 %shard_map.69 = (f32[184,128]{1,0:T(8,128)S(1)}, f32[184,128]{1,0:T(8,128)S(1)}, f32[176,128]{1,0:T(8,128)S(1)}, f32[176,128]{1,0:T(8,128)S(1)}) custom-call(f32[96,24,128]{2,1,0:T(8,128)} %bitcast.14, s32[16,24,128]{2,1,0:T(8,128)} %mat.1), custom_call_target="tpu_custom_call" | custom-call | tf_op jit(solution)/shard_map/pallas_call | solution.py:47
  1.9 2.8 %collective-permute-start = (f32[184,128]{1,0:T(8,128)S(1)}, f32[184,128]{1,0:T(8,128)S(1)}, u32[]{:S(2)}, u32[]{:S(2)}) collective-permute-start(f32[184,128]{1,0:T(8,128)S(1)} %get-tuple-element.38), channel_id=1, source_target_pairs={{0,4},{4,8},{8,12},{12,16},{16,20},{20,24},{24,28},{28,32},{32,36}... | collective-permute-start | bytes 282632 | tf_op jit(solution)/shard_map/ppermute | solution.py:604
  4.6 0.0 collective-permute-start.1
  4.6 1.2 %collective-permute-start.2 = (f32[176,128]{1,0:T(8,128)S(1)}, f32[176,128]{1,0:T(8,128)S(1)}, u32[]{:S(2)}, u32[]{:S(2)}) collective-permute-start(f32[176,128]{1,0:T(8,128)S(1)} %get-tuple-element.40), channel_id=1, source_target_pairs={{0,1},{1,2},{2,3},{3,0},{4,5},{5,6},{6,7},{7,4},{8,9},{9,10},{10,1... | collective-permute-start | bytes 270344 | tf_op jit(solution)/shard_map/ppermute | solution.py:604
  5.9 1.5 %collective-permute-start.3 = (f32[176,128]{1,0:T(8,128)S(1)}, f32[176,128]{1,0:T(8,128)S(1)}, u32[]{:S(2)}, u32[]{:S(2)}) collective-permute-start(f32[176,128]{1,0:T(8,128)S(1)} %get-tuple-element.41), channel_id=1, source_target_pairs={{0,3},{1,0},{2,1},{3,2},{4,7},{5,4},{6,5},{7,6},{8,11},{9,8},{10,9... | collective-permute-start | bytes 270344 | tf_op jit(solution)/shard_map/ppermute | solution.py:604
  7.3 1.5 %shard_map.68 = (f32[384,128]{1,0:T(8,128)S(1)}, f32[2304,128]{1,0:T(8,128)S(1)}, f32[384,128]{1,0:T(8,128)S(1)}, f32[384,128]{1,0:T(8,128)S(1)}, f32[384,128]{1...) custom-call(f32[2304,128]{1,0:T(8,128)S(1)} %bitcast.15, ...), custom_call_target="tpu_custom_call" | custom-call | flops 4000000 | bytes 4000000 | tf_op jit(solution)/shard_map/pallas_call | solution.py:47
  8.8 0.4 collective-permute-done.2.ylo
  9.2 0.0 collective-permute-done.3.yhi
  9.2 0.0 collective-permute-done.xlo
  9.2 0.7 shard_map.70
  10.0 18.8 %all_to_all.21 = f32[32,16,128]{2,1,0:T(8,128)S(1)} all-to-all(f32[32,16,128]{2,1,0:T(8,128)S(1)} %bitcast.22), channel_id=1, replica_groups=mesh['gx'=32,'gy'=4] {'gx'}, dimensions={0} | all-to-all | bytes 524288 | tf_op jit(solution)/shard_map/all_to_all | solution.py:640
  28.7 0.5 shard_map.71
  29.2 12.5 %all_to_all.22 = f32[32,16,128]{2,1,0:T(8,128)S(1)} all-to-all(f32[32,16,128]{2,1,0:T(8,128)S(1)} %bitcast.19), channel_id=1, replica_groups=mesh['gx'=32,'gy'=4] {'gx'}, dimensions={0} | all-to-all | bytes 524288 | tf_op jit(solution)/shard_map/all_to_all | solution.py:642
  41.7 1.5 %shard_map.72 = (f32[2304,128]{1,0:T(8,128)S(1)}, f32[240,128]{1,0:T(8,128)S(1)}) custom-call(f32[512,128]{1,0:T(8,128)S(1)} %bitcast.17, f32[3072,128]{1,0:T(8,128)S(1)} %get-tuple-element.44.sol, f32[384,128]{1,0:T(8,128)S(1)} %get-tuple-element.36.lsp, f32[384,128]{1,0:T(8,128)S(1)} %get-tuple-element.37.rsp, f32[128,128]{1,0:T(8,128)S(1)} %get-tuple-element.45.lsp_h, ...), custom_call_target="tpu_custom_call" | custom-call | tf_op jit(solution)/shard_map/pallas_call | solution.py:47
  43.2 2.7 %collective-permute-start.6 = (f32[240,128]{1,0:T(8,128)S(1)}, f32[240,128]{1,0:T(8,128)S(1)}, u32[]{:S(2)}, u32[]{:S(2)}) collective-permute-start(f32[240,128]{1,0:T(8,128)S(1)} %get-tuple-element.50.rec0), channel_id=1, source_target_pairs={{0,3},{1,0},{2,1},{3,2},{4,7},{5,4},{6,5},{7,6},{8,11},{9,8},{10,9... | collective-permute-start | bytes 368648 | tf_op jit(solution)/shard_map/ppermute | solution.py:604
  45.9 0.3 collective-permute-start.5
  46.3 0.3 collective-permute-start.4
  46.6 1.8 %shard_map.73 = (bf16[128,256]{1,0:T(8,128)(2,1)S(1)}, f32[128,256]{1,0:T(8,128)S(1)}, s32[8,256]{1,0:T(8,128)S(1)}, f32[384,128]{1,0:T(8,128)S(1)}, f32[8,256]{...) custom-call(s32[1,256]{1,0:T(1,128)S(1)} %bitcast.24, ...), custom_call_target="tpu_custom_call" | custom-call | flops 4000000 | bytes 4000000 | tf_op jit(solution)/shard_map/pallas_call | solution.py:47
  48.4 2.6 %collective-permute-done.6.rec3 = f32[240,128]{1,0:T(8,128)S(1)} collective-permute-done((f32[240,128]{1,0:T(8,128)S(1)}, f32[240,128]{1,0:T(8,128)S(1)}, u32[]{:S(2)}, u32[]{:S(2)}) %collective-permute-start.6) | collective-permute-done | bytes 122912 | tf_op jit(solution)/shard_map/ppermute | solution.py:604
  51.0 0.8 %collective-permute-done.5.rec2 = f32[240,128]{1,0:T(8,128)S(1)} collective-permute-done((f32[240,128]{1,0:T(8,128)S(1)}, f32[240,128]{1,0:T(8,128)S(1)}, u32[]{:S(2)}, u32[]{:S(2)}) %collective-permute-start.5) | collective-permute-done | bytes 122912 | tf_op jit(solution)/shard_map/ppermute | solution.py:604
  51.8 3.5 %collective-permute-done.4.rec1 = f32[240,128]{1,0:T(8,128)S(1)} collective-permute-done((f32[240,128]{1,0:T(8,128)S(1)}, f32[240,128]{1,0:T(8,128)S(1)}, u32[]{:S(2)}, u32[]{:S(2)}) %collective-permute-start.4) | collective-permute-done | bytes 122912 | tf_op jit(solution)/shard_map/ppermute | solution.py:604
  55.3 0.9 %shard_map.74 = (f32[2304,128]{1,0:T(8,128)S(1)}, f32[128,128]{1,0:T(8,128)S(1)}) custom-call(f32[240,128]{1,0:T(8,128)S(1)} %get-tuple-element.50.rec0, f32[240,128]{1,0:T(8,128)S(1)} %collective-permute-done.4.rec1, f32[240,128]{1,0:T(8,128)S(1)} %collective-permute-done.5.rec2, f32[240,128]{1,0:T(8,128)S(1)} %collective-permute-done.6.rec3, ...), custom_call_target="tpu_custom_call" | custom-call | tf_op jit(solution)/shard_map/pallas_call | solution.py:47
  56.3 13.1 %all_to_all.23 = f32[128,1,128]{2,1,0:T(1,128)S(1)} all-to-all(f32[128,1,128]{2,1,0:T(1,128)S(1)} %bitcast.23), channel_id=1, replica_groups=mesh['gx'=32,'gy'=4] {'gx','gy'}, dimensions={0} | all-to-all | bytes 131072 | tf_op jit(solution)/shard_map/all_to_all | solution.py:671
  69.4 1.6 %shard_map.75 = (f32[12,128]{1,0:T(8,128)}, f32[2304,128]{1,0:T(8,128)}) custom-call(f32[128,128]{1,0:T(8,128)S(1)} %bitcast.21, f32[384,128]{1,0:T(8,128)S(1)} %get-tuple-element.60.table, f32[2304,128]{1,0:T(8,128)S(1)} %get-tuple-element.61.made), custom_call_target="tpu_custom_call" | custom-call | tf_op jit(solution)/shard_map/pallas_call | solution.py:47
  (11 shorter events, 0.0 us)
Async XLA Ops:
  0.6 6.7 %copy-start.1 = (s32[16,24,128]{2,1,0:T(8,128)S(1)}, s32[16,24,128]{2,1,0:T(8,128)}, u32[]{:S(2)}) copy-start(s32[16,24,128]{2,1,0:T(8,128)} %mat.1) | copy-start | bytes 589828
  0.6 6.7 %copy-start = (f32[6,16,24,128]{3,2,1,0:T(8,128)S(1)}, f32[6,16,24,128]{3,2,1,0:T(8,128)}, u32[]{:S(2)}) copy-start(f32[6,16,24,128]{3,2,1,0:T(8,128)} %param.5) | copy-start | bytes 3538948
  0.6 6.7 %copy-start.4 = (f32[16]{0:T(128)S(1)}, f32[16]{0:T(128)}, u32[]{:S(2)}) copy-start(f32[16]{0:T(128)} %perm_hbm.1) | copy-start | bytes 196
  1.9 7.4 %collective-permute-start = (f32[184,128]{1,0:T(8,128)S(1)}, f32[184,128]{1,0:T(8,128)S(1)}, u32[]{:S(2)}, u32[]{:S(2)}) collective-permute-start(f32[184,128]{1,0:T(8,128)S(1)} %get-tuple-element.38), channel_id=1, source_target_pairs={{0,4},{4,8},{8,12},{12,16},{16,20},{20,24},{24,28},{28,32},{32,36}... | collective-permute-start | bytes 282632 | tf_op jit(solution)/shard_map/ppermute | solution.py:604
  4.6 4.6 %collective-permute-start.1 = (f32[184,128]{1,0:T(8,128)S(1)}, f32[184,128]{1,0:T(8,128)S(1)}, u32[]{:S(2)}, u32[]{:S(2)}) collective-permute-start(f32[184,128]{1,0:T(8,128)S(1)} %get-tuple-element.39), channel_id=1, source_target_pairs={{0,124},{4,0},{8,4},{12,8},{16,12},{20,16},{24,20},{28,24},{32,28}... | collective-permute-start | bytes 282632 | tf_op jit(solution)/shard_map/ppermute | solution.py:604
  4.6 4.6 %collective-permute-start.2 = (f32[176,128]{1,0:T(8,128)S(1)}, f32[176,128]{1,0:T(8,128)S(1)}, u32[]{:S(2)}, u32[]{:S(2)}) collective-permute-start(f32[176,128]{1,0:T(8,128)S(1)} %get-tuple-element.40), channel_id=1, source_target_pairs={{0,1},{1,2},{2,3},{3,0},{4,5},{5,6},{6,7},{7,4},{8,9},{9,10},{10,1... | collective-permute-start | bytes 270344 | tf_op jit(solution)/shard_map/ppermute | solution.py:604
  5.9 3.4 %collective-permute-start.3 = (f32[176,128]{1,0:T(8,128)S(1)}, f32[176,128]{1,0:T(8,128)S(1)}, u32[]{:S(2)}, u32[]{:S(2)}) collective-permute-start(f32[176,128]{1,0:T(8,128)S(1)} %get-tuple-element.41), channel_id=1, source_target_pairs={{0,3},{1,0},{2,1},{3,2},{4,7},{5,4},{6,5},{7,6},{8,11},{9,8},{10,9... | collective-permute-start | bytes 270344 | tf_op jit(solution)/shard_map/ppermute | solution.py:604
  41.7 5.0 %copy-start.2 = (s32[256]{0:T(256)S(1)}, s32[256]{0:T(256)}, u32[]{:S(2)}) copy-start(s32[256]{0:T(256)} %cell_hbm.1) | copy-start | bytes 3076
  41.7 5.0 %copy-start.3 = (s32[256,1]{0,1:T(1,128)S(1)}, s32[256,1]{0,1:T(1,128)}, u32[]{:S(2)}) copy-start(s32[256,1]{0,1:T(1,128)} %param.9) | copy-start | bytes 3076
  43.2 7.8 %collective-permute-start.6 = (f32[240,128]{1,0:T(8,128)S(1)}, f32[240,128]{1,0:T(8,128)S(1)}, u32[]{:S(2)}, u32[]{:S(2)}) collective-permute-start(f32[240,128]{1,0:T(8,128)S(1)} %get-tuple-element.50.rec0), channel_id=1, source_target_pairs={{0,3},{1,0},{2,1},{3,2},{4,7},{5,4},{6,5},{7,6},{8,11},{9,8},{10,9... | collective-permute-start | bytes 368648 | tf_op jit(solution)/shard_map/ppermute | solution.py:604
  45.9 5.9 %collective-permute-start.5 = (f32[240,128]{1,0:T(8,128)S(1)}, f32[240,128]{1,0:T(8,128)S(1)}, u32[]{:S(2)}, u32[]{:S(2)}) collective-permute-start(f32[240,128]{1,0:T(8,128)S(1)} %get-tuple-element.50.rec0), channel_id=1, source_target_pairs={{0,2},{1,3},{2,0},{3,1},{4,6},{5,7},{6,4},{7,5},{8,10},{9,11},{10,... | collective-permute-start | bytes 368648 | tf_op jit(solution)/shard_map/ppermute | solution.py:604
  46.3 9.1 %collective-permute-start.4 = (f32[240,128]{1,0:T(8,128)S(1)}, f32[240,128]{1,0:T(8,128)S(1)}, u32[]{:S(2)}, u32[]{:S(2)}) collective-permute-start(f32[240,128]{1,0:T(8,128)S(1)} %get-tuple-element.50.rec0), channel_id=1, source_target_pairs={{0,1},{1,2},{2,3},{3,0},{4,5},{5,6},{6,7},{7,4},{8,9},{9,10},{10,1... | collective-permute-start | bytes 368648 | tf_op jit(solution)/shard_map/ppermute | solution.py:604

commit v4 on v3

--- a/solution.py
+++ b/solution.py
@@ -351,7 +351,7 @@
 
 
 def second_body(
-    back, sol, lsp, rsp, lsp_h, rsp_h, scaled, gys, ly, ry, soly, rec, mid, inc, out, r2
+    back, sol, lsp, rsp, lsp_h, rsp_h, scaled, gys, ly, ry, r2, rec, mid, inc, out
 ):
     for c in range(6):
         inc[ds(c * ROWS, ROWS), :] = back[ds(c, ROWS, 16), :]
@@ -406,7 +406,6 @@
         for c in range(6):
             here = ds(c * CX * CY + y, CX, CY)
             us[c] = r2[here, :] + g * us[c]
-            soly[here, :] = us[c]
     for c in range(6):
         rec[ds(c * CX, CX), :] = us[c]
     rec[ds(6 * CX, CX), :] = ly[ds(0, CX, CY), :]
@@ -418,8 +417,8 @@
 
 
 def patches_body(
-    cell_row, owner_row, cell_hbm, soly, ly, ry,
-    hot, spread, ranks, table, base, z_hot, x_left, x_right, lines, cell, sem,
+    cell_row, owner_row, cell_hbm, reduced, gys, ly, ry,
+    soly, hot, spread, ranks, table, base, z_hot, x_left, x_right, lines, cell, sem,
 ):
     copy = pltpu.make_async_copy(cell_hbm, cell, sem.at[0])
     copy.start()
@@ -449,10 +448,16 @@
     table[ds(0, NZ), :] = KAPPA * sin_theta * cos_phi[0:1]
     table[ds(NZ, NZ), :] = KAPPA * sin_theta * sin_phi[0:1]
     table[ds(2 * NZ, NZ), :] = KAPPA * cos_theta
+    us = [jnp.zeros((CX, NZ), F32)] * 6
+    for y in reversed(range(CY)):
+        g = gys[ds(y * CX, CX), :]
+        for c in range(6):
+            at = ds(c * CX * CY + y, CX, CY)
+            us[c] = reduced[at, :] + g * us[c]
+            soly[at, :] = us[c]
+            lines[ds(y * 8 + c, CX, CY * 8), :] = us[c]
     for x_own in range(CX):
         at = ds(x_own * CY, CY)
-        for c in range(6):
-            lines[ds(x_own * (CY * 8) + c, CY, 8), :] = soly[ds((c * CX + x_own) * CY, CY), :]
         lines[ds(x_own * (CY * 8) + 6, CY, 8), :] = ly[at, :]
         lines[ds(x_own * (CY * 8) + 7, CY, 8), :] = ry[at, :]
     copy.wait()
@@ -489,14 +494,17 @@
 ):
     gy = lax.axis_index("gy")
 
-    def get(rec, k):
-        return rec[ds(k * CX, CX), :]
+    def get(choices, k):
+        value = choices[-1][ds(k * CX, CX), :]
+        for at, rec in choices[:-1]:
+            value = jnp.where(gy == at, rec[ds(k * CX, CX), :], value)
+        return value
 
     zero = jnp.zeros((CX, NZ), F32)
 
     def sweep(order, up):
         m, n = [zero] * 6, zero
-        near, far, own, other = (8, 0, 14, 6) if up else (0, 8, 6, 14)
+        near, far, mine, other = (8, 0, 14, 6) if up else (0, 8, 6, 14)
         for rec, valid in order:
             cross = get(rec, 7)
             gain = 1.0 / (1.0 - get(rec, other) * n)
@@ -505,19 +513,34 @@
                 + cross * (m[c] + n * (gain * (get(rec, far + c) + get(rec, other) * m[c])))
                 for c in range(6)
             ]
-            m = [jnp.where(valid, v, 0.0) for v in value]
-            n = jnp.where(valid, get(rec, own) + cross * (n * (gain * cross)), 0.0)
+            m = [jnp.where(valid, v, old) for v, old in zip(value, m)]
+            n = jnp.where(valid, get(rec, mine) + cross * (n * (gain * cross)), n)
         return m, n
 
-    below, below_gain = sweep([(rec3, gy >= 3), (rec2, gy >= 2), (rec1, gy >= 1)], True)
-    above, above_gain = sweep([(rec1, gy <= 0), (rec2, gy <= 1), (rec3, gy <= 2)], False)
-    a, cross, d = get(rec0, 6), get(rec0, 7), get(rec0, 14)
+    below, below_gain = sweep(
+        [
+            (((1, rec1), (2, rec2), rec3), gy >= 1),
+            (((2, rec3), rec2), gy >= 2),
+            ((rec1,), gy >= 3),
+        ],
+        True,
+    )
+    above, above_gain = sweep(
+        [
+            (((0, rec3), (1, rec2), rec1), gy <= 2),
+            (((0, rec2), rec3), gy <= 1),
+            ((rec1,), gy <= 0),
+        ],
+        False,
+    )
+    own = (rec0,)
+    a, cross, d = get(own, 6), get(own, 7), get(own, 14)
     ll, lt = 1.0 - a * below_gain, -cross * above_gain
     tl, tt = -cross * below_gain, 1.0 - d * above_gain
     over = 1.0 / (ll * tt - lt * tl)
     for c in range(6):
-        p = get(rec0, c) + a * below[c] + cross * above[c]
-        q = get(rec0, 8 + c) + cross * below[c] + d * above[c]
+        p = get(own, c) + a * below[c] + cross * above[c]
+        q = get(own, 8 + c) + cross * below[c] + d * above[c]
         lead, tail = (p * tt - lt * q) * over, (ll * q - tl * p) * over
         inc[ds(c * CX, CX), :] = below[c] + below_gain * lead
         out[ds(c * CX, CX), :] = above[c] + above_gain * tail
@@ -640,21 +663,23 @@
     rec = lax.all_to_all(send.reshape(NB, 16, NZ), "gx", 0, 0, tiled=True)
     (back,) = call(join_body, [(NB * 16, NZ)], [rec.reshape(NB * 16, NZ)], [(NB * 8, NZ)] * 4)
     back = lax.all_to_all(back.reshape(NB, 16, NZ), "gx", 0, 0, tiled=True)
-    soly, rec = call(
+    reduced, rec = call(
         second_body,
         [block, (15 * CX, NZ)],
         [back.reshape(NB * 16, NZ), sol, lsp, rsp, lsp_h, rsp_h, scaled, gys, ly, ry],
-        [(6 * CX * ROWS, NZ), (6 * ROWS, NZ), (6 * ROWS, NZ), block],
-    )
-    others = [shift(rec, "gy", k) for k in (1, 2, 3)]
+        [(6 * CX * ROWS, NZ), (6 * ROWS, NZ), (6 * ROWS, NZ)],
+    )
+    others = [
+        lax.ppermute(rec, "gy", [(i, i ^ k) for i in range(NBY)]) for k in (1, 2, 3)
+    ]
     ints, sampled = jax.ShapeDtypeStruct((8, PATCH), jnp.int32), (CX, PATCH)
     ones = jax.ShapeDtypeStruct((NZ, PATCH), BF16)
-    hot, static, ranks, table, base, z_hot, x_left, x_right = call(
+    soly, hot, static, ranks, table, base, z_hot, x_left, x_right = call(
         patches_body,
-        [ones, (NZ, PATCH), ints, (3 * NZ, NZ), (8, PATCH), ones, sampled, sampled],
+        [block, ones, (NZ, PATCH), ints, (3 * NZ, NZ), (8, PATCH), ones, sampled, sampled],
         [
             patch_cell.reshape(1, PATCH), patch_owner.reshape(1, PATCH), patch_cell,
-            soly, ly, ry,
+            reduced, gys, ly, ry,
         ],
         [(CX * CY * 8, NZ), pltpu.SMEM((PATCH,), jnp.int32)],
         hbm=(2,),

time: 71.2 us -> 70.8 us (level)
  waiting for transfers between devices: 7.35 us -> 3.34 us
  blocking collectives: 44.3 us -> 47.1 us
  Pallas kernels: 9.7 us -> 10.5 us
    ppermute x7 -> x4, waiting for transfers between devices: 7.35 us -> 0.42 us  [shift(): lax.ppermute(value, axis, [(i, (i + by) % count) for i in range(count)])]
    ppermute x0 -> x3, starting transfers between devices: none -> 3.43 us  [local(): lax.ppermute(rec, 'gy', [(i, i ^ k) for i in range(NBY)])]
    ppermute x7 -> x4, starting transfers between devices: 8.85 us -> 5.43 us  [shift(): lax.ppermute(value, axis, [(i, (i + by) % count) for i in range(count)])]
    ppermute x0 -> x3, waiting for transfers between devices: none -> 2.92 us  [local(): lax.ppermute(rec, 'gy', [(i, i ^ k) for i in range(NBY)])]
    all_to_all x1, blocking collectives: 13.1 us -> 15.9 us  [local(): recv = lax.all_to_all(send, ('gx', 'gy'), 0, 0, tiled=True)]
    pallas_call x8, Pallas kernels: 9.7 us -> 10.5 us  [call(): pl.pallas_call(body, out_shape=shapes, in_specs=[place(i, hbm) for i in r...]
  transfers between devices with their start and end apart: 7 -> 7, of which waited for: 4 -> 4; matrix products, arithmetic and copies ran while one was open for 0% -> 0% of each run, Pallas kernels for 5% -> 6%
where the time goes in v4:
time: 70.8 us; the launch traced here: 70.6 us
  blocking collectives  47.1 us (67%)
  Pallas kernels  10.5 us (15%)
  starting transfers between devices  8.86 us (13%)
  waiting for transfers between devices  3.34 us (5%)
  between operations  0.72 us (1%)
    all_to_all x1, blocking collectives, local(): rec = lax.all_to_all(send.reshape(NB, 16, NZ), 'gx', 0, 0, tiled=True)  18.8 us
    all_to_all x1, blocking collectives, local(): recv = lax.all_to_all(send, ('gx', 'gy'), 0, 0, tiled=True)  15.9 us
    all_to_all x1, blocking collectives, local(): back = lax.all_to_all(back.reshape(NB, 16, NZ), 'gx', 0, 0, tiled=True)  12.5 us
    pallas_call x8, Pallas kernels, call(): pl.pallas_call(body, out_shape=shapes, in_specs=[place(i, hbm) for i in r...  10.5 us
    ppermute x4, starting transfers between devices, shift(): lax.ppermute(value, axis, [(i, (i + by) % count) for i in range(count)])  5.43 us
    ppermute x3, starting transfers between devices, local(): lax.ppermute(rec, 'gy', [(i, i ^ k) for i in range(NBY)])  3.43 us
    ppermute x3, waiting for transfers between devices, local(): lax.ppermute(rec, 'gy', [(i, i ^ k) for i in range(NBY)])  2.92 us
  transfers between devices with their start and end apart: 7, of which 4 were waited for; matrix products, arithmetic and copies ran while one was open for 0% of the time, Pallas kernels for 6%

profile of v4, /device:TPU:1, one launch (start us, length us, event | category | flops | bytes accessed | tf_op | source)
XLA Modules:
  0.0 70.6 jit_solution(4372724354759518635)
XLA Ops:
  0.7 1.2 %shard_map.69 = (f32[184,128]{1,0:T(8,128)S(1)}, f32[184,128]{1,0:T(8,128)S(1)}, f32[176,128]{1,0:T(8,128)S(1)}, f32[176,128]{1,0:T(8,128)S(1)}) custom-call(f32[96,24,128]{2,1,0:T(8,128)} %bitcast.14, s32[16,24,128]{2,1,0:T(8,128)} %mat.1), custom_call_target="tpu_custom_call" | custom-call | tf_op jit(solution)/shard_map/pallas_call | solution.py:47
  1.9 2.8 %collective-permute-start = (f32[184,128]{1,0:T(8,128)S(1)}, f32[184,128]{1,0:T(8,128)S(1)}, u32[]{:S(2)}, u32[]{:S(2)}) collective-permute-start(f32[184,128]{1,0:T(8,128)S(1)} %get-tuple-element.39), channel_id=1, source_target_pairs={{0,4},{4,8},{8,12},{12,16},{16,20},{20,24},{24,28},{28,32},{32,36}... | collective-permute-start | bytes 282632 | tf_op jit(solution)/shard_map/ppermute | solution.py:627
  4.6 0.0 collective-permute-start.1
  4.6 1.2 %collective-permute-start.2 = (f32[176,128]{1,0:T(8,128)S(1)}, f32[176,128]{1,0:T(8,128)S(1)}, u32[]{:S(2)}, u32[]{:S(2)}) collective-permute-start(f32[176,128]{1,0:T(8,128)S(1)} %get-tuple-element.41), channel_id=1, source_target_pairs={{0,1},{1,2},{2,3},{3,0},{4,5},{5,6},{6,7},{7,4},{8,9},{9,10},{10,1... | collective-permute-start | bytes 270344 | tf_op jit(solution)/shard_map/ppermute | solution.py:627
  5.9 1.5 %collective-permute-start.3 = (f32[176,128]{1,0:T(8,128)S(1)}, f32[176,128]{1,0:T(8,128)S(1)}, u32[]{:S(2)}, u32[]{:S(2)}) collective-permute-start(f32[176,128]{1,0:T(8,128)S(1)} %get-tuple-element.42), channel_id=1, source_target_pairs={{0,3},{1,0},{2,1},{3,2},{4,7},{5,4},{6,5},{7,6},{8,11},{9,8},{10,9... | collective-permute-start | bytes 270344 | tf_op jit(solution)/shard_map/ppermute | solution.py:627
  7.3 1.5 %shard_map.68 = (f32[384,128]{1,0:T(8,128)S(1)}, f32[2304,128]{1,0:T(8,128)S(1)}, f32[384,128]{1,0:T(8,128)S(1)}, f32[384,128]{1,0:T(8,128)S(1)}, f32[384,128]{1...) custom-call(f32[2304,128]{1,0:T(8,128)S(1)} %bitcast.15, ...), custom_call_target="tpu_custom_call" | custom-call | flops 4000000 | bytes 4000000 | tf_op jit(solution)/shard_map/pallas_call | solution.py:47
  8.8 0.4 collective-permute-done.2.ylo
  9.2 0.0 collective-permute-done.3.yhi
  9.2 0.0 collective-permute-done.xlo
  9.2 0.7 shard_map.70
  10.0 18.8 %all_to_all.21 = f32[32,16,128]{2,1,0:T(8,128)S(1)} all-to-all(f32[32,16,128]{2,1,0:T(8,128)S(1)} %bitcast.22), channel_id=1, replica_groups=mesh['gx'=32,'gy'=4] {'gx'}, dimensions={0} | all-to-all | bytes 524288 | tf_op jit(solution)/shard_map/all_to_all | solution.py:663
  28.7 0.5 shard_map.71
  29.2 12.5 %all_to_all.22 = f32[32,16,128]{2,1,0:T(8,128)S(1)} all-to-all(f32[32,16,128]{2,1,0:T(8,128)S(1)} %bitcast.19), channel_id=1, replica_groups=mesh['gx'=32,'gy'=4] {'gx'}, dimensions={0} | all-to-all | bytes 524288 | tf_op jit(solution)/shard_map/all_to_all | solution.py:665
  41.7 1.4 %shard_map.72 = (f32[2304,128]{1,0:T(8,128)S(1)}, f32[240,128]{1,0:T(8,128)S(1)}) custom-call(f32[512,128]{1,0:T(8,128)S(1)} %bitcast.17, f32[3072,128]{1,0:T(8,128)S(1)} %get-tuple-element.45.sol, f32[384,128]{1,0:T(8,128)S(1)} %get-tuple-element.37.lsp, f32[384,128]{1,0:T(8,128)S(1)} %get-tuple-element.38.rsp, f32[128,128]{1,0:T(8,128)S(1)} %get-tuple-element.46.lsp_h, ...), custom_call_target="tpu_custom_call" | custom-call | tf_op jit(solution)/shard_map/pallas_call | solution.py:47
  43.0 2.8 %collective-permute-start.6 = (f32[240,128]{1,0:T(8,128)S(1)}, f32[240,128]{1,0:T(8,128)S(1)}, u32[]{:S(2)}, u32[]{:S(2)}) collective-permute-start(f32[240,128]{1,0:T(8,128)S(1)} %get-tuple-element.51.rec0), channel_id=1, source_target_pairs={{0,3},{1,2},{2,1},{3,0},{4,7},{5,6},{6,5},{7,4},{8,11},{9,10},{10,... | collective-permute-start | bytes 368648 | tf_op jit(solution)/shard_map/ppermute | solution.py:673
  45.8 0.3 collective-permute-start.5
  46.1 0.3 collective-permute-start.4
  46.5 2.7 %shard_map.73 = (f32[2304,128]{1,0:T(8,128)S(1)}, bf16[128,256]{1,0:T(8,128)(2,1)S(1)}, f32[128,256]{1,0:T(8,128)S(1)}, s32[8,256]{1,0:T(8,128)S(1)}, f32[384,12...) custom-call(s32[1,256]{1,0:T(1,128)S(1)} %bitcast.24, ...), custom_call_target="tpu_custom_call" | custom-call | flops 4000000 | bytes 4000000 | tf_op jit(solution)/shard_map/pallas_call | solution.py:47
  49.2 1.8 %collective-permute-done.6.rec3 = f32[240,128]{1,0:T(8,128)S(1)} collective-permute-done((f32[240,128]{1,0:T(8,128)S(1)}, f32[240,128]{1,0:T(8,128)S(1)}, u32[]{:S(2)}, u32[]{:S(2)}) %collective-permute-start.6) | collective-permute-done | bytes 122912 | tf_op jit(solution)/shard_map/ppermute | solution.py:673
  51.0 0.7 collective-permute-done.5.rec2
  51.7 0.5 collective-permute-done.4.rec1
  52.1 0.9 %shard_map.74 = (f32[2304,128]{1,0:T(8,128)S(1)}, f32[128,128]{1,0:T(8,128)S(1)}) custom-call(f32[240,128]{1,0:T(8,128)S(1)} %get-tuple-element.51.rec0, f32[240,128]{1,0:T(8,128)S(1)} %collective-permute-done.4.rec1, f32[240,128]{1,0:T(8,128)S(1)} %collective-permute-done.5.rec2, f32[240,128]{1,0:T(8,128)S(1)} %collective-permute-done.6.rec3, ...), custom_call_target="tpu_custom_call" | custom-call | tf_op jit(solution)/shard_map/pallas_call | solution.py:47
  53.0 15.9 %all_to_all.23 = f32[128,1,128]{2,1,0:T(1,128)S(1)} all-to-all(f32[128,1,128]{2,1,0:T(1,128)S(1)} %bitcast.23), channel_id=1, replica_groups=mesh['gx'=32,'gy'=4] {'gx','gy'}, dimensions={0} | all-to-all | bytes 131072 | tf_op jit(solution)/shard_map/all_to_all | solution.py:696
  68.9 1.6 %shard_map.75 = (f32[12,128]{1,0:T(8,128)}, f32[2304,128]{1,0:T(8,128)}) custom-call(f32[128,128]{1,0:T(8,128)S(1)} %bitcast.21, f32[384,128]{1,0:T(8,128)S(1)} %get-tuple-element.62.table, f32[2304,128]{1,0:T(8,128)S(1)} %get-tuple-element.63.made), custom_call_target="tpu_custom_call" | custom-call | tf_op jit(solution)/shard_map/pallas_call | solution.py:47
  (11 shorter events, 0.0 us)
Async XLA Ops:
  0.6 6.7 %copy-start.1 = (s32[16,24,128]{2,1,0:T(8,128)S(1)}, s32[16,24,128]{2,1,0:T(8,128)}, u32[]{:S(2)}) copy-start(s32[16,24,128]{2,1,0:T(8,128)} %mat.1) | copy-start | bytes 589828
  0.6 6.7 %copy-start = (f32[6,16,24,128]{3,2,1,0:T(8,128)S(1)}, f32[6,16,24,128]{3,2,1,0:T(8,128)}, u32[]{:S(2)}) copy-start(f32[6,16,24,128]{3,2,1,0:T(8,128)} %param.5) | copy-start | bytes 3538948
  0.6 6.7 %copy-start.4 = (f32[16]{0:T(128)S(1)}, f32[16]{0:T(128)}, u32[]{:S(2)}) copy-start(f32[16]{0:T(128)} %perm_hbm.1) | copy-start | bytes 196
  1.9 7.4 %collective-permute-start = (f32[184,128]{1,0:T(8,128)S(1)}, f32[184,128]{1,0:T(8,128)S(1)}, u32[]{:S(2)}, u32[]{:S(2)}) collective-permute-start(f32[184,128]{1,0:T(8,128)S(1)} %get-tuple-element.39), channel_id=1, source_target_pairs={{0,4},{4,8},{8,12},{12,16},{16,20},{20,24},{24,28},{28,32},{32,36}... | collective-permute-start | bytes 282632 | tf_op jit(solution)/shard_map/ppermute | solution.py:627
  4.6 4.6 %collective-permute-start.1 = (f32[184,128]{1,0:T(8,128)S(1)}, f32[184,128]{1,0:T(8,128)S(1)}, u32[]{:S(2)}, u32[]{:S(2)}) collective-permute-start(f32[184,128]{1,0:T(8,128)S(1)} %get-tuple-element.40), channel_id=1, source_target_pairs={{0,124},{4,0},{8,4},{12,8},{16,12},{20,16},{24,20},{28,24},{32,28}... | collective-permute-start | bytes 282632 | tf_op jit(solution)/shard_map/ppermute | solution.py:627
  4.6 4.6 %collective-permute-start.2 = (f32[176,128]{1,0:T(8,128)S(1)}, f32[176,128]{1,0:T(8,128)S(1)}, u32[]{:S(2)}, u32[]{:S(2)}) collective-permute-start(f32[176,128]{1,0:T(8,128)S(1)} %get-tuple-element.41), channel_id=1, source_target_pairs={{0,1},{1,2},{2,3},{3,0},{4,5},{5,6},{6,7},{7,4},{8,9},{9,10},{10,1... | collective-permute-start | bytes 270344 | tf_op jit(solution)/shard_map/ppermute | solution.py:627
  5.9 3.4 %collective-permute-start.3 = (f32[176,128]{1,0:T(8,128)S(1)}, f32[176,128]{1,0:T(8,128)S(1)}, u32[]{:S(2)}, u32[]{:S(2)}) collective-permute-start(f32[176,128]{1,0:T(8,128)S(1)} %get-tuple-element.42), channel_id=1, source_target_pairs={{0,3},{1,0},{2,1},{3,2},{4,7},{5,4},{6,5},{7,6},{8,11},{9,8},{10,9... | collective-permute-start | bytes 270344 | tf_op jit(solution)/shard_map/ppermute | solution.py:627
  41.7 4.8 %copy-start.2 = (s32[256]{0:T(256)S(1)}, s32[256]{0:T(256)}, u32[]{:S(2)}) copy-start(s32[256]{0:T(256)} %cell_hbm.1) | copy-start | bytes 3076
  41.7 4.8 %copy-start.3 = (s32[256,1]{0,1:T(1,128)S(1)}, s32[256,1]{0,1:T(1,128)}, u32[]{:S(2)}) copy-start(s32[256,1]{0,1:T(1,128)} %param.9) | copy-start | bytes 3076
  43.0 7.9 %collective-permute-start.6 = (f32[240,128]{1,0:T(8,128)S(1)}, f32[240,128]{1,0:T(8,128)S(1)}, u32[]{:S(2)}, u32[]{:S(2)}) collective-permute-start(f32[240,128]{1,0:T(8,128)S(1)} %get-tuple-element.51.rec0), channel_id=1, source_target_pairs={{0,3},{1,2},{2,1},{3,0},{4,7},{5,6},{6,5},{7,4},{8,11},{9,10},{10,... | collective-permute-start | bytes 368648 | tf_op jit(solution)/shard_map/ppermute | solution.py:673
  45.8 5.9 %collective-permute-start.5 = (f32[240,128]{1,0:T(8,128)S(1)}, f32[240,128]{1,0:T(8,128)S(1)}, u32[]{:S(2)}, u32[]{:S(2)}) collective-permute-start(f32[240,128]{1,0:T(8,128)S(1)} %get-tuple-element.51.rec0), channel_id=1, source_target_pairs={{0,2},{1,3},{2,0},{3,1},{4,6},{5,7},{6,4},{7,5},{8,10},{9,11},{10,... | collective-permute-start | bytes 368648 | tf_op jit(solution)/shard_map/ppermute | solution.py:673
  46.1 6.0 %collective-permute-start.4 = (f32[240,128]{1,0:T(8,128)S(1)}, f32[240,128]{1,0:T(8,128)S(1)}, u32[]{:S(2)}, u32[]{:S(2)}) collective-permute-start(f32[240,128]{1,0:T(8,128)S(1)} %get-tuple-element.51.rec0), channel_id=1, source_target_pairs={{0,1},{1,0},{2,3},{3,2},{4,5},{5,4},{6,7},{7,6},{8,9},{9,8},{10,11... | collective-permute-start | bytes 368648 | tf_op jit(solution)/shard_map/ppermute | solution.py:673

commit v5 on v4

--- a/solution.py
+++ b/solution.py
@@ -370,7 +370,7 @@
             )
         return carry
 
-    lax.fori_loop(0, CX, settle, 0, unroll=2)
+    lax.fori_loop(0, CX, settle, 0, unroll=CX)
 
     def main(c, x):
         return mid[ds((c * CX + x) * ROWS, CY), :]

time: 70.8 us -> 70.8 us (level)
  no operation moved by 1% of the time
where the time goes in v5:
time: 70.8 us; the launch traced here: 70.5 us
  blocking collectives  47.1 us (67%)
  Pallas kernels  10.4 us (15%)
  starting transfers between devices  8.86 us (13%)
  waiting for transfers between devices  3.34 us (5%)
  between operations  0.71 us (1%)
    all_to_all x1, blocking collectives, local(): rec = lax.all_to_all(send.reshape(NB, 16, NZ), 'gx', 0, 0, tiled=True)  18.8 us
    all_to_all x1, blocking collectives, local(): recv = lax.all_to_all(send, ('gx', 'gy'), 0, 0, tiled=True)  15.9 us
    all_to_all x1, blocking collectives, local(): back = lax.all_to_all(back.reshape(NB, 16, NZ), 'gx', 0, 0, tiled=True)  12.5 us
    pallas_call x8, Pallas kernels, call(): pl.pallas_call(body, out_shape=shapes, in_specs=[place(i, hbm) for i in r...  10.4 us
    ppermute x4, starting transfers between devices, shift(): lax.ppermute(value, axis, [(i, (i + by) % count) for i in range(count)])  5.43 us
    ppermute x3, starting transfers between devices, local(): lax.ppermute(rec, 'gy', [(i, i ^ k) for i in range(NBY)])  3.42 us
    ppermute x3, waiting for transfers between devices, local(): lax.ppermute(rec, 'gy', [(i, i ^ k) for i in range(NBY)])  2.92 us
  transfers between devices with their start and end apart: 7, of which 4 were waited for; matrix products, arithmetic and copies ran while one was open for 0% of the time, Pallas kernels for 6%

profile of v5, /device:TPU:1, one launch (start us, length us, event | category | flops | bytes accessed | tf_op | source)
XLA Modules:
  0.0 70.5 jit_solution(4756079622272406223)
XLA Ops:
  0.7 1.2 %shard_map.69 = (f32[184,128]{1,0:T(8,128)S(1)}, f32[184,128]{1,0:T(8,128)S(1)}, f32[176,128]{1,0:T(8,128)S(1)}, f32[176,128]{1,0:T(8,128)S(1)}) custom-call(f32[96,24,128]{2,1,0:T(8,128)} %bitcast.14, s32[16,24,128]{2,1,0:T(8,128)} %mat.1), custom_call_target="tpu_custom_call" | custom-call | tf_op jit(solution)/shard_map/pallas_call | solution.py:47
  1.9 2.8 %collective-permute-start = (f32[184,128]{1,0:T(8,128)S(1)}, f32[184,128]{1,0:T(8,128)S(1)}, u32[]{:S(2)}, u32[]{:S(2)}) collective-permute-start(f32[184,128]{1,0:T(8,128)S(1)} %get-tuple-element.39), channel_id=1, source_target_pairs={{0,4},{4,8},{8,12},{12,16},{16,20},{20,24},{24,28},{28,32},{32,36}... | collective-permute-start | bytes 282632 | tf_op jit(solution)/shard_map/ppermute | solution.py:627
  4.6 0.0 collective-permute-start.1
  4.6 1.2 %collective-permute-start.2 = (f32[176,128]{1,0:T(8,128)S(1)}, f32[176,128]{1,0:T(8,128)S(1)}, u32[]{:S(2)}, u32[]{:S(2)}) collective-permute-start(f32[176,128]{1,0:T(8,128)S(1)} %get-tuple-element.41), channel_id=1, source_target_pairs={{0,1},{1,2},{2,3},{3,0},{4,5},{5,6},{6,7},{7,4},{8,9},{9,10},{10,1... | collective-permute-start | bytes 270344 | tf_op jit(solution)/shard_map/ppermute | solution.py:627
  5.9 1.5 %collective-permute-start.3 = (f32[176,128]{1,0:T(8,128)S(1)}, f32[176,128]{1,0:T(8,128)S(1)}, u32[]{:S(2)}, u32[]{:S(2)}) collective-permute-start(f32[176,128]{1,0:T(8,128)S(1)} %get-tuple-element.42), channel_id=1, source_target_pairs={{0,3},{1,0},{2,1},{3,2},{4,7},{5,4},{6,5},{7,6},{8,11},{9,8},{10,9... | collective-permute-start | bytes 270344 | tf_op jit(solution)/shard_map/ppermute | solution.py:627
  7.3 1.5 %shard_map.68 = (f32[384,128]{1,0:T(8,128)S(1)}, f32[2304,128]{1,0:T(8,128)S(1)}, f32[384,128]{1,0:T(8,128)S(1)}, f32[384,128]{1,0:T(8,128)S(1)}, f32[384,128]{1...) custom-call(f32[2304,128]{1,0:T(8,128)S(1)} %bitcast.15, ...), custom_call_target="tpu_custom_call" | custom-call | flops 4000000 | bytes 4000000 | tf_op jit(solution)/shard_map/pallas_call | solution.py:47
  8.8 0.4 collective-permute-done.2.ylo
  9.2 0.0 collective-permute-done.3.yhi
  9.2 0.0 collective-permute-done.xlo
  9.2 0.7 shard_map.70
  10.0 18.8 %all_to_all.21 = f32[32,16,128]{2,1,0:T(8,128)S(1)} all-to-all(f32[32,16,128]{2,1,0:T(8,128)S(1)} %bitcast.22), channel_id=1, replica_groups=mesh['gx'=32,'gy'=4] {'gx'}, dimensions={0} | all-to-all | bytes 524288 | tf_op jit(solution)/shard_map/all_to_all | solution.py:663
  28.7 0.5 shard_map.71
  29.2 12.5 %all_to_all.22 = f32[32,16,128]{2,1,0:T(8,128)S(1)} all-to-all(f32[32,16,128]{2,1,0:T(8,128)S(1)} %bitcast.19), channel_id=1, replica_groups=mesh['gx'=32,'gy'=4] {'gx'}, dimensions={0} | all-to-all | bytes 524288 | tf_op jit(solution)/shard_map/all_to_all | solution.py:665
  41.7 1.3 %shard_map.72 = (f32[2304,128]{1,0:T(8,128)S(1)}, f32[240,128]{1,0:T(8,128)S(1)}) custom-call(f32[512,128]{1,0:T(8,128)S(1)} %bitcast.17, f32[3072,128]{1,0:T(8,128)S(1)} %get-tuple-element.45.sol, f32[384,128]{1,0:T(8,128)S(1)} %get-tuple-element.37.lsp, f32[384,128]{1,0:T(8,128)S(1)} %get-tuple-element.38.rsp, f32[128,128]{1,0:T(8,128)S(1)} %get-tuple-element.46.lsp_h, ...), custom_call_target="tpu_custom_call" | custom-call | tf_op jit(solution)/shard_map/pallas_call | solution.py:47
  43.0 2.8 %collective-permute-start.6 = (f32[240,128]{1,0:T(8,128)S(1)}, f32[240,128]{1,0:T(8,128)S(1)}, u32[]{:S(2)}, u32[]{:S(2)}) collective-permute-start(f32[240,128]{1,0:T(8,128)S(1)} %get-tuple-element.51.rec0), channel_id=1, source_target_pairs={{0,3},{1,2},{2,1},{3,0},{4,7},{5,6},{6,5},{7,4},{8,11},{9,10},{10,... | collective-permute-start | bytes 368648 | tf_op jit(solution)/shard_map/ppermute | solution.py:673
  45.7 0.3 collective-permute-start.5
  46.1 0.3 collective-permute-start.4
  46.4 2.7 %shard_map.73 = (f32[2304,128]{1,0:T(8,128)S(1)}, bf16[128,256]{1,0:T(8,128)(2,1)S(1)}, f32[128,256]{1,0:T(8,128)S(1)}, s32[8,256]{1,0:T(8,128)S(1)}, f32[384,12...) custom-call(s32[1,256]{1,0:T(1,128)S(1)} %bitcast.24, ...), custom_call_target="tpu_custom_call" | custom-call | flops 4000000 | bytes 4000000 | tf_op jit(solution)/shard_map/pallas_call | solution.py:47
  49.2 1.8 %collective-permute-done.6.rec3 = f32[240,128]{1,0:T(8,128)S(1)} collective-permute-done((f32[240,128]{1,0:T(8,128)S(1)}, f32[240,128]{1,0:T(8,128)S(1)}, u32[]{:S(2)}, u32[]{:S(2)}) %collective-permute-start.6) | collective-permute-done | bytes 122912 | tf_op jit(solution)/shard_map/ppermute | solution.py:673
  50.9 0.7 collective-permute-done.5.rec2
  51.6 0.5 collective-permute-done.4.rec1
  52.1 0.9 %shard_map.74 = (f32[2304,128]{1,0:T(8,128)S(1)}, f32[128,128]{1,0:T(8,128)S(1)}) custom-call(f32[240,128]{1,0:T(8,128)S(1)} %get-tuple-element.51.rec0, f32[240,128]{1,0:T(8,128)S(1)} %collective-permute-done.4.rec1, f32[240,128]{1,0:T(8,128)S(1)} %collective-permute-done.5.rec2, f32[240,128]{1,0:T(8,128)S(1)} %collective-permute-done.6.rec3, ...), custom_call_target="tpu_custom_call" | custom-call | tf_op jit(solution)/shard_map/pallas_call | solution.py:47
  53.0 15.9 %all_to_all.23 = f32[128,1,128]{2,1,0:T(1,128)S(1)} all-to-all(f32[128,1,128]{2,1,0:T(1,128)S(1)} %bitcast.23), channel_id=1, replica_groups=mesh['gx'=32,'gy'=4] {'gx','gy'}, dimensions={0} | all-to-all | bytes 131072 | tf_op jit(solution)/shard_map/all_to_all | solution.py:696
  68.9 1.6 %shard_map.75 = (f32[12,128]{1,0:T(8,128)}, f32[2304,128]{1,0:T(8,128)}) custom-call(f32[128,128]{1,0:T(8,128)S(1)} %bitcast.21, f32[384,128]{1,0:T(8,128)S(1)} %get-tuple-element.62.table, f32[2304,128]{1,0:T(8,128)S(1)} %get-tuple-element.63.made), custom_call_target="tpu_custom_call" | custom-call | tf_op jit(solution)/shard_map/pallas_call | solution.py:47
  (11 shorter events, 0.0 us)
Async XLA Ops:
  0.6 6.7 %copy-start.1 = (s32[16,24,128]{2,1,0:T(8,128)S(1)}, s32[16,24,128]{2,1,0:T(8,128)}, u32[]{:S(2)}) copy-start(s32[16,24,128]{2,1,0:T(8,128)} %mat.1) | copy-start | bytes 589828
  0.6 6.7 %copy-start = (f32[6,16,24,128]{3,2,1,0:T(8,128)S(1)}, f32[6,16,24,128]{3,2,1,0:T(8,128)}, u32[]{:S(2)}) copy-start(f32[6,16,24,128]{3,2,1,0:T(8,128)} %param.5) | copy-start | bytes 3538948
  0.6 6.7 %copy-start.4 = (f32[16]{0:T(128)S(1)}, f32[16]{0:T(128)}, u32[]{:S(2)}) copy-start(f32[16]{0:T(128)} %perm_hbm.1) | copy-start | bytes 196
  1.9 7.4 %collective-permute-start = (f32[184,128]{1,0:T(8,128)S(1)}, f32[184,128]{1,0:T(8,128)S(1)}, u32[]{:S(2)}, u32[]{:S(2)}) collective-permute-start(f32[184,128]{1,0:T(8,128)S(1)} %get-tuple-element.39), channel_id=1, source_target_pairs={{0,4},{4,8},{8,12},{12,16},{16,20},{20,24},{24,28},{28,32},{32,36}... | collective-permute-start | bytes 282632 | tf_op jit(solution)/shard_map/ppermute | solution.py:627
  4.6 4.6 %collective-permute-start.1 = (f32[184,128]{1,0:T(8,128)S(1)}, f32[184,128]{1,0:T(8,128)S(1)}, u32[]{:S(2)}, u32[]{:S(2)}) collective-permute-start(f32[184,128]{1,0:T(8,128)S(1)} %get-tuple-element.40), channel_id=1, source_target_pairs={{0,124},{4,0},{8,4},{12,8},{16,12},{20,16},{24,20},{28,24},{32,28}... | collective-permute-start | bytes 282632 | tf_op jit(solution)/shard_map/ppermute | solution.py:627
  4.6 4.6 %collective-permute-start.2 = (f32[176,128]{1,0:T(8,128)S(1)}, f32[176,128]{1,0:T(8,128)S(1)}, u32[]{:S(2)}, u32[]{:S(2)}) collective-permute-start(f32[176,128]{1,0:T(8,128)S(1)} %get-tuple-element.41), channel_id=1, source_target_pairs={{0,1},{1,2},{2,3},{3,0},{4,5},{5,6},{6,7},{7,4},{8,9},{9,10},{10,1... | collective-permute-start | bytes 270344 | tf_op jit(solution)/shard_map/ppermute | solution.py:627
  5.9 3.4 %collective-permute-start.3 = (f32[176,128]{1,0:T(8,128)S(1)}, f32[176,128]{1,0:T(8,128)S(1)}, u32[]{:S(2)}, u32[]{:S(2)}) collective-permute-start(f32[176,128]{1,0:T(8,128)S(1)} %get-tuple-element.42), channel_id=1, source_target_pairs={{0,3},{1,0},{2,1},{3,2},{4,7},{5,4},{6,5},{7,6},{8,11},{9,8},{10,9... | collective-permute-start | bytes 270344 | tf_op jit(solution)/shard_map/ppermute | solution.py:627
  41.7 4.8 %copy-start.2 = (s32[256]{0:T(256)S(1)}, s32[256]{0:T(256)}, u32[]{:S(2)}) copy-start(s32[256]{0:T(256)} %cell_hbm.1) | copy-start | bytes 3076
  41.7 4.8 %copy-start.3 = (s32[256,1]{0,1:T(1,128)S(1)}, s32[256,1]{0,1:T(1,128)}, u32[]{:S(2)}) copy-start(s32[256,1]{0,1:T(1,128)} %param.9) | copy-start | bytes 3076
  43.0 7.9 %collective-permute-start.6 = (f32[240,128]{1,0:T(8,128)S(1)}, f32[240,128]{1,0:T(8,128)S(1)}, u32[]{:S(2)}, u32[]{:S(2)}) collective-permute-start(f32[240,128]{1,0:T(8,128)S(1)} %get-tuple-element.51.rec0), channel_id=1, source_target_pairs={{0,3},{1,2},{2,1},{3,0},{4,7},{5,6},{6,5},{7,4},{8,11},{9,10},{10,... | collective-permute-start | bytes 368648 | tf_op jit(solution)/shard_map/ppermute | solution.py:673
  45.7 5.9 %collective-permute-start.5 = (f32[240,128]{1,0:T(8,128)S(1)}, f32[240,128]{1,0:T(8,128)S(1)}, u32[]{:S(2)}, u32[]{:S(2)}) collective-permute-start(f32[240,128]{1,0:T(8,128)S(1)} %get-tuple-element.51.rec0), channel_id=1, source_target_pairs={{0,2},{1,3},{2,0},{3,1},{4,6},{5,7},{6,4},{7,5},{8,10},{9,11},{10,... | collective-permute-start | bytes 368648 | tf_op jit(solution)/shard_map/ppermute | solution.py:673
  46.1 6.0 %collective-permute-start.4 = (f32[240,128]{1,0:T(8,128)S(1)}, f32[240,128]{1,0:T(8,128)S(1)}, u32[]{:S(2)}, u32[]{:S(2)}) collective-permute-start(f32[240,128]{1,0:T(8,128)S(1)} %get-tuple-element.51.rec0), channel_id=1, source_target_pairs={{0,1},{1,0},{2,3},{3,2},{4,5},{5,4},{6,7},{7,6},{8,9},{9,8},{10,11... | collective-permute-start | bytes 368648 | tf_op jit(solution)/shard_map/ppermute | solution.py:673

commit v6 on v5

--- a/solution.py
+++ b/solution.py
@@ -575,7 +575,7 @@
 
 
 def sine_cosine(v):
-    k = jnp.floor(v * (2.0 / math.pi) + 0.5)
+    k = (v * (2.0 / math.pi) + 12582912.0) - 12582912.0
     r = ((v - k * 1.5703125) - k * 4.837512969970703125e-4) - k * 7.54978995489188e-8
     z = r * r
     s = ((-1.9515295891e-4 * z + 8.3321608736e-3) * z - 1.6666654611e-1) * z * r + r

time: 70.8 us -> 70.8 us (level)
  no operation moved by 1% of the time
where the time goes in v6:
time: 70.8 us; the launch traced here: 70.5 us
  blocking collectives  47.1 us (67%)
  Pallas kernels  10.4 us (15%)
  starting transfers between devices  8.86 us (13%)
  waiting for transfers between devices  3.35 us (5%)
  between operations  0.71 us (1%)
    all_to_all x1, blocking collectives, local(): rec = lax.all_to_all(send.reshape(NB, 16, NZ), 'gx', 0, 0, tiled=True)  18.8 us
    all_to_all x1, blocking collectives, local(): recv = lax.all_to_all(send, ('gx', 'gy'), 0, 0, tiled=True)  15.9 us
    all_to_all x1, blocking collectives, local(): back = lax.all_to_all(back.reshape(NB, 16, NZ), 'gx', 0, 0, tiled=True)  12.5 us
    pallas_call x8, Pallas kernels, call(): pl.pallas_call(body, out_shape=shapes, in_specs=[place(i, hbm) for i in r...  10.4 us
    ppermute x4, starting transfers between devices, shift(): lax.ppermute(value, axis, [(i, (i + by) % count) for i in range(count)])  5.43 us
    ppermute x3, starting transfers between devices, local(): lax.ppermute(rec, 'gy', [(i, i ^ k) for i in range(NBY)])  3.42 us
    ppermute x3, waiting for transfers between devices, local(): lax.ppermute(rec, 'gy', [(i, i ^ k) for i in range(NBY)])  2.93 us
  transfers between devices with their start and end apart: 7, of which 4 were waited for; matrix products, arithmetic and copies ran while one was open for 0% of the time, Pallas kernels for 6%

profile of v6, /device:TPU:1, one launch (start us, length us, event | category | flops | bytes accessed | tf_op | source)
XLA Modules:
  0.0 70.5 jit_solution(16875312695189341143)
XLA Ops:
  0.7 1.2 %shard_map.69 = (f32[184,128]{1,0:T(8,128)S(1)}, f32[184,128]{1,0:T(8,128)S(1)}, f32[176,128]{1,0:T(8,128)S(1)}, f32[176,128]{1,0:T(8,128)S(1)}) custom-call(f32[96,24,128]{2,1,0:T(8,128)} %bitcast.14, s32[16,24,128]{2,1,0:T(8,128)} %mat.1), custom_call_target="tpu_custom_call" | custom-call | tf_op jit(solution)/shard_map/pallas_call | solution.py:47
  1.9 2.8 %collective-permute-start = (f32[184,128]{1,0:T(8,128)S(1)}, f32[184,128]{1,0:T(8,128)S(1)}, u32[]{:S(2)}, u32[]{:S(2)}) collective-permute-start(f32[184,128]{1,0:T(8,128)S(1)} %get-tuple-element.39), channel_id=1, source_target_pairs={{0,4},{4,8},{8,12},{12,16},{16,20},{20,24},{24,28},{28,32},{32,36}... | collective-permute-start | bytes 282632 | tf_op jit(solution)/shard_map/ppermute | solution.py:627
  4.6 0.0 collective-permute-start.1
  4.6 1.2 %collective-permute-start.2 = (f32[176,128]{1,0:T(8,128)S(1)}, f32[176,128]{1,0:T(8,128)S(1)}, u32[]{:S(2)}, u32[]{:S(2)}) collective-permute-start(f32[176,128]{1,0:T(8,128)S(1)} %get-tuple-element.41), channel_id=1, source_target_pairs={{0,1},{1,2},{2,3},{3,0},{4,5},{5,6},{6,7},{7,4},{8,9},{9,10},{10,1... | collective-permute-start | bytes 270344 | tf_op jit(solution)/shard_map/ppermute | solution.py:627
  5.9 1.5 %collective-permute-start.3 = (f32[176,128]{1,0:T(8,128)S(1)}, f32[176,128]{1,0:T(8,128)S(1)}, u32[]{:S(2)}, u32[]{:S(2)}) collective-permute-start(f32[176,128]{1,0:T(8,128)S(1)} %get-tuple-element.42), channel_id=1, source_target_pairs={{0,3},{1,0},{2,1},{3,2},{4,7},{5,4},{6,5},{7,6},{8,11},{9,8},{10,9... | collective-permute-start | bytes 270344 | tf_op jit(solution)/shard_map/ppermute | solution.py:627
  7.3 1.5 %shard_map.68 = (f32[384,128]{1,0:T(8,128)S(1)}, f32[2304,128]{1,0:T(8,128)S(1)}, f32[384,128]{1,0:T(8,128)S(1)}, f32[384,128]{1,0:T(8,128)S(1)}, f32[384,128]{1...) custom-call(f32[2304,128]{1,0:T(8,128)S(1)} %bitcast.15, ...), custom_call_target="tpu_custom_call" | custom-call | flops 4000000 | bytes 4000000 | tf_op jit(solution)/shard_map/pallas_call | solution.py:47
  8.8 0.4 collective-permute-done.2.ylo
  9.2 0.0 collective-permute-done.3.yhi
  9.2 0.0 collective-permute-done.xlo
  9.2 0.7 shard_map.70
  10.0 18.8 %all_to_all.21 = f32[32,16,128]{2,1,0:T(8,128)S(1)} all-to-all(f32[32,16,128]{2,1,0:T(8,128)S(1)} %bitcast.22), channel_id=1, replica_groups=mesh['gx'=32,'gy'=4] {'gx'}, dimensions={0} | all-to-all | bytes 524288 | tf_op jit(solution)/shard_map/all_to_all | solution.py:663
  28.7 0.5 shard_map.71
  29.2 12.5 %all_to_all.22 = f32[32,16,128]{2,1,0:T(8,128)S(1)} all-to-all(f32[32,16,128]{2,1,0:T(8,128)S(1)} %bitcast.19), channel_id=1, replica_groups=mesh['gx'=32,'gy'=4] {'gx'}, dimensions={0} | all-to-all | bytes 524288 | tf_op jit(solution)/shard_map/all_to_all | solution.py:665
  41.7 1.3 %shard_map.72 = (f32[2304,128]{1,0:T(8,128)S(1)}, f32[240,128]{1,0:T(8,128)S(1)}) custom-call(f32[512,128]{1,0:T(8,128)S(1)} %bitcast.17, f32[3072,128]{1,0:T(8,128)S(1)} %get-tuple-element.45.sol, f32[384,128]{1,0:T(8,128)S(1)} %get-tuple-element.37.lsp, f32[384,128]{1,0:T(8,128)S(1)} %get-tuple-element.38.rsp, f32[128,128]{1,0:T(8,128)S(1)} %get-tuple-element.46.lsp_h, ...), custom_call_target="tpu_custom_call" | custom-call | tf_op jit(solution)/shard_map/pallas_call | solution.py:47
  43.0 2.8 %collective-permute-start.6 = (f32[240,128]{1,0:T(8,128)S(1)}, f32[240,128]{1,0:T(8,128)S(1)}, u32[]{:S(2)}, u32[]{:S(2)}) collective-permute-start(f32[240,128]{1,0:T(8,128)S(1)} %get-tuple-element.51.rec0), channel_id=1, source_target_pairs={{0,3},{1,2},{2,1},{3,0},{4,7},{5,6},{6,5},{7,4},{8,11},{9,10},{10,... | collective-permute-start | bytes 368648 | tf_op jit(solution)/shard_map/ppermute | solution.py:673
  45.7 0.3 collective-permute-start.5
  46.1 0.3 collective-permute-start.4
  46.4 2.7 %shard_map.73 = (f32[2304,128]{1,0:T(8,128)S(1)}, bf16[128,256]{1,0:T(8,128)(2,1)S(1)}, f32[128,256]{1,0:T(8,128)S(1)}, s32[8,256]{1,0:T(8,128)S(1)}, f32[384,12...) custom-call(s32[1,256]{1,0:T(1,128)S(1)} %bitcast.24, ...), custom_call_target="tpu_custom_call" | custom-call | flops 4000000 | bytes 4000000 | tf_op jit(solution)/shard_map/pallas_call | solution.py:47
  49.2 1.8 %collective-permute-done.6.rec3 = f32[240,128]{1,0:T(8,128)S(1)} collective-permute-done((f32[240,128]{1,0:T(8,128)S(1)}, f32[240,128]{1,0:T(8,128)S(1)}, u32[]{:S(2)}, u32[]{:S(2)}) %collective-permute-start.6) | collective-permute-done | bytes 122912 | tf_op jit(solution)/shard_map/ppermute | solution.py:673
  50.9 0.7 collective-permute-done.5.rec2
  51.6 0.5 collective-permute-done.4.rec1
  52.1 0.9 %shard_map.74 = (f32[2304,128]{1,0:T(8,128)S(1)}, f32[128,128]{1,0:T(8,128)S(1)}) custom-call(f32[240,128]{1,0:T(8,128)S(1)} %get-tuple-element.51.rec0, f32[240,128]{1,0:T(8,128)S(1)} %collective-permute-done.4.rec1, f32[240,128]{1,0:T(8,128)S(1)} %collective-permute-done.5.rec2, f32[240,128]{1,0:T(8,128)S(1)} %collective-permute-done.6.rec3, ...), custom_call_target="tpu_custom_call" | custom-call | tf_op jit(solution)/shard_map/pallas_call | solution.py:47
  53.0 15.9 %all_to_all.23 = f32[128,1,128]{2,1,0:T(1,128)S(1)} all-to-all(f32[128,1,128]{2,1,0:T(1,128)S(1)} %bitcast.23), channel_id=1, replica_groups=mesh['gx'=32,'gy'=4] {'gx','gy'}, dimensions={0} | all-to-all | bytes 131072 | tf_op jit(solution)/shard_map/all_to_all | solution.py:696
  68.9 1.6 %shard_map.75 = (f32[12,128]{1,0:T(8,128)}, f32[2304,128]{1,0:T(8,128)}) custom-call(f32[128,128]{1,0:T(8,128)S(1)} %bitcast.21, f32[384,128]{1,0:T(8,128)S(1)} %get-tuple-element.62.table, f32[2304,128]{1,0:T(8,128)S(1)} %get-tuple-element.63.made), custom_call_target="tpu_custom_call" | custom-call | tf_op jit(solution)/shard_map/pallas_call | solution.py:47
  (11 shorter events, 0.0 us)
Async XLA Ops:
  0.6 6.7 %copy-start.1 = (s32[16,24,128]{2,1,0:T(8,128)S(1)}, s32[16,24,128]{2,1,0:T(8,128)}, u32[]{:S(2)}) copy-start(s32[16,24,128]{2,1,0:T(8,128)} %mat.1) | copy-start | bytes 589828
  0.6 6.7 %copy-start = (f32[6,16,24,128]{3,2,1,0:T(8,128)S(1)}, f32[6,16,24,128]{3,2,1,0:T(8,128)}, u32[]{:S(2)}) copy-start(f32[6,16,24,128]{3,2,1,0:T(8,128)} %param.5) | copy-start | bytes 3538948
  0.6 6.7 %copy-start.4 = (f32[16]{0:T(128)S(1)}, f32[16]{0:T(128)}, u32[]{:S(2)}) copy-start(f32[16]{0:T(128)} %perm_hbm.1) | copy-start | bytes 196
  1.9 7.4 %collective-permute-start = (f32[184,128]{1,0:T(8,128)S(1)}, f32[184,128]{1,0:T(8,128)S(1)}, u32[]{:S(2)}, u32[]{:S(2)}) collective-permute-start(f32[184,128]{1,0:T(8,128)S(1)} %get-tuple-element.39), channel_id=1, source_target_pairs={{0,4},{4,8},{8,12},{12,16},{16,20},{20,24},{24,28},{28,32},{32,36}... | collective-permute-start | bytes 282632 | tf_op jit(solution)/shard_map/ppermute | solution.py:627
  4.6 4.6 %collective-permute-start.1 = (f32[184,128]{1,0:T(8,128)S(1)}, f32[184,128]{1,0:T(8,128)S(1)}, u32[]{:S(2)}, u32[]{:S(2)}) collective-permute-start(f32[184,128]{1,0:T(8,128)S(1)} %get-tuple-element.40), channel_id=1, source_target_pairs={{0,124},{4,0},{8,4},{12,8},{16,12},{20,16},{24,20},{28,24},{32,28}... | collective-permute-start | bytes 282632 | tf_op jit(solution)/shard_map/ppermute | solution.py:627
  4.6 4.6 %collective-permute-start.2 = (f32[176,128]{1,0:T(8,128)S(1)}, f32[176,128]{1,0:T(8,128)S(1)}, u32[]{:S(2)}, u32[]{:S(2)}) collective-permute-start(f32[176,128]{1,0:T(8,128)S(1)} %get-tuple-element.41), channel_id=1, source_target_pairs={{0,1},{1,2},{2,3},{3,0},{4,5},{5,6},{6,7},{7,4},{8,9},{9,10},{10,1... | collective-permute-start | bytes 270344 | tf_op jit(solution)/shard_map/ppermute | solution.py:627
  5.9 3.4 %collective-permute-start.3 = (f32[176,128]{1,0:T(8,128)S(1)}, f32[176,128]{1,0:T(8,128)S(1)}, u32[]{:S(2)}, u32[]{:S(2)}) collective-permute-start(f32[176,128]{1,0:T(8,128)S(1)} %get-tuple-element.42), channel_id=1, source_target_pairs={{0,3},{1,0},{2,1},{3,2},{4,7},{5,4},{6,5},{7,6},{8,11},{9,8},{10,9... | collective-permute-start | bytes 270344 | tf_op jit(solution)/shard_map/ppermute | solution.py:627
  41.7 4.8 %copy-start.2 = (s32[256]{0:T(256)S(1)}, s32[256]{0:T(256)}, u32[]{:S(2)}) copy-start(s32[256]{0:T(256)} %cell_hbm.1) | copy-start | bytes 3076
  41.7 4.8 %copy-start.3 = (s32[256,1]{0,1:T(1,128)S(1)}, s32[256,1]{0,1:T(1,128)}, u32[]{:S(2)}) copy-start(s32[256,1]{0,1:T(1,128)} %param.9) | copy-start | bytes 3076
  43.0 7.9 %collective-permute-start.6 = (f32[240,128]{1,0:T(8,128)S(1)}, f32[240,128]{1,0:T(8,128)S(1)}, u32[]{:S(2)}, u32[]{:S(2)}) collective-permute-start(f32[240,128]{1,0:T(8,128)S(1)} %get-tuple-element.51.rec0), channel_id=1, source_target_pairs={{0,3},{1,2},{2,1},{3,0},{4,7},{5,6},{6,5},{7,4},{8,11},{9,10},{10,... | collective-permute-start | bytes 368648 | tf_op jit(solution)/shard_map/ppermute | solution.py:673
  45.7 5.9 %collective-permute-start.5 = (f32[240,128]{1,0:T(8,128)S(1)}, f32[240,128]{1,0:T(8,128)S(1)}, u32[]{:S(2)}, u32[]{:S(2)}) collective-permute-start(f32[240,128]{1,0:T(8,128)S(1)} %get-tuple-element.51.rec0), channel_id=1, source_target_pairs={{0,2},{1,3},{2,0},{3,1},{4,6},{5,7},{6,4},{7,5},{8,10},{9,11},{10,... | collective-permute-start | bytes 368648 | tf_op jit(solution)/shard_map/ppermute | solution.py:673
  46.1 6.0 %collective-permute-start.4 = (f32[240,128]{1,0:T(8,128)S(1)}, f32[240,128]{1,0:T(8,128)S(1)}, u32[]{:S(2)}, u32[]{:S(2)}) collective-permute-start(f32[240,128]{1,0:T(8,128)S(1)} %get-tuple-element.51.rec0), channel_id=1, source_target_pairs={{0,1},{1,0},{2,3},{3,2},{4,5},{5,4},{6,7},{7,6},{8,9},{9,8},{10,11... | collective-permute-start | bytes 368648 | tf_op jit(solution)/shard_map/ppermute | solution.py:673
